TPU v7x, 32 devices: a whole 2x2x4 slice. The times are simulated.
32 devices in a mesh: gx: 8 (over y, x, core), gy: 4 (over z).
Axes of the slice: x: 2, y: 2, z: 4, core: 2. Of those that a mesh axis runs over, the one named last changes fastest.
Arguments:
- soil_velocity: float32 [3, 32, 128, 512], P(None, None, 'gx', 'gy'), may hold values from -6 to 6
- soil_stress: float32 [6, 32, 128, 512], P(None, None, 'gx', 'gy'), may hold values from -6 to 6
- buoyancy: float32 [32, 128, 512], P(None, 'gx', 'gy'), may hold values from 0.5 to 1
- lame_first: float32 [32, 128, 512], P(None, 'gx', 'gy'), may hold values from 0.2 to 0.8
- shear_modulus: float32 [32, 128, 512], P(None, 'gx', 'gy'), may hold values from 0.1 to 0.6
- stiffness: bfloat16 [2048, 256, 256], P(('gx', 'gy')), may hold values from -1 to 5
- storey_drift: float32 [2048, 256], P(('gx', 'gy')), may hold values from -6 to 6
- drift_rate: float32 [2048, 256], P(('gx', 'gy')), may hold values from -6 to 6
- coupling: float32 [2048, 256], P(('gx', 'gy')), may hold values from 0.05 to 0.5
- contact: float32 [2048, 64], P(('gx', 'gy')), may hold values from 0.1 to 10
- dof_counts: int32 [2048], P(('gx', 'gy')), may hold values from 3 to 255, as said below
- owner_tile: int32 [2048, 1], P(('gx', 'gy')), may hold values from 0 to 31; in each aligned block of 64 rows (0 to 63, 64 to 127, ...) at most 2 rows name the same one
- corner_cell: int32 [2048], P(('gx', 'gy')), may hold values from 0 to 1088
Outputs:
- final_velocity: float32 [3, 32, 128, 512], P(None, None, 'gx', 'gy')
- final_drift: float32 [2048, 256], P(('gx', 'gy'))
- final_rate: float32 [2048, 256], P(('gx', 'gy'))
Inputs may be any that keep to these rules, and one draw needn't show every extreme that they name: `dof_counts`: a multiple of 3; the first building of every device holds the most. `owner_tile`: the index of the tile's device along gx then gy; among the 64 buildings of one device no tile appears more than 2 times, and some tile appears exactly 2 times in some device's buildings; every tile holds some building. `corner_cell`: encodes the footprint's first cell within the owner tile as x * 121 + y, so that the whole footprint lies in that tile.
All inputs are finite; a program needn't handle non-finite values.
Results may differ from a plain program's by a relative error of at most 0.002.
Values sent between devices are 32-bit elements; how exact they have to be, the bound alone decides.
No kernel may reach another device: no remote copies, remote signals or barrier semaphores. Data moves between devices by JAX's collectives and lax.ppermute only.
A program may use at most 128 MiB of HBM per device.

v0:
```python
import jax
import jax.numpy as jnp
from jax import lax
from jax.experimental import pallas as pl
from jax.experimental.pallas import tpu as pltpu
from jax.sharding import PartitionSpec as P

FOOT = 8
CAP = 2
PAD = 8

near = 9.0 / 8.0
far = 1.0 / 24.0
time_step = 0.3
exact = lax.Precision.HIGHEST
f32 = jnp.float32

AT_X, AT_Y, AT_RATE, AT_COUPLING, AT_NEXT, AT_SQUARE = 64, 65, 66, 69, 72, 75


def call(kernel, name, outs, args, scratch=()):
    size = sum(a.size * a.dtype.itemsize for a in args) + sum(o.size * o.dtype.itemsize for o in outs)
    return pl.pallas_call(
        kernel,
        name=name,
        out_shape=outs,
        scratch_shapes=list(scratch),
        cost_estimate=pl.CostEstimate(flops=size, bytes_accessed=size, transcendentals=0),
        compiler_params=pltpu.CompilerParams(vmem_limit_bytes=32 * 2**20),
    )(*args)


def shape(*dims):
    return jax.ShapeDtypeStruct(dims, f32)


def ring(block, axis, step):
    size = lax.axis_size(axis)
    return lax.ppermute(block, axis, [(i, (i + step) % size) for i in range(size)])


def diagonal(block):
    nx, ny = lax.axis_size("gx"), lax.axis_size("gy")
    route = [
        (((i + 1) % nx) * ny + (j + 1) % ny, i * ny + j) for i in range(nx) for j in range(ny)
    ]
    return lax.ppermute(block, ("gx", "gy"), route)


def lanes_of(value):
    return lax.broadcasted_iota(jnp.int32, value.shape, len(value.shape) - 1)


def roll(value, amount):
    return pltpu.roll(value, amount % value.shape[-1], len(value.shape) - 1)


def packed(pieces):
    result = None
    for slab, first, count, amount in pieces:
        moved = roll(slab, amount) if amount else slab
        if result is None:
            result = moved
        else:
            lane = lanes_of(slab)
            result = jnp.where((lane >= first) & (lane < first + count), moved, result)
    return result


def send_columns(pack_ref, out_ref):
    rows, width = out_ref.shape
    for block in range(width // 128):
        part = pack_ref[block * 128 : (block + 1) * 128, :]
        out_ref[:, block * 128 : (block + 1) * 128] = part.T[:rows]


def receive_columns(south_ref, north_ref, from_south, south_ok, north_ok, out_ref):
    rows, width = south_ref.shape
    for block in range(width // 128):
        cut = slice(block * 128, (block + 1) * 128)
        south = jnp.where(south_ok, south_ref[:, cut], 0.0)
        north = jnp.where(north_ok, north_ref[:, cut], 0.0)
        row = lax.broadcasted_iota(jnp.int32, south.shape, 0)
        taken = row == from_south[0]
        for other in from_south[1:]:
            taken = taken | (row == other)
        part = jnp.where(taken, south, north)
        whole = jnp.concatenate([part, jnp.zeros((128 - rows, 128), f32)], axis=0)
        out_ref[cut, :] = whole.T


def slopes(f, ghost, forward):
    lane = lanes_of(f)
    last = f.shape[-1] - 1
    up1 = roll(jnp.where(lane == 0, ghost, f), -1)
    down1 = roll(jnp.where(lane == last, ghost, f), 1)
    if forward:
        up2 = roll(jnp.where(lane <= 1, ghost, f), -2)
        return near * (up1 - f) - far * (up2 - down1)
    down2 = roll(jnp.where(lane >= last - 1, ghost, f), 2)
    return near * (f - down1) - far * (up1 - down2)


def across(ext, c, x, forward, layers):
    def at(d):
        return ext[c, x + 2 + d, PAD : PAD + layers, :]

    if forward:
        return near * (at(1) - at(0)) - far * (at(2) - at(-1))
    return near * (at(0) - at(-1)) - far * (at(1) - at(-2))


def down(ext, c, x, forward, layers):
    def at(d):
        return ext[c, x + 2, PAD + d : PAD + layers + d, :]

    if forward:
        return near * (at(1) - at(0)) - far * (at(2) - at(-1))
    return near * (at(0) - at(-1)) - far * (at(1) - at(-2))


def place():
    gx, gy = lax.axis_index("gx"), lax.axis_index("gy")
    nx, ny = lax.axis_size("gx"), lax.axis_size("gy")
    return gx > 0, gx < nx - 1, gy > 0, gy < ny - 1


def fill(ext, c, source, src, size_x, layers):
    for x in range(size_x):
        ext[c, x + 2, 0:PAD, :] = jnp.zeros((PAD, 128), f32)
        ext[c, x + 2, PAD : PAD + layers, :] = source[src, x * layers : (x + 1) * layers, :]
        ext[c, x + 2, PAD + layers : PAD + layers + PAD, :] = jnp.zeros((PAD, 128), f32)


def first_kernel(layers, v_ref, b_ref, m_ref, vt_ref, up_ref, dn_ref, col_ref, pack):
    size_x = v_ref.shape[1] // layers

    for x in range(size_x):
        cut = pl.ds(x * layers, layers)
        slab = [v_ref[c, pl.ds(x, layers, stride=size_x), :] for c in range(3)]
        buoy = b_ref[pl.ds(x, layers, stride=size_x), :]
        shear = m_ref[pl.ds(x, layers, stride=size_x), :]
        for c in range(3):
            vt_ref[c, cut, :] = slab[c]
        pack[cut, :] = packed(
            [
                (slab[0], 0, 3, 1),
                (slab[1], 3, 3, 5),
                (slab[2], 6, 3, 7),
                (buoy, 9, 1, 9),
                (shear, 10, 1, 10),
            ]
        )
        if x == 0:
            dn_ref[0] = slab[0]
            dn_ref[1] = slab[1]
            dn_ref[3] = slab[2]
            dn_ref[5] = buoy
            dn_ref[6] = shear
        if x == 1:
            dn_ref[2] = slab[1]
            dn_ref[4] = slab[2]
        if x == size_x - 2:
            up_ref[0] = slab[0]
        if x == size_x - 1:
            for c in range(3):
                up_ref[1 + c] = slab[c]
    send_columns(pack, col_ref)


def material_kernel(
    layers, b_ref, l_ref, m_ref, east_ref, north_ref, diag_ref, out_ref, bs, ms, tb, tm, cols
):
    size_x = b_ref.shape[0] // layers
    _, east_ok, _, north_ok = place()
    receive_columns(north_ref, north_ref, (0,), north_ok, north_ok, cols)
    inner = slice(PAD, PAD + layers)
    for x in range(size_x):
        bs[x, inner, :] = b_ref[pl.ds(x, layers, stride=size_x), :]
        ms[x, inner, :] = m_ref[pl.ds(x, layers, stride=size_x), :]
        part = cols[x * layers : (x + 1) * layers, :]
        tb[x, inner, :] = roll(part, -9)
        tm[x, inner, :] = roll(part, -10)
    bs[size_x, inner, :] = east_ref[5]
    ms[size_x, inner, :] = east_ref[6]
    tm[size_x, inner, :] = diag_ref[...]
    zero = jnp.zeros((PAD, 128), f32)
    for x in range(size_x + 1):
        bs[x, PAD + layers : PAD + layers + PAD, :] = zero
        ms[x, PAD + layers : PAD + layers + PAD, :] = zero
        tm[x, PAD + layers : PAD + layers + PAD, :] = zero
    below = slice(PAD + 1, PAD + layers + 1)

    def step(x, carry):
        cut = pl.ds(pl.multiple_of(x * layers, layers), layers)
        b, m = bs[x, inner, :], ms[x, inner, :]
        lane = lanes_of(b)
        layer = lax.broadcasted_iota(jnp.int32, b.shape, 0)
        in_x = (x < size_x - 1) | east_ok
        in_y = (lane < 127) | north_ok
        in_z = layer < layers - 1

        def north(value, ghost):
            return roll(jnp.where(lane == 0, ghost, value), -1)

        b_e = jnp.where(in_x, bs[x + 1, inner, :], b)
        b_n = jnp.where(in_y, north(b, tb[x, inner, :]), b)
        b_z = jnp.where(in_z, bs[x, below, :], b)
        m_e = jnp.where(in_x, ms[x + 1, inner, :], m)
        m_n = jnp.where(in_y, north(m, tm[x, inner, :]), m)
        m_z = jnp.where(in_z, ms[x, below, :], m)
        m_en = jnp.where(in_y & in_x, north(ms[x + 1, inner, :], tm[x + 1, inner, :]), m)
        m_ez = jnp.where(in_z & in_x, ms[x + 1, below, :], m)
        m_nz = jnp.where(in_z & in_y, north(ms[x, below, :], tm[x, below, :]), m)
        out_ref[0, cut, :] = time_step * l_ref[pl.ds(x, layers, stride=size_x), :]
        out_ref[1, cut, :] = (2.0 * time_step) * m
        out_ref[2, cut, :] = (0.25 * time_step) * (m + m_e + m_n + m_en)
        out_ref[3, cut, :] = (0.25 * time_step) * (m + m_e + m_z + m_ez)
        out_ref[4, cut, :] = (0.25 * time_step) * (m + m_n + m_z + m_nz)
        out_ref[5, cut, :] = (0.5 * time_step) * (b + b_e)
        out_ref[6, cut, :] = (0.5 * time_step) * (b + b_n)
        out_ref[7, cut, :] = (0.5 * time_step) * (b + b_z)
        return carry

    lax.fori_loop(0, size_x, step, 0)


def stress_kernel(
    layers,
    first,
    v_ref,
    s_ref,
    mat_ref,
    west_ref,
    east_ref,
    south_ref,
    north_ref,
    out_ref,
    up_ref,
    dn_ref,
    col_ref,
    ext,
    cols,
    pack,
):
    size_x = v_ref.shape[1] // layers
    west_ok, east_ok, south_ok, north_ok = place()
    receive_columns(south_ref, north_ref, (0, 3, 4, 6), south_ok, north_ok, cols)
    for c in range(3):
        fill(ext, c, v_ref, c, size_x, layers)
    inner = slice(PAD, PAD + layers)
    for row, c, x in ((0, 0, 0), (1, 0, 1), (2, 1, 1), (3, 2, 1)):
        ext[c, x, inner, :] = jnp.where(west_ok, west_ref[row], 0.0)
    for row, c, x in ((0, 0, 0), (1, 1, 0), (2, 1, 1), (3, 2, 0), (4, 2, 1)):
        ext[c, size_x + 2 + x, inner, :] = jnp.where(east_ok, east_ref[row], 0.0)

    def step(x, carry):
        cut = pl.ds(pl.multiple_of(x * layers, layers), layers)
        ghost = cols[cut, :]
        vx, vy, vz = [ext[c, x + 2, inner, :] for c in range(3)]
        gx, gy, gz = roll(ghost, -1), roll(ghost, -5), roll(ghost, -7)

        def old(c):
            if first:
                return s_ref[c, pl.ds(x, layers, stride=size_x), :]
            return s_ref[c, cut, :]

        dx = across(ext, 0, x, False, layers)
        dy = slopes(vy, gy, False)
        dz = down(ext, 2, x, False, layers)
        both = mat_ref[0, cut, :] * (dx + dy + dz)
        twice = mat_ref[1, cut, :]
        xx = old(0) + (both + twice * dx)
        yy = old(1) + (both + twice * dy)
        zz = old(2) + (both + twice * dz)
        xy = old(3) + mat_ref[2, cut, :] * (
            slopes(vx, gx, True) + across(ext, 1, x, True, layers)
        )
        xz = old(4) + mat_ref[3, cut, :] * (
            down(ext, 0, x, True, layers) + across(ext, 2, x, True, layers)
        )
        yz = old(5) + mat_ref[4, cut, :] * (
            down(ext, 1, x, True, layers) + slopes(vz, gz, True)
        )
        for c, value in enumerate((xx, yy, zz, xy, xz, yz)):
            out_ref[c, cut, :] = value
        pack[cut, :] = packed([(yy, 0, 3, 1), (xy, 3, 3, 5), (yz, 6, 3, 8)])
        return carry

    lax.fori_loop(0, size_x, step, 0)
    send_columns(pack, col_ref)

    def slab(c, x):
        return out_ref[c, x * layers : (x + 1) * layers, :]

    for row, (c, x) in enumerate(((0, 1), (3, 2), (3, 1), (4, 2), (4, 1))):
        up_ref[row] = slab(c, size_x - x)
    for row, (c, x) in enumerate(((0, 0), (0, 1), (3, 0), (4, 0))):
        dn_ref[row] = slab(c, x)


def velocity_kernel(
    layers,
    last,
    v_ref,
    s_ref,
    mat_ref,
    west_ref,
    east_ref,
    south_ref,
    north_ref,
    push_ref,
    *refs,
):
    if last:
        out_ref, ext, cols = refs
    else:
        out_ref, up_ref, dn_ref, col_ref, ext, cols, pack = refs
    size_x = v_ref.shape[1] // layers
    west_ok, east_ok, south_ok, north_ok = place()
    receive_columns(south_ref, north_ref, (0, 3, 4, 6, 7), south_ok, north_ok, cols)
    for c, src in enumerate((0, 3, 4, 5, 2)):
        fill(ext, c, s_ref, src, size_x, layers)
    inner = slice(PAD, PAD + layers)
    for row, c, x in ((0, 0, 1), (1, 1, 0), (2, 1, 1), (3, 2, 0), (4, 2, 1)):
        ext[c, x, inner, :] = jnp.where(west_ok, west_ref[row], 0.0)
    for row, c, x in ((0, 0, 0), (1, 0, 1), (2, 1, 0), (3, 2, 0)):
        ext[c, size_x + 2 + x, inner, :] = jnp.where(east_ok, east_ref[row], 0.0)

    def step(x, carry):
        cut = pl.ds(pl.multiple_of(x * layers, layers), layers)
        ghost = cols[cut, :]
        yy, xy, yz = s_ref[1, cut, :], ext[1, x + 2, inner, :], ext[3, x + 2, inner, :]
        gyy, gxy, gyz = roll(ghost, -1), roll(ghost, -5), roll(ghost, -8)
        ax = across(ext, 0, x, True, layers) + slopes(xy, gxy, False) + down(ext, 2, x, False, layers)
        ay = across(ext, 1, x, False, layers) + slopes(yy, gyy, True) + down(ext, 3, x, False, layers)
        az = across(ext, 2, x, False, layers) + slopes(yz, gyz, False) + down(ext, 4, x, True, layers)
        layer = lax.broadcasted_iota(jnp.int32, yy.shape, 0)
        fresh = []
        for c, accel in enumerate((ax, ay, az)):
            pushed = jnp.where(layer == 0, push_ref[c, pl.ds(x, 1), :], 0.0)
            fresh.append(v_ref[c, cut, :] + mat_ref[5 + c, cut, :] * accel + pushed)
        if last:
            for c in range(3):
                out_ref[c, pl.ds(x, layers, stride=size_x), :] = fresh[c]
        else:
            for c in range(3):
                out_ref[c, cut, :] = fresh[c]
            pack[cut, :] = packed([(fresh[0], 0, 3, 1), (fresh[1], 3, 3, 5), (fresh[2], 6, 3, 7)])
        return carry

    lax.fori_loop(0, size_x, step, 0)
    if last:
        return
    send_columns(pack, col_ref)

    def slab(c, x):
        return out_ref[c, x * layers : (x + 1) * layers, :]

    for row, (c, x) in enumerate(((0, 2), (0, 1), (1, 1), (2, 1))):
        up_ref[row] = slab(c, size_x - x)
    for row, (c, x) in enumerate(((0, 0), (1, 0), (1, 1), (2, 0), (2, 1))):
        dn_ref[row] = slab(c, x)


def third(value, e):
    d = lanes_of(value).astype(f32)
    return d - 3.0 * jnp.floor((d + 0.5) * (1.0 / 3.0)) == e


def column(row):
    n = row.shape[1]
    same = lax.broadcasted_iota(jnp.int32, (n, n), 0) == lax.broadcasted_iota(jnp.int32, (n, n), 1)
    return jnp.sum(jnp.where(same, row, 0.0), axis=1, keepdims=True)


def table_kernel(
    span,
    pull_ref,
    drift_ref,
    rate_ref,
    coupling_ref,
    contact_ref,
    counts_ref,
    owner_ref,
    corner_ref,
    out_ref,
    slot_ref,
    base_ref,
):
    number, width = rate_ref.shape
    slots = out_ref.shape[0]
    counts = column(counts_ref[...].astype(f32))
    mask = lax.broadcasted_iota(jnp.int32, (number, width), 1).astype(f32) < counts
    rate = jnp.where(mask, rate_ref[...], 0.0)
    coupling = jnp.where(mask, coupling_ref[...], 0.0)
    base = jnp.where(
        mask, rate - time_step * pull_ref[...] - time_step * coupling * rate, 0.0
    )
    base_ref[...] = base
    contact = contact_ref[...]
    weights = contact / jnp.sum(contact, axis=1, keepdims=True)
    corner = column(corner_ref[...].astype(f32))
    start_x = jnp.floor((corner + 0.5) * (1.0 / span))
    start_y = corner - start_x * span
    row = jnp.concatenate([weights, jnp.zeros((number, 128 - weights.shape[1]), f32)], axis=1)
    lane = lanes_of(row)
    row = jnp.where(lane == AT_X, start_x, row)
    row = jnp.where(lane == AT_Y, start_y, row)
    sums = (
        (AT_RATE, coupling * rate),
        (AT_COUPLING, coupling),
        (AT_NEXT, coupling * base),
        (AT_SQUARE, time_step * coupling * coupling),
    )
    for at, value in sums:
        for e in range(3):
            total = jnp.sum(jnp.where(third(value, e), value, 0.0), axis=1, keepdims=True)
            row = jnp.where(lane == at + e, total, row)
    owner = owner_ref[...].astype(f32)
    owner_col = column(owner)
    same = owner_col == owner
    i = lax.broadcasted_iota(jnp.int32, same.shape, 0)
    j = lax.broadcasted_iota(jnp.int32, same.shape, 1)
    slot_row = owner * CAP + jnp.sum(jnp.where(same & (i < j), 1.0, 0.0), axis=0, keepdims=True)
    slot_col = owner_col * CAP + jnp.sum(jnp.where(same & (j < i), 1.0, 0.0), axis=1, keepdims=True)
    to_slot = lax.broadcasted_iota(jnp.int32, (slots, number), 0).astype(f32) == slot_row
    of_slot = lax.broadcasted_iota(jnp.int32, (number, slots), 1).astype(f32) == slot_col
    slot_ref[...] = jnp.where(of_slot, 1.0, 0.0)
    out_ref[...] = jnp.dot(
        jnp.where(to_slot, 1.0, 0.0), row, precision=exact, preferred_element_type=f32
    )


def motion(maps_ref, v_ref, layers):
    size_x, slots, size_y = maps_ref.shape
    total = [jnp.zeros((slots, size_y), f32) for _ in range(3)]
    for x in range(size_x):
        part = maps_ref[x]
        for c in range(3):
            total[c] = total[c] + part * v_ref[c, x * layers : x * layers + 1, :]
    return [jnp.sum(t, axis=1, keepdims=True) for t in total]


def spread(maps_ref, reaction, out_ref):
    size_x = maps_ref.shape[0]
    for x in range(size_x):
        part = maps_ref[x]
        for c in range(3):
            out_ref[c, x : x + 1, :] = jnp.sum(part * reaction[c], axis=0, keepdims=True)


def surface_kernel(layers, table_ref, v_ref, maps_ref, moved_ref, push_ref):
    size_x = maps_ref.shape[0]
    table = table_ref[...]
    lane = lanes_of(table)
    off_y = lane - table[:, AT_Y : AT_Y + 1].astype(jnp.int32)
    start_x = table[:, AT_X : AT_X + 1]
    within = (off_y >= 0) & (off_y < FOOT)
    inside = jnp.where(within, off_y, 0)
    lines = []
    for a in range(FOOT):
        picked = jnp.take_along_axis(table, inside + a * FOOT, axis=1)
        lines.append(jnp.where(within, picked, 0.0))
    for x in range(size_x):
        value = jnp.zeros(table.shape, f32)
        for a in range(FOOT):
            value = jnp.where(start_x == float(x - a), lines[a], value)
        maps_ref[x] = value
    moved = motion(maps_ref, v_ref, layers)
    reaction = []
    rows = jnp.zeros(table.shape, f32)
    for c in range(3):
        rest, slope = (table[:, at + c : at + c + 1] for at in (AT_RATE, AT_COUPLING))
        reaction.append(time_step * FOOT * (rest - slope * moved[c]))
        rows = jnp.where(lane == c, moved[c], rows)
    moved_ref[...] = rows
    spread(maps_ref, reaction, push_ref)


def surface_again_kernel(layers, table_ref, v_ref, maps_ref, before_ref, moved_ref, push_ref):
    table, before = table_ref[...], before_ref[...]
    lane = lanes_of(table)
    moved = motion(maps_ref, v_ref, layers)
    reaction = []
    rows = before
    for c in range(3):
        rest, square, slope = (
            table[:, at + c : at + c + 1] for at in (AT_NEXT, AT_SQUARE, AT_COUPLING)
        )
        rest = rest + square * before[:, c : c + 1]
        reaction.append(time_step * FOOT * (rest - slope * moved[c]))
        rows = jnp.where(lane == 3 + c, moved[c], rows)
    moved_ref[...] = rows
    spread(maps_ref, reaction, push_ref)


def spread_thirds(moved, at, value):
    result = jnp.zeros(value.shape, f32)
    for e in range(3):
        result = jnp.where(third(value, e), moved[:, at + e : at + e + 1], result)
    return result


def halfway_kernel(
    moved_ref, slot_ref, base_ref, drift_ref, coupling_ref, counts_ref, rate_out, drift_out, m_out
):
    moved = jnp.dot(slot_ref[...], moved_ref[...], precision=exact, preferred_element_type=f32)
    m_out[...] = moved
    coupling = coupling_ref[...]
    counts = column(counts_ref[...].astype(f32))
    mask = lanes_of(coupling).astype(f32) < counts
    rate = base_ref[...] + time_step * coupling * spread_thirds(moved, 0, coupling)
    rate = jnp.where(mask, rate, 0.0)
    rate_out[...] = rate
    drift_out[...] = jnp.where(mask, drift_ref[...] + time_step * rate, 0.0)


def end_kernel(
    moved_ref, rate_ref, drift_ref, pull_ref, coupling_ref, counts_ref, drift_out, rate_out
):
    coupling = coupling_ref[...]
    counts = column(counts_ref[...].astype(f32))
    mask = lanes_of(coupling).astype(f32) < counts
    rate = rate_ref[...]
    relative = rate - spread_thirds(moved_ref[...], 3, coupling)
    rate = rate - time_step * pull_ref[...] - time_step * coupling * relative
    rate = jnp.where(mask, rate, 0.0)
    rate_out[...] = rate
    drift_out[...] = jnp.where(mask, drift_ref[...] + time_step * rate, 0.0)


def trade(rows):
    devices = lax.axis_size("gx") * lax.axis_size("gy")
    blocks = rows.reshape(devices, CAP, rows.shape[1])
    blocks = lax.all_to_all(blocks, ("gx", "gy"), split_axis=0, concat_axis=0, tiled=True)
    return blocks.reshape(rows.shape)


def pull_of(stiffness, drift):
    return jnp.einsum(
        "bij,bj->bi", stiffness, drift.astype(jnp.bfloat16), preferred_element_type=f32
    )


def body(
    soil_velocity,
    soil_stress,
    buoyancy,
    lame_first,
    shear_modulus,
    stiffness,
    storey_drift,
    drift_rate,
    coupling,
    contact,
    dof_counts,
    owner_tile,
    corner_cell,
):
    layers, size_x, size_y = buoyancy.shape
    cells = layers * size_x
    number, width = storey_drift.shape
    slots = lax.axis_size("gx") * lax.axis_size("gy") * CAP
    span = size_y - FOOT + 1
    v = soil_velocity.reshape(3, cells, size_y)
    s = soil_stress.reshape(6, cells, size_y)
    buoy, lame, shear = (a.reshape(cells, size_y) for a in (buoyancy, lame_first, shear_modulus))
    counts, owner, corner = (a.reshape(1, number) for a in (dof_counts, owner_tile, corner_cell))

    def bind(kernel, *fixed):
        def bound(*refs):
            kernel(*fixed, *refs)

        return bound

    def vm(*dims):
        return pltpu.VMEM(dims, f32)

    field = vm(cells, size_y)
    tall = layers + 2 * PAD
    vt, up, dn, col = call(
        bind(first_kernel, layers),
        "edges",
        (shape(3, cells, size_y), shape(4, layers, size_y), shape(7, layers, size_y), shape(16, cells)),
        (v, buoy, shear),
        [field],
    )

    def exchange(up, dn, col):
        west = ring(up, "gx", 1)
        east = ring(dn, "gx", -1)
        south = ring(col, "gy", 1)
        north = ring(col, "gy", -1)
        return west, east, south, north

    halo = exchange(up, dn, col)
    corner_rows = diagonal(dn[6])
    counted = jnp.arange(width)[None, :] < dof_counts[:, None]
    pull = pull_of(stiffness, jnp.where(counted, storey_drift, 0.0))
    table, of_slot, base = call(
        bind(table_kernel, span),
        "table",
        (shape(slots, 128), shape(number, slots), shape(number, width)),
        (pull, storey_drift, drift_rate, coupling, contact, counts, owner, corner),
    )
    table = trade(table)
    (material,) = call(
        bind(material_kernel, layers),
        "material",
        (shape(8, cells, size_y),),
        (buoy, lame, shear, halo[1], halo[3], corner_rows),
        [vm(size_x + 1, tall, size_y) for _ in range(4)] + [field],
    )

    def stress_step(first, v, s, halo):
        return call(
            bind(stress_kernel, layers, first),
            "stress",
            (
                shape(6, cells, size_y),
                shape(5, layers, size_y),
                shape(4, layers, size_y),
                shape(16, cells),
            ),
            (v, s, material, *halo),
            [vm(3, size_x + 4, tall, size_y), field, field],
        )

    def velocity_step(last, v, s, halo, push):
        outs = [shape(3, cells, size_y)]
        scratch = [vm(5, size_x + 4, tall, size_y), field]
        if not last:
            outs += [shape(4, layers, size_y), shape(5, layers, size_y), shape(16, cells)]
            scratch += [field]
        return call(
            bind(velocity_kernel, layers, last),
            "velocity",
            tuple(outs),
            (v, s, material, *halo, push),
            scratch,
        )

    st, up, dn, col = stress_step(True, vt, s, halo)
    halo = exchange(up, dn, col)
    maps, moved, push = call(
        bind(surface_kernel, layers),
        "surface",
        (shape(size_x, slots, size_y), shape(slots, 128), shape(3, size_x, size_y)),
        (table, vt),
    )
    vt, up, dn, col = velocity_step(False, vt, st, halo, push)
    halo = exchange(up, dn, col)
    moved, push = call(
        bind(surface_again_kernel, layers),
        "surface_again",
        (shape(slots, 128), shape(3, size_x, size_y)),
        (table, vt, maps, moved),
    )
    moved = trade(moved)
    st, up, dn, col = stress_step(False, vt, st, halo)
    halo = exchange(up, dn, col)
    rate, drift, moved = call(
        halfway_kernel,
        "halfway",
        (shape(number, width), shape(number, width), shape(number, 128)),
        (moved, of_slot, base, storey_drift, coupling, counts),
    )
    pull = pull_of(stiffness, drift)
    drift, rate = call(
        end_kernel,
        "end",
        (shape(number, width), shape(number, width)),
        (moved, rate, drift, pull, coupling, counts),
    )
    (v,) = velocity_step(True, vt, st, halo, push)
    return v.reshape(soil_velocity.shape), drift, rate


def solution(mesh):
    both = ("gx", "gy")
    soil = P(None, None, "gx", "gy")
    cell = P(None, "gx", "gy")
    placed = (
        soil,
        soil,
        cell,
        cell,
        cell,
        P(both, None, None),
        P(both, None),
        P(both, None),
        P(both, None),
        P(both, None),
        P(both),
        P(both, None),
        P(both),
    )
    return jax.shard_map(
        body,
        mesh=mesh,
        in_specs=placed,
        out_specs=(soil, P(both, None), P(both, None)),
        check_vma=False,
    )
```

profile of v0, /device:TPU:0, one launch (start us, length us, event | category | flops | bytes accessed | tf_op | source)
XLA Modules:
  0.0 92.8 jit_solution(8931648973170665741)
XLA Ops:
  0.6 0.0 copy-start.7
  0.6 0.9 %copy-done.7 = f32[32,16,128]{2,1,0:T(8,128)S(1)} copy-done((f32[32,16,128]{2,1,0:T(8,128)S(1)}, f32[32,16,128]{2,1,0:T(8,128)}, u32[]{:S(2)}) %copy-start.7) | copy-done | bytes 262168
  1.6 0.9 %copy-done.9 = f32[32,16,128]{2,1,0:T(8,128)S(1)} copy-done((f32[32,16,128]{2,1,0:T(8,128)S(1)}, f32[32,16,128]{2,1,0:T(8,128)}, u32[]{:S(2)}) %copy-start.9) | copy-done | bytes 262168
  2.5 1.1 %copy-done.10 = f32[3,32,16,128]{3,2,1,0:T(8,128)S(1)} copy-done((f32[3,32,16,128]{3,2,1,0:T(8,128)S(1)}, f32[3,32,16,128]{3,2,1,0:T(8,128)}, u32[]{:S(2)}) %copy-start.10) | copy-done | bytes 786456
  3.7 0.7 edges.1
  4.4 0.0 copy-start.16
  4.4 0.0 copy-start.17
  4.4 0.0 copy-start.18
  4.4 3.1 %collective-permute-start.4 = (f32[16,512]{1,0:T(8,128)S(1)}, f32[16,512]{1,0:T(8,128)S(1)}, u32[]{:S(2)}, u32[]{:S(2)}) collective-permute-start(f32[16,512]{1,0:T(8,128)S(1)} %get-tuple-element.34), channel_id=1, source_target_pairs={{0,1},{1,2},{2,3},{3,0},{4,5},{5,6},{6,7},{7,4},{8,9},{9,10},{10,1... | collective-permute-start | bytes 98312 | tf_op jit(solution)/shard_map/ppermute | solution.py:39
  7.5 2.1 %collective-permute-start.1 = (f32[16,512]{1,0:T(8,128)S(1)}, f32[16,512]{1,0:T(8,128)S(1)}, u32[]{:S(2)}, u32[]{:S(2)}) collective-permute-start(f32[16,512]{1,0:T(8,128)S(1)} %get-tuple-element.34), channel_id=1, source_target_pairs={{0,3},{1,0},{2,1},{3,2},{4,7},{5,4},{6,5},{7,6},{8,11},{9,8},{10,9... | collective-permute-start | bytes 98312 | tf_op jit(solution)/shard_map/ppermute | solution.py:39
  9.6 1.6 %collective-permute-start = (f32[7,32,128]{2,1,0:T(8,128)S(1)}, f32[7,32,128]{2,1,0:T(8,128)S(1)}, u32[]{:S(2)}, u32[]{:S(2)}) collective-permute-start(f32[7,32,128]{2,1,0:T(8,128)S(1)} %get-tuple-element.33), channel_id=1, source_target_pairs={{0,28},{4,0},{8,4},{12,8},{16,12},{20,16},{24,20},{28,24},{1,29},{... | collective-permute-start | bytes 344072 | tf_op jit(solution)/shard_map/ppermute | solution.py:39
  11.2 2.4 %collective-permute-start.2 = (f32[32,128]{1,0:T(8,128)S(1)}, f32[32,128]{1,0:T(8,128)S(1)}, u32[]{:S(2)}, u32[]{:S(2)}) collective-permute-start(f32[32,128]{1,0:T(8,128)S(1)} %slice_bitcast_fusion), channel_id=1, source_target_pairs={{5,0},{6,1},{7,2},{4,3},{9,4},{10,5},{11,6},{8,7},{13,8},{14,9},{1... | collective-permute-start | bytes 49160 | tf_op jit(solution)/shard_map/ppermute | solution.py:47
  13.5 0.0 collective-permute-start.3
  13.5 0.9 fusion.4
  14.5 0.5 collective-permute-done.2.refs_5_
  15.0 0.0 collective-permute-done.1.refs_4_.refs_6_
  15.0 0.0 collective-permute-done.refs_3_.refs_4_
  15.0 0.9 %copy-done.8 = f32[32,16,128]{2,1,0:T(8,128)S(1)} copy-done((f32[32,16,128]{2,1,0:T(8,128)S(1)}, f32[32,16,128]{2,1,0:T(8,128)}, u32[]{:S(2)}) %copy-start.8) | copy-done | bytes 262168
  15.9 0.9 %copy-done.13 = f32[32,16,128]{2,1,0:T(8,128)S(1)} copy-done((f32[32,16,128]{2,1,0:T(8,128)S(1)}, f32[32,16,128]{2,1,0:T(8,128)}, u32[]{:S(2)}) %copy-start.13) | copy-done | bytes 262168
  16.9 1.9 %material.1.refs_2_ = f32[8,512,128]{2,1,0:T(8,128)S(1)} custom-call(f32[512,128]{1,0:T(8,128)S(1)} %bitcast.29, f32[512,128]{1,0:T(8,128)S(1)} %bitcast.35, f32[512,128]{1,0:T(8,128)S(1)} %bitcast.31, f32[7,32,128]{2,1,0:T(8,128)S(1)} %collective-permute-done.refs_3_.refs_4_, f32[16,512]{1,0:T(8,128)S(1)} %collective-permute-done.1.refs_4_.refs_6_, ...), custom_call_target="tpu_custom_call" | custom-call | flops 3047424 | bytes 3047424 | tf_op jit(solution)/shard_map/material/pallas_call | solution.py:23
  18.8 0.0 collective-permute-done.3.refs_3_
  18.8 0.0 copy-start.6
  18.8 1.4 %copy-done.6 = f32[6,32,16,128]{3,2,1,0:T(8,128)S(1)} copy-done((f32[6,32,16,128]{3,2,1,0:T(8,128)S(1)}, f32[6,32,16,128]{3,2,1,0:T(8,128)}, u32[]{:S(2)}) %copy-start.6) | copy-done | bytes 1572888
  20.2 4.4 %stress.2 = (f32[6,512,128]{2,1,0:T(8,128)S(1)}, f32[5,32,128]{2,1,0:T(8,128)S(1)}, f32[4,32,128]{2,1,0:T(8,128)S(1)}, f32[16,512]{1,0:T(8,128)S(1)}) custom-call(f32[3,512,128]{2,1,0:T(8,128)S(1)} %get-tuple-element.32.refs_0_.refs_1_, f32[6,512,128]{2,1,0:T(8,128)S(1)} %bitcast.27, f32[8,512,128]{2,1,0:T(8,128)S(1)} %material.1.refs_2_, ...), custom_call_target="tpu_custom_call" | custom-call | flops 6455296 | bytes 6455296 | tf_op jit(solution)/shard_map/stress/pallas_call | solution.py:23
  24.7 1.2 %copy-done.3 = f32[6,512,128]{2,1,0:T(8,128)} copy-done((f32[6,512,128]{2,1,0:T(8,128)}, f32[6,512,128]{2,1,0:T(8,128)S(1)}, u32[]{:S(2)}) %copy-start.3) | copy-done | bytes 1572888
  25.9 2.3 %collective-permute-start.6 = (f32[4,32,128]{2,1,0:T(8,128)S(1)}, f32[4,32,128]{2,1,0:T(8,128)S(1)}, u32[]{:S(2)}, u32[]{:S(2)}) collective-permute-start(f32[4,32,128]{2,1,0:T(8,128)S(1)} %get-tuple-element.38), channel_id=1, source_target_pairs={{0,28},{4,0},{8,4},{12,8},{16,12},{20,16},{24,20},{28,24},{1,29},{... | collective-permute-start | bytes 196616 | tf_op jit(solution)/shard_map/ppermute | solution.py:39
  28.2 0.0 collective-permute-start.5
  28.2 5.6 %fusion.2 = f32[64,1,256]{2,1,0:T(1,128)S(1)} fusion(bf16[64,256,256]{2,1,0:T(8,128)(2,1)} %param.18, bf16[64,256,1]{1,0,2:T(8,128)(2,1)S(1)} %fusion.4), kind=kOutput, calls=%fused_computation.4 | convolution fusion | flops 8388608 | bytes 8486912 | tf_op jit(solution)/shard_map/bij,bj->bi/dot_general | solution.py:541
  33.8 0.0 copy-done.14
  33.9 1.0 %table.1 = (f32[64,128]{1,0:T(8,128)}, f32[64,64]{1,0:T(8,128)S(1)}, f32[64,256]{1,0:T(8,128)S(1)}) custom-call(f32[64,256]{1,0:T(8,128)S(1)} %bitcast.37, f32[64,256]{1,0:T(8,128)S(1)} %copy-done.11, f32[64,256]{1,0:T(8,128)S(1)} %copy-done.14, f32[64,256]{1,0:T(8,128)S(1)} %copy-done.12, f32[64,64]{1,0:T(8,128)S(1)} %copy-done.15, s32[1,64]{1,0:T(1,128)S(1)} %bitcast.39, ...), custom_call_target="tpu_custom_call" | custom-call | flops 393984 | bytes 393984 | tf_op jit(solution)/shard_map/table/pallas_call | solution.py:23
  35.0 6.0 %all-to-all-start = ((f32[32,2,128]{2,1,0:T(2,128)}), f32[32,2,128]{2,1,0:T(2,128)S(1)}, u32[]{:S(2)}, u32[]{:S(2)}) async-start(f32[32,2,128]{2,1,0:T(2,128)} %bitcast.11), calls=%async_computation | async-start | bytes 65536 | tf_op jit(solution)/shard_map/all_to_all | solution.py:536
  41.0 3.7 %collective-permute-start.8 = (f32[16,512]{1,0:T(8,128)S(1)}, f32[16,512]{1,0:T(8,128)S(1)}, u32[]{:S(2)}, u32[]{:S(2)}) collective-permute-start(f32[16,512]{1,0:T(8,128)S(1)} %get-tuple-element.39), channel_id=1, source_target_pairs={{0,3},{1,0},{2,1},{3,2},{4,7},{5,4},{6,5},{7,6},{8,11},{9,8},{10,9... | collective-permute-start | bytes 98312 | tf_op jit(solution)/shard_map/ppermute | solution.py:39
  44.6 0.0 collective-permute-start.7
  44.6 3.7 %all-to-all-done = f32[32,2,128]{2,1,0:T(2,128)S(1)} async-done(((f32[32,2,128]{2,1,0:T(2,128)}), f32[32,2,128]{2,1,0:T(2,128)S(1)}, u32[]{:S(2)}, u32[]{:S(2)}) %all-to-all-start) | async-done | bytes 32800 | tf_op jit(solution)/shard_map/all_to_all | solution.py:536
  48.3 1.0 %surface.1 = (f32[16,64,128]{2,1,0:T(8,128)S(1)}, f32[64,128]{1,0:T(8,128)S(1)}, f32[3,16,128]{2,1,0:T(8,128)S(1)}) custom-call(f32[64,128]{1,0:T(8,128)S(1)} %bitcast.33, f32[3,512,128]{2,1,0:T(8,128)S(1)} %get-tuple-element.32.refs_0_.refs_1_), custom_call_target="tpu_custom_call" | custom-call | flops 1400832 | bytes 1400832 | tf_op jit(solution)/shard_map/surface/pallas_call | solution.py:23
  49.4 0.0 collective-permute-done.8.refs_6_
  49.4 1.0 %collective-permute-done.7.refs_5_ = f32[16,512]{1,0:T(8,128)S(1)} collective-permute-done((f32[16,512]{1,0:T(8,128)S(1)}, f32[16,512]{1,0:T(8,128)S(1)}, u32[]{:S(2)}, u32[]{:S(2)}) %collective-permute-start.7) | collective-permute-done | bytes 32800 | tf_op jit(solution)/shard_map/ppermute | solution.py:39
  50.3 0.0 collective-permute-done.6.refs_4_
  50.4 0.0 collective-permute-done.5.refs_3_
  50.4 1.4 %copy-done.4 = f32[6,512,128]{2,1,0:T(8,128)S(1)} copy-done((f32[6,512,128]{2,1,0:T(8,128)S(1)}, f32[6,512,128]{2,1,0:T(8,128)}, u32[]{:S(2)}) %copy-start.4) | copy-done | bytes 1572888
  51.8 4.3 %velocity.2 = (f32[3,512,128]{2,1,0:T(8,128)S(1)}, f32[4,32,128]{2,1,0:T(8,128)S(1)}, f32[5,32,128]{2,1,0:T(8,128)S(1)}, f32[16,512]{1,0:T(8,128)S(1)}) custom-call(f32[3,512,128]{2,1,0:T(8,128)S(1)} %get-tuple-element.32.refs_0_.refs_1_, f32[6,512,128]{2,1,0:T(8,128)S(1)} %copy-done.4, f32[8,512,128]{2,1,0:T(8,128)S(1)} %material.1.refs_2_, ...), custom_call_target="tpu_custom_call" | custom-call | flops 5660672 | bytes 5660672 | tf_op jit(solution)/shard_map/velocity/pallas_call | solution.py:23
  56.1 0.9 surface_again.1
  57.0 0.9 copy-done
  57.9 2.8 %all-to-all-start.1 = ((f32[32,2,128]{2,1,0:T(2,128)}), f32[32,2,128]{2,1,0:T(2,128)S(1)}, u32[]{:S(2)}, u32[]{:S(2)}) async-start(f32[32,2,128]{2,1,0:T(2,128)} %bitcast.14), calls=%async_computation.1 | async-start | bytes 65536 | tf_op jit(solution)/shard_map/all_to_all | solution.py:536
  60.7 3.7 %collective-permute-start.12 = (f32[16,512]{1,0:T(8,128)S(1)}, f32[16,512]{1,0:T(8,128)S(1)}, u32[]{:S(2)}, u32[]{:S(2)}) collective-permute-start(f32[16,512]{1,0:T(8,128)S(1)} %get-tuple-element.45), channel_id=1, source_target_pairs={{0,3},{1,0},{2,1},{3,2},{4,7},{5,4},{6,5},{7,6},{8,11},{9,8},{10,9... | collective-permute-start | bytes 98312 | tf_op jit(solution)/shard_map/ppermute | solution.py:39
  64.3 0.0 collective-permute-start.11
  64.3 0.0 collective-permute-start.9
  64.3 2.6 %collective-permute-start.10 = (f32[5,32,128]{2,1,0:T(8,128)S(1)}, f32[5,32,128]{2,1,0:T(8,128)S(1)}, u32[]{:S(2)}, u32[]{:S(2)}) collective-permute-start(f32[5,32,128]{2,1,0:T(8,128)S(1)} %get-tuple-element.44), channel_id=1, source_target_pairs={{0,28},{4,0},{8,4},{12,8},{16,12},{20,16},{24,20},{28,24},{1,29},{... | collective-permute-start | bytes 245768 | tf_op jit(solution)/shard_map/ppermute | solution.py:39
  67.0 1.0 %all-to-all-done.1 = f32[32,2,128]{2,1,0:T(2,128)S(1)} async-done(((f32[32,2,128]{2,1,0:T(2,128)}), f32[32,2,128]{2,1,0:T(2,128)S(1)}, u32[]{:S(2)}, u32[]{:S(2)}) %all-to-all-start.1) | async-done | bytes 32800 | tf_op jit(solution)/shard_map/all_to_all | solution.py:536
  68.0 0.3 halfway.1
  68.3 0.0 collective-permute-done.12.refs_6_
  68.3 1.7 %collective-permute-done.11.refs_5_ = f32[16,512]{1,0:T(8,128)S(1)} collective-permute-done((f32[16,512]{1,0:T(8,128)S(1)}, f32[16,512]{1,0:T(8,128)S(1)}, u32[]{:S(2)}, u32[]{:S(2)}) %collective-permute-start.11) | collective-permute-done | bytes 32800 | tf_op jit(solution)/shard_map/ppermute | solution.py:39
  70.0 0.0 collective-permute-done.9.refs_3_
  70.0 0.0 collective-permute-done.10.refs_4_
  70.1 1.1 %copy-done.1 = f32[3,512,128]{2,1,0:T(8,128)S(1)} copy-done((f32[3,512,128]{2,1,0:T(8,128)S(1)}, f32[3,512,128]{2,1,0:T(8,128)}, u32[]{:S(2)}) %copy-start.1) | copy-done | bytes 786456
  71.2 1.4 %copy-done.5 = f32[6,512,128]{2,1,0:T(8,128)S(1)} copy-done((f32[6,512,128]{2,1,0:T(8,128)S(1)}, f32[6,512,128]{2,1,0:T(8,128)}, u32[]{:S(2)}) %copy-start.5) | copy-done | bytes 1572888
  72.6 4.3 %stress.3 = (f32[6,512,128]{2,1,0:T(8,128)S(1)}, f32[5,32,128]{2,1,0:T(8,128)S(1)}, f32[4,32,128]{2,1,0:T(8,128)S(1)}, f32[16,512]{1,0:T(8,128)S(1)}) custom-call(f32[3,512,128]{2,1,0:T(8,128)S(1)} %copy-done.1, f32[6,512,128]{2,1,0:T(8,128)S(1)} %copy-done.5, f32[8,512,128]{2,1,0:T(8,128)S(1)} %material.1.refs_2_, ...), custom_call_target="tpu_custom_call" | custom-call | flops 6422528 | bytes 6422528 | tf_op jit(solution)/shard_map/stress/pallas_call | solution.py:23
  76.9 2.8 %collective-permute-start.16 = (f32[16,512]{1,0:T(8,128)S(1)}, f32[16,512]{1,0:T(8,128)S(1)}, u32[]{:S(2)}, u32[]{:S(2)}) collective-permute-start(f32[16,512]{1,0:T(8,128)S(1)} %get-tuple-element.49), channel_id=1, source_target_pairs={{0,3},{1,0},{2,1},{3,2},{4,7},{5,4},{6,5},{7,6},{8,11},{9,8},{10,9... | collective-permute-start | bytes 98312 | tf_op jit(solution)/shard_map/ppermute | solution.py:39
  79.8 0.0 collective-permute-start.15
  79.8 2.4 %collective-permute-start.14 = (f32[4,32,128]{2,1,0:T(8,128)S(1)}, f32[4,32,128]{2,1,0:T(8,128)S(1)}, u32[]{:S(2)}, u32[]{:S(2)}) collective-permute-start(f32[4,32,128]{2,1,0:T(8,128)S(1)} %get-tuple-element.48), channel_id=1, source_target_pairs={{0,28},{4,0},{8,4},{12,8},{16,12},{20,16},{24,20},{28,24},{1,29},{... | collective-permute-start | bytes 196616 | tf_op jit(solution)/shard_map/ppermute | solution.py:39
  82.2 5.6 %fusion = f32[64,1,256]{2,1,0:T(1,128)S(1)} fusion(bf16[64,256,256]{2,1,0:T(8,128)(2,1)} %param.18, bf16[64,256,1]{1,0,2:T(8,128)(2,1)S(1)} %convert_bitcast_fusion), kind=kOutput, calls=%fused_computation.1 | convolution fusion | flops 8388608 | bytes 8486912 | tf_op jit(solution)/shard_map/bij,bj->bi/dot_general | solution.py:541
  87.8 0.8 end.1
  88.7 0.0 collective-permute-done.13.refs_3_
  88.7 4.1 %velocity.3 = f32[3,512,128]{2,1,0:T(8,128)} custom-call(f32[3,512,128]{2,1,0:T(8,128)S(1)} %copy-done.2, f32[6,512,128]{2,1,0:T(8,128)S(1)} %get-tuple-element.46.refs_1_, f32[8,512,128]{2,1,0:T(8,128)S(1)} %material.1.refs_2_, f32[5,32,128]{2,1,0:T(8,128)S(1)} %collective-permute-done.13.refs_3_, f32[4,32,128]{2,1,0:T(8,128)S(1)} %collective-permute-done.14.refs_4_, ...), custom_call_target="tpu_custom_call" | custom-call | flops 5480448 | bytes 5480448 | tf_op jit(solution)/shard_map/velocity/pallas_call | solution.py:23
  (30 shorter events, 0.1 us)
Async XLA Ops:
  0.6 1.0 %copy-start.7 = (f32[32,16,128]{2,1,0:T(8,128)S(1)}, f32[32,16,128]{2,1,0:T(8,128)}, u32[]{:S(2)}) copy-start(f32[32,16,128]{2,1,0:T(8,128)} %param.15) | copy-start | bytes 786436
  1.6 0.9 %copy-start.9 = (f32[32,16,128]{2,1,0:T(8,128)S(1)}, f32[32,16,128]{2,1,0:T(8,128)}, u32[]{:S(2)}) copy-start(f32[32,16,128]{2,1,0:T(8,128)} %param.17) | copy-start | bytes 786436
  2.5 1.1 %copy-start.10 = (f32[3,32,16,128]{3,2,1,0:T(8,128)S(1)}, f32[3,32,16,128]{3,2,1,0:T(8,128)}, u32[]{:S(2)}) copy-start(f32[3,32,16,128]{3,2,1,0:T(8,128)} %param.13) | copy-start | bytes 2359300
  3.7 30.2 %copy-start.14 = (f32[64,256]{1,0:T(8,128)S(1)}, f32[64,256]{1,0:T(8,128)}, u32[]{:S(2)}) copy-start(f32[64,256]{1,0:T(8,128)} %refs_2_.1) | copy-start | bytes 196612
  3.7 30.2 %copy-start.15 = (f32[64,64]{1,0:T(8,128)S(1)}, f32[64,64]{1,0:T(8,128)}, u32[]{:S(2)}) copy-start(f32[64,64]{1,0:T(8,128)} %refs_4_.1) | copy-start | bytes 49156
  4.4 29.5 %copy-start.11 = (f32[64,256]{1,0:T(8,128)S(1)}, f32[64,256]{1,0:T(8,128)}, u32[]{:S(2)}) copy-start(f32[64,256]{1,0:T(8,128)} %drift_ref.1) | copy-start | bytes 196612
  4.4 29.5 %copy-start.12 = (f32[64,256]{1,0:T(8,128)S(1)}, f32[64,256]{1,0:T(8,128)}, u32[]{:S(2)}) copy-start(f32[64,256]{1,0:T(8,128)} %coupling_ref.3) | copy-start | bytes 196612
  4.4 29.5 %copy-start.16 = (s32[64]{0:T(128)S(1)}, s32[64]{0:T(128)}, u32[]{:S(2)}) copy-start(s32[64]{0:T(128)} %param.23) | copy-start | bytes 772
  4.4 29.5 %copy-start.17 = (s32[64,1]{0,1:T(1,128)S(1)}, s32[64,1]{0,1:T(1,128)}, u32[]{:S(2)}) copy-start(s32[64,1]{0,1:T(1,128)} %param.24) | copy-start | bytes 772
  4.4 29.5 %copy-start.18 = (s32[64]{0:T(128)S(1)}, s32[64]{0:T(128)}, u32[]{:S(2)}) copy-start(s32[64]{0:T(128)} %param.25) | copy-start | bytes 772
  4.4 14.4 %collective-permute-start.4 = (f32[16,512]{1,0:T(8,128)S(1)}, f32[16,512]{1,0:T(8,128)S(1)}, u32[]{:S(2)}, u32[]{:S(2)}) collective-permute-start(f32[16,512]{1,0:T(8,128)S(1)} %get-tuple-element.34), channel_id=1, source_target_pairs={{0,1},{1,2},{2,3},{3,0},{4,5},{5,6},{6,7},{7,4},{8,9},{9,10},{10,1... | collective-permute-start | bytes 98312 | tf_op jit(solution)/shard_map/ppermute | solution.py:39
  7.5 7.5 %collective-permute-start.1 = (f32[16,512]{1,0:T(8,128)S(1)}, f32[16,512]{1,0:T(8,128)S(1)}, u32[]{:S(2)}, u32[]{:S(2)}) collective-permute-start(f32[16,512]{1,0:T(8,128)S(1)} %get-tuple-element.34), channel_id=1, source_target_pairs={{0,3},{1,0},{2,1},{3,2},{4,7},{5,4},{6,5},{7,6},{8,11},{9,8},{10,9... | collective-permute-start | bytes 98312 | tf_op jit(solution)/shard_map/ppermute | solution.py:39
  9.6 5.4 %collective-permute-start = (f32[7,32,128]{2,1,0:T(8,128)S(1)}, f32[7,32,128]{2,1,0:T(8,128)S(1)}, u32[]{:S(2)}, u32[]{:S(2)}) collective-permute-start(f32[7,32,128]{2,1,0:T(8,128)S(1)} %get-tuple-element.33), channel_id=1, source_target_pairs={{0,28},{4,0},{8,4},{12,8},{16,12},{20,16},{24,20},{28,24},{1,29},{... | collective-permute-start | bytes 344072 | tf_op jit(solution)/shard_map/ppermute | solution.py:39
  11.2 3.8 %collective-permute-start.2 = (f32[32,128]{1,0:T(8,128)S(1)}, f32[32,128]{1,0:T(8,128)S(1)}, u32[]{:S(2)}, u32[]{:S(2)}) collective-permute-start(f32[32,128]{1,0:T(8,128)S(1)} %slice_bitcast_fusion), channel_id=1, source_target_pairs={{5,0},{6,1},{7,2},{4,3},{9,4},{10,5},{11,6},{8,7},{13,8},{14,9},{1... | collective-permute-start | bytes 49160 | tf_op jit(solution)/shard_map/ppermute | solution.py:47
  13.5 5.3 %collective-permute-start.3 = (f32[4,32,128]{2,1,0:T(8,128)S(1)}, f32[4,32,128]{2,1,0:T(8,128)S(1)}, u32[]{:S(2)}, u32[]{:S(2)}) collective-permute-start(f32[4,32,128]{2,1,0:T(8,128)S(1)} %get-tuple-element.35), channel_id=1, source_target_pairs={{0,4},{4,8},{8,12},{12,16},{16,20},{20,24},{24,28},{28,0},{1,5},{5... | collective-permute-start | bytes 196616 | tf_op jit(solution)/shard_map/ppermute | solution.py:39
  15.0 1.0 %copy-start.8 = (f32[32,16,128]{2,1,0:T(8,128)S(1)}, f32[32,16,128]{2,1,0:T(8,128)}, u32[]{:S(2)}) copy-start(f32[32,16,128]{2,1,0:T(8,128)} %param.15) | copy-start | bytes 786436
  15.9 0.9 %copy-start.13 = (f32[32,16,128]{2,1,0:T(8,128)S(1)}, f32[32,16,128]{2,1,0:T(8,128)}, u32[]{:S(2)}) copy-start(f32[32,16,128]{2,1,0:T(8,128)} %param.16) | copy-start | bytes 786436
  18.8 1.4 %copy-start.6 = (f32[6,32,16,128]{3,2,1,0:T(8,128)S(1)}, f32[6,32,16,128]{3,2,1,0:T(8,128)}, u32[]{:S(2)}) copy-start(f32[6,32,16,128]{3,2,1,0:T(8,128)} %param.14) | copy-start | bytes 4718596
  24.7 1.2 %copy-start.3 = (f32[6,512,128]{2,1,0:T(8,128)}, f32[6,512,128]{2,1,0:T(8,128)S(1)}, u32[]{:S(2)}) copy-start(f32[6,512,128]{2,1,0:T(8,128)S(1)} %get-tuple-element.36.refs_1_) | copy-start | bytes 4718596
  25.9 24.5 %collective-permute-start.6 = (f32[4,32,128]{2,1,0:T(8,128)S(1)}, f32[4,32,128]{2,1,0:T(8,128)S(1)}, u32[]{:S(2)}, u32[]{:S(2)}) collective-permute-start(f32[4,32,128]{2,1,0:T(8,128)S(1)} %get-tuple-element.38), channel_id=1, source_target_pairs={{0,28},{4,0},{8,4},{12,8},{16,12},{20,16},{24,20},{28,24},{1,29},{... | collective-permute-start | bytes 196616 | tf_op jit(solution)/shard_map/ppermute | solution.py:39
  28.2 22.2 %collective-permute-start.5 = (f32[5,32,128]{2,1,0:T(8,128)S(1)}, f32[5,32,128]{2,1,0:T(8,128)S(1)}, u32[]{:S(2)}, u32[]{:S(2)}) collective-permute-start(f32[5,32,128]{2,1,0:T(8,128)S(1)} %get-tuple-element.37), channel_id=1, source_target_pairs={{0,4},{4,8},{8,12},{12,16},{16,20},{20,24},{24,28},{28,0},{1,5},{5... | collective-permute-start | bytes 245768 | tf_op jit(solution)/shard_map/ppermute | solution.py:39
  35.0 13.4 %all-to-all-start = ((f32[32,2,128]{2,1,0:T(2,128)}), f32[32,2,128]{2,1,0:T(2,128)S(1)}, u32[]{:S(2)}, u32[]{:S(2)}) async-start(f32[32,2,128]{2,1,0:T(2,128)} %bitcast.11), calls=%async_computation | async-start | bytes 65536 | tf_op jit(solution)/shard_map/all_to_all | solution.py:536
  41.0 8.4 %collective-permute-start.8 = (f32[16,512]{1,0:T(8,128)S(1)}, f32[16,512]{1,0:T(8,128)S(1)}, u32[]{:S(2)}, u32[]{:S(2)}) collective-permute-start(f32[16,512]{1,0:T(8,128)S(1)} %get-tuple-element.39), channel_id=1, source_target_pairs={{0,3},{1,0},{2,1},{3,2},{4,7},{5,4},{6,5},{7,6},{8,11},{9,8},{10,9... | collective-permute-start | bytes 98312 | tf_op jit(solution)/shard_map/ppermute | solution.py:39
  44.6 5.7 %collective-permute-start.7 = (f32[16,512]{1,0:T(8,128)S(1)}, f32[16,512]{1,0:T(8,128)S(1)}, u32[]{:S(2)}, u32[]{:S(2)}) collective-permute-start(f32[16,512]{1,0:T(8,128)S(1)} %get-tuple-element.39), channel_id=1, source_target_pairs={{0,1},{1,2},{2,3},{3,0},{4,5},{5,6},{6,7},{7,4},{8,9},{9,10},{10,1... | collective-permute-start | bytes 98312 | tf_op jit(solution)/shard_map/ppermute | solution.py:39
  50.4 1.4 %copy-start.4 = (f32[6,512,128]{2,1,0:T(8,128)S(1)}, f32[6,512,128]{2,1,0:T(8,128)}, u32[]{:S(2)}) copy-start(f32[6,512,128]{2,1,0:T(8,128)} %copy-done.3) | copy-start | bytes 4718596
  57.0 0.9 copy-start
  57.9 10.2 %all-to-all-start.1 = ((f32[32,2,128]{2,1,0:T(2,128)}), f32[32,2,128]{2,1,0:T(2,128)S(1)}, u32[]{:S(2)}, u32[]{:S(2)}) async-start(f32[32,2,128]{2,1,0:T(2,128)} %bitcast.14), calls=%async_computation.1 | async-start | bytes 65536 | tf_op jit(solution)/shard_map/all_to_all | solution.py:536
  60.7 7.7 %collective-permute-start.12 = (f32[16,512]{1,0:T(8,128)S(1)}, f32[16,512]{1,0:T(8,128)S(1)}, u32[]{:S(2)}, u32[]{:S(2)}) collective-permute-start(f32[16,512]{1,0:T(8,128)S(1)} %get-tuple-element.45), channel_id=1, source_target_pairs={{0,3},{1,0},{2,1},{3,2},{4,7},{5,4},{6,5},{7,6},{8,11},{9,8},{10,9... | collective-permute-start | bytes 98312 | tf_op jit(solution)/shard_map/ppermute | solution.py:39
  64.3 5.7 %collective-permute-start.11 = (f32[16,512]{1,0:T(8,128)S(1)}, f32[16,512]{1,0:T(8,128)S(1)}, u32[]{:S(2)}, u32[]{:S(2)}) collective-permute-start(f32[16,512]{1,0:T(8,128)S(1)} %get-tuple-element.45), channel_id=1, source_target_pairs={{0,1},{1,2},{2,3},{3,0},{4,5},{5,6},{6,7},{7,4},{8,9},{9,10},{10,1... | collective-permute-start | bytes 98312 | tf_op jit(solution)/shard_map/ppermute | solution.py:39
  64.3 5.7 %collective-permute-start.9 = (f32[4,32,128]{2,1,0:T(8,128)S(1)}, f32[4,32,128]{2,1,0:T(8,128)S(1)}, u32[]{:S(2)}, u32[]{:S(2)}) collective-permute-start(f32[4,32,128]{2,1,0:T(8,128)S(1)} %get-tuple-element.43), channel_id=1, source_target_pairs={{0,4},{4,8},{8,12},{12,16},{16,20},{20,24},{24,28},{28,0},{1,5},{5... | collective-permute-start | bytes 196616 | tf_op jit(solution)/shard_map/ppermute | solution.py:39
  64.3 5.7 %collective-permute-start.10 = (f32[5,32,128]{2,1,0:T(8,128)S(1)}, f32[5,32,128]{2,1,0:T(8,128)S(1)}, u32[]{:S(2)}, u32[]{:S(2)}) collective-permute-start(f32[5,32,128]{2,1,0:T(8,128)S(1)} %get-tuple-element.44), channel_id=1, source_target_pairs={{0,28},{4,0},{8,4},{12,8},{16,12},{20,16},{24,20},{28,24},{1,29},{... | collective-permute-start | bytes 245768 | tf_op jit(solution)/shard_map/ppermute | solution.py:39
  70.0 1.1 %copy-start.1 = (f32[3,512,128]{2,1,0:T(8,128)S(1)}, f32[3,512,128]{2,1,0:T(8,128)}, u32[]{:S(2)}) copy-start(f32[3,512,128]{2,1,0:T(8,128)} %copy-done) | copy-start | bytes 2359300
  71.2 1.4 %copy-start.5 = (f32[6,512,128]{2,1,0:T(8,128)S(1)}, f32[6,512,128]{2,1,0:T(8,128)}, u32[]{:S(2)}) copy-start(f32[6,512,128]{2,1,0:T(8,128)} %copy-done.3) | copy-start | bytes 4718596
  72.6 16.1 %copy-start.2 = (f32[3,512,128]{2,1,0:T(8,128)S(1)}, f32[3,512,128]{2,1,0:T(8,128)}, u32[]{:S(2)}) copy-start(f32[3,512,128]{2,1,0:T(8,128)} %copy-done) | copy-start | bytes 2359300
  76.9 11.7 %collective-permute-start.16 = (f32[16,512]{1,0:T(8,128)S(1)}, f32[16,512]{1,0:T(8,128)S(1)}, u32[]{:S(2)}, u32[]{:S(2)}) collective-permute-start(f32[16,512]{1,0:T(8,128)S(1)} %get-tuple-element.49), channel_id=1, source_target_pairs={{0,3},{1,0},{2,1},{3,2},{4,7},{5,4},{6,5},{7,6},{8,11},{9,8},{10,9... | collective-permute-start | bytes 98312 | tf_op jit(solution)/shard_map/ppermute | solution.py:39
  79.8 8.9 %collective-permute-start.15 = (f32[16,512]{1,0:T(8,128)S(1)}, f32[16,512]{1,0:T(8,128)S(1)}, u32[]{:S(2)}, u32[]{:S(2)}) collective-permute-start(f32[16,512]{1,0:T(8,128)S(1)} %get-tuple-element.49), channel_id=1, source_target_pairs={{0,1},{1,2},{2,3},{3,0},{4,5},{5,6},{6,7},{7,4},{8,9},{9,10},{10,1... | collective-permute-start | bytes 98312 | tf_op jit(solution)/shard_map/ppermute | solution.py:39
  79.8 8.9 %collective-permute-start.14 = (f32[4,32,128]{2,1,0:T(8,128)S(1)}, f32[4,32,128]{2,1,0:T(8,128)S(1)}, u32[]{:S(2)}, u32[]{:S(2)}) collective-permute-start(f32[4,32,128]{2,1,0:T(8,128)S(1)} %get-tuple-element.48), channel_id=1, source_target_pairs={{0,28},{4,0},{8,4},{12,8},{16,12},{20,16},{24,20},{28,24},{1,29},{... | collective-permute-start | bytes 196616 | tf_op jit(solution)/shard_map/ppermute | solution.py:39
  82.2 6.5 %collective-permute-start.13 = (f32[5,32,128]{2,1,0:T(8,128)S(1)}, f32[5,32,128]{2,1,0:T(8,128)S(1)}, u32[]{:S(2)}, u32[]{:S(2)}) collective-permute-start(f32[5,32,128]{2,1,0:T(8,128)S(1)} %get-tuple-element.47), channel_id=1, source_target_pairs={{0,4},{4,8},{8,12},{12,16},{16,20},{20,24},{24,28},{28,0},{1,5},{5... | collective-permute-start | bytes 245768 | tf_op jit(solution)/shard_map/ppermute | solution.py:39
where the time goes:
time: 93.7 us; the launch traced here: 92.8 us
  starting transfers between devices  35.5 us (38%)
  Pallas kernels  23.9 us (26%)
  local copies, waits for them, and re-layouts  12.4 us (13%)
  matrix products  11.3 us (12%)
  waiting for transfers between devices  7.95 us (8%)
    ppermute x16, starting transfers between devices, ring(): lax.ppermute(block, axis, [(i, (i + step) % size) for i in range(size)])  24.4 us
    pallas_call x11, Pallas kernels, call(): pl.pallas_call(kernel, name=name, out_shape=outs, scratch_shapes=list(scr...  23.9 us
    unnamed x38, local copies, waits for them, and re-layouts  12.4 us
    dot_general x2, matrix products, pull_of(): jnp.einsum('bij,bj->bi', stiffness, drift.astype(jnp.bfloat16), preferred...  11.3 us
    all_to_all x2, starting transfers between devices, trade(): lax.all_to_all(blocks, ('gx', 'gy'), split_axis=0, concat_axis=0, tiled=T...  8.77 us
    all_to_all x2, waiting for transfers between devices, trade(): lax.all_to_all(blocks, ('gx', 'gy'), split_axis=0, concat_axis=0, tiled=T...  4.74 us
    ppermute x16, waiting for transfers between devices, ring(): lax.ppermute(block, axis, [(i, (i + step) % size) for i in range(size)])  2.7 us
    ppermute x1, starting transfers between devices, diagonal(): return lax.ppermute(block, ('gx', 'gy'), route)  2.35 us
  transfers between devices with their start and end apart: 19, of which 5 were waited for; matrix products, arithmetic and copies ran while one was open for 13% of the time, Pallas kernels for 5%

commit v1 on v0

--- a/solution.py
+++ b/solution.py
@@ -8,6 +8,7 @@
 FOOT = 8
 CAP = 2
 PAD = 8
+STRIP = 8
 
 near = 9.0 / 8.0
 far = 1.0 / 24.0
@@ -15,36 +16,72 @@
 exact = lax.Precision.HIGHEST
 f32 = jnp.float32
 
-AT_X, AT_Y, AT_RATE, AT_COUPLING, AT_NEXT, AT_SQUARE = 64, 65, 66, 69, 72, 75
-
-
-def call(kernel, name, outs, args, scratch=()):
-    size = sum(a.size * a.dtype.itemsize for a in args) + sum(o.size * o.dtype.itemsize for o in outs)
+AT_X, AT_Y, AT_RATE, AT_COUPLING, AT_SQUARE, AT_CORNER = 64, 65, 66, 69, 72, 75
+FIRST, SECOND, AT_NEXT = 0, 3, 8
+
+
+COSTS = {
+    "first": 30_000_000,
+    "load": 20_000_000,
+    "material": 10_000_000,
+    "stress": 25_000_000,
+    "surface": 10_000_000,
+    "pull": 30_000_000,
+    "velocity": 25_000_000,
+    "motion_again": 10_000_000,
+    "finish": 60_000_000,
+}
+
+
+class Far:
+    def __init__(self, value):
+        self.value = value
+
+
+def call(kernel, name, outs, args, scratch=(), far_outs=()):
+    cost = COSTS[name]
+    specs, values = [], []
+    for a in args:
+        far = isinstance(a, Far)
+        a = a.value if far else a
+        values.append(pltpu.with_memory_space_constraint(a, pltpu.HBM if far else pltpu.VMEM))
+        specs.append(pl.BlockSpec(memory_space=pl.ANY if far else pltpu.VMEM))
     return pl.pallas_call(
         kernel,
         name=name,
         out_shape=outs,
+        in_specs=specs,
+        out_specs=tuple(
+            pl.BlockSpec(memory_space=pl.ANY if i in far_outs else pltpu.VMEM)
+            for i in range(len(outs))
+        ),
         scratch_shapes=list(scratch),
-        cost_estimate=pl.CostEstimate(flops=size, bytes_accessed=size, transcendentals=0),
-        compiler_params=pltpu.CompilerParams(vmem_limit_bytes=32 * 2**20),
-    )(*args)
+        cost_estimate=pl.CostEstimate(flops=cost, bytes_accessed=cost, transcendentals=0),
+        compiler_params=pltpu.CompilerParams(vmem_limit_bytes=16 * 2**20),
+    )(*values)
 
 
 def shape(*dims):
     return jax.ShapeDtypeStruct(dims, f32)
+
+
+def near_by(*dims, dtype=f32):
+    return pltpu.VMEM(dims, dtype)
+
+
+def fetch(sources, targets, sems):
+    copies = [
+        pltpu.make_async_copy(source, target, sems.at[i])
+        for i, (source, target) in enumerate(zip(sources, targets))
+    ]
+    for copy in copies:
+        copy.start()
+    return copies
 
 
 def ring(block, axis, step):
     size = lax.axis_size(axis)
     return lax.ppermute(block, axis, [(i, (i + step) % size) for i in range(size)])
-
-
-def diagonal(block):
-    nx, ny = lax.axis_size("gx"), lax.axis_size("gy")
-    route = [
-        (((i + 1) % nx) * ny + (j + 1) % ny, i * ny + j) for i in range(nx) for j in range(ny)
-    ]
-    return lax.ppermute(block, ("gx", "gy"), route)
 
 
 def lanes_of(value):
@@ -132,9 +169,8 @@
         ext[c, x + 2, PAD + layers : PAD + layers + PAD, :] = jnp.zeros((PAD, 128), f32)
 
 
-def first_kernel(layers, v_ref, b_ref, m_ref, vt_ref, up_ref, dn_ref, col_ref, pack):
+def edges(layers, v_ref, b_ref, m_ref, vt_ref, bt_ref, mt_ref, up_ref, dn_ref, col_ref, pack):
     size_x = v_ref.shape[1] // layers
-
     for x in range(size_x):
         cut = pl.ds(x * layers, layers)
         slab = [v_ref[c, pl.ds(x, layers, stride=size_x), :] for c in range(3)]
@@ -142,6 +178,8 @@
         shear = m_ref[pl.ds(x, layers, stride=size_x), :]
         for c in range(3):
             vt_ref[c, cut, :] = slab[c]
+        bt_ref[cut, :] = buoy
+        mt_ref[cut, :] = shear
         pack[cut, :] = packed(
             [
                 (slab[0], 0, 3, 1),
@@ -168,22 +206,43 @@
     send_columns(pack, col_ref)
 
 
+def load_kernel(layers, s_hbm, l_hbm, st_ref, lt_ref, s_ref, l_ref, sems):
+    size_x = l_ref.shape[0] // layers
+    sources = [s_hbm.at[c] for c in range(6)] + [l_hbm]
+    targets = [s_ref.at[c] for c in range(6)] + [l_ref]
+    copies = fetch(sources, targets, sems)
+    for c, copy in enumerate(copies):
+        copy.wait()
+        for x in range(size_x):
+            cut = pl.ds(x * layers, layers)
+            if c < 6:
+                st_ref[c, cut, :] = s_ref[c, pl.ds(x, layers, stride=size_x), :]
+            else:
+                lt_ref[cut, :] = l_ref[pl.ds(x, layers, stride=size_x), :]
+
+
 def material_kernel(
-    layers, b_ref, l_ref, m_ref, east_ref, north_ref, diag_ref, out_ref, bs, ms, tb, tm, cols
+    layers, b_ref, l_ref, m_ref, east_ref, north_ref, table_ref, out_ref, bs, ms, tb, tm, cols
 ):
     size_x = b_ref.shape[0] // layers
     _, east_ok, _, north_ok = place()
+    nx, ny = lax.axis_size("gx"), lax.axis_size("gy")
+    beyond = lax.rem(lax.axis_index("gx") + 1, nx) * ny + lax.rem(lax.axis_index("gy") + 1, ny)
     receive_columns(north_ref, north_ref, (0,), north_ok, north_ok, cols)
     inner = slice(PAD, PAD + layers)
     for x in range(size_x):
-        bs[x, inner, :] = b_ref[pl.ds(x, layers, stride=size_x), :]
-        ms[x, inner, :] = m_ref[pl.ds(x, layers, stride=size_x), :]
-        part = cols[x * layers : (x + 1) * layers, :]
+        cut = slice(x * layers, (x + 1) * layers)
+        bs[x, inner, :] = b_ref[cut, :]
+        ms[x, inner, :] = m_ref[cut, :]
+        part = cols[cut, :]
         tb[x, inner, :] = roll(part, -9)
         tm[x, inner, :] = roll(part, -10)
     bs[size_x, inner, :] = east_ref[5]
     ms[size_x, inner, :] = east_ref[6]
-    tm[size_x, inner, :] = diag_ref[...]
+    line = jnp.broadcast_to(table_ref[pl.ds(beyond * CAP, 1), :], (layers, 128))
+    own = lanes_of(line) - AT_CORNER == lax.broadcasted_iota(jnp.int32, line.shape, 0)
+    corner = jnp.sum(jnp.where(own, line, 0.0), axis=1, keepdims=True)
+    tm[size_x, inner, :] = jnp.broadcast_to(corner, line.shape)
     zero = jnp.zeros((PAD, 128), f32)
     for x in range(size_x + 1):
         bs[x, PAD + layers : PAD + layers + PAD, :] = zero
@@ -212,7 +271,7 @@
         m_en = jnp.where(in_y & in_x, north(ms[x + 1, inner, :], tm[x + 1, inner, :]), m)
         m_ez = jnp.where(in_z & in_x, ms[x + 1, below, :], m)
         m_nz = jnp.where(in_z & in_y, north(ms[x, below, :], tm[x, below, :]), m)
-        out_ref[0, cut, :] = time_step * l_ref[pl.ds(x, layers, stride=size_x), :]
+        out_ref[0, cut, :] = time_step * l_ref[cut, :]
         out_ref[1, cut, :] = (2.0 * time_step) * m
         out_ref[2, cut, :] = (0.25 * time_step) * (m + m_e + m_n + m_en)
         out_ref[3, cut, :] = (0.25 * time_step) * (m + m_e + m_z + m_ez)
@@ -222,7 +281,7 @@
         out_ref[7, cut, :] = (0.5 * time_step) * (b + b_z)
         return carry
 
-    lax.fori_loop(0, size_x, step, 0)
+    lax.fori_loop(0, size_x, step, 0, unroll=4)
 
 
 def stress_kernel(
@@ -239,10 +298,14 @@
     up_ref,
     dn_ref,
     col_ref,
-    ext,
-    cols,
-    pack,
+    *refs,
 ):
+    if first:
+        kept_hbm, ext, cols, pack, sems = refs
+        keep = pltpu.make_async_copy(mat_ref, kept_hbm, sems.at[0])
+        keep.start()
+    else:
+        ext, cols, pack = refs
     size_x = v_ref.shape[1] // layers
     west_ok, east_ok, south_ok, north_ok = place()
     receive_columns(south_ref, north_ref, (0, 3, 4, 6), south_ok, north_ok, cols)
@@ -261,8 +324,6 @@
         gx, gy, gz = roll(ghost, -1), roll(ghost, -5), roll(ghost, -7)
 
         def old(c):
-            if first:
-                return s_ref[c, pl.ds(x, layers, stride=size_x), :]
             return s_ref[c, cut, :]
 
         dx = across(ext, 0, x, False, layers)
@@ -287,7 +348,7 @@
         pack[cut, :] = packed([(yy, 0, 3, 1), (xy, 3, 3, 5), (yz, 6, 3, 8)])
         return carry
 
-    lax.fori_loop(0, size_x, step, 0)
+    lax.fori_loop(0, size_x, step, 0, unroll=4)
     send_columns(pack, col_ref)
 
     def slab(c, x):
@@ -297,6 +358,8 @@
         up_ref[row] = slab(c, size_x - x)
     for row, (c, x) in enumerate(((0, 0), (0, 1), (3, 0), (4, 0))):
         dn_ref[row] = slab(c, x)
+    if first:
+        keep.wait()
 
 
 def velocity_kernel(
@@ -313,10 +376,11 @@
     *refs,
 ):
     if last:
-        out_ref, ext, cols = refs
+        out_hbm, out_ref, ext, cols, sems = refs
     else:
         out_ref, up_ref, dn_ref, col_ref, ext, cols, pack = refs
     size_x = v_ref.shape[1] // layers
+    parts = size_x // STRIP
     west_ok, east_ok, south_ok, north_ok = place()
     receive_columns(south_ref, north_ref, (0, 3, 4, 6, 7), south_ok, north_ok, cols)
     for c, src in enumerate((0, 3, 4, 5, 2)):
@@ -342,14 +406,22 @@
             fresh.append(v_ref[c, cut, :] + mat_ref[5 + c, cut, :] * accel + pushed)
         if last:
             for c in range(3):
-                out_ref[c, pl.ds(x, layers, stride=size_x), :] = fresh[c]
+                out_ref[x // STRIP, c, :, lax.rem(x, STRIP), :] = fresh[c]
         else:
             for c in range(3):
                 out_ref[c, cut, :] = fresh[c]
             pack[cut, :] = packed([(fresh[0], 0, 3, 1), (fresh[1], 3, 3, 5), (fresh[2], 6, 3, 7)])
         return carry
 
-    lax.fori_loop(0, size_x, step, 0)
+    leaving = []
+    for part in range(parts):
+        lax.fori_loop(part * STRIP, (part + 1) * STRIP, step, 0, unroll=4)
+        if last:
+            leaving += fetch(
+                [out_ref.at[part]], [out_hbm.at[:, :, part]], sems.at[pl.ds(part, 1)]
+            )
+    for copy in leaving:
+        copy.wait()
     if last:
         return
     send_columns(pack, col_ref)
@@ -374,10 +446,28 @@
     return jnp.sum(jnp.where(same, row, 0.0), axis=1, keepdims=True)
 
 
-def table_kernel(
+def slot_table(owner_ref, slots):
+    number = owner_ref.shape[1]
+    owner = owner_ref[...].astype(f32)
+    owner_col = column(owner)
+    same = owner_col == owner
+    i = lax.broadcasted_iota(jnp.int32, same.shape, 0)
+    j = lax.broadcasted_iota(jnp.int32, same.shape, 1)
+    slot_row = owner * CAP + jnp.sum(jnp.where(same & (i < j), 1.0, 0.0), axis=0, keepdims=True)
+    slot_col = owner_col * CAP + jnp.sum(jnp.where(same & (j < i), 1.0, 0.0), axis=1, keepdims=True)
+    to_slot = lax.broadcasted_iota(jnp.int32, (slots, number), 0).astype(f32) == slot_row
+    of_slot = lax.broadcasted_iota(jnp.int32, (number, slots), 1).astype(f32) == slot_col
+    return jnp.where(to_slot, 1.0, 0.0), jnp.where(of_slot, 1.0, 0.0)
+
+
+def counted(counts_ref, shape):
+    return lax.broadcasted_iota(jnp.int32, shape, 1).astype(f32) < column(
+        counts_ref[...].astype(f32)
+    )
+
+
+def table(
     span,
-    pull_ref,
-    drift_ref,
     rate_ref,
     coupling_ref,
     contact_ref,
@@ -385,19 +475,12 @@
     owner_ref,
     corner_ref,
     out_ref,
-    slot_ref,
-    base_ref,
 ):
     number, width = rate_ref.shape
     slots = out_ref.shape[0]
-    counts = column(counts_ref[...].astype(f32))
-    mask = lax.broadcasted_iota(jnp.int32, (number, width), 1).astype(f32) < counts
+    mask = counted(counts_ref, (number, width))
     rate = jnp.where(mask, rate_ref[...], 0.0)
     coupling = jnp.where(mask, coupling_ref[...], 0.0)
-    base = jnp.where(
-        mask, rate - time_step * pull_ref[...] - time_step * coupling * rate, 0.0
-    )
-    base_ref[...] = base
     contact = contact_ref[...]
     weights = contact / jnp.sum(contact, axis=1, keepdims=True)
     corner = column(corner_ref[...].astype(f32))
@@ -410,26 +493,78 @@
     sums = (
         (AT_RATE, coupling * rate),
         (AT_COUPLING, coupling),
-        (AT_NEXT, coupling * base),
         (AT_SQUARE, time_step * coupling * coupling),
     )
+    row = sums_by_third(row, sums)
+    to_slot, _ = slot_table(owner_ref, slots)
+    out_ref[...] = jnp.dot(to_slot, row, precision=exact, preferred_element_type=f32)
+
+
+def first_kernel(layers, span, *refs):
+    far, outs, scratch = refs[:9], refs[9:16], refs[16:]
+    near, pack, sems = scratch[:9], scratch[9], scratch[10]
+    copies = fetch(far, near, sems)
+    for copy in copies[3:]:
+        copy.wait()
+    table(span, *near[3:], outs[6])
+    for copy in copies[:3]:
+        copy.wait()
+    edges(layers, *near[:3], *outs[:6], pack)
+    first = outs[2][pl.ds(0, layers), 0:1]
+    spot = lax.broadcasted_iota(jnp.int32, (layers, 128), 1) - AT_CORNER
+    own = spot == lax.broadcasted_iota(jnp.int32, (layers, 128), 0)
+    outs[6][...] += jnp.sum(jnp.where(own, first, 0.0), axis=0, keepdims=True)
+
+
+def sums_by_third(row, sums):
+    lane = lanes_of(row)
     for at, value in sums:
         for e in range(3):
             total = jnp.sum(jnp.where(third(value, e), value, 0.0), axis=1, keepdims=True)
             row = jnp.where(lane == at + e, total, row)
-    owner = owner_ref[...].astype(f32)
-    owner_col = column(owner)
-    same = owner_col == owner
-    i = lax.broadcasted_iota(jnp.int32, same.shape, 0)
-    j = lax.broadcasted_iota(jnp.int32, same.shape, 1)
-    slot_row = owner * CAP + jnp.sum(jnp.where(same & (i < j), 1.0, 0.0), axis=0, keepdims=True)
-    slot_col = owner_col * CAP + jnp.sum(jnp.where(same & (j < i), 1.0, 0.0), axis=1, keepdims=True)
-    to_slot = lax.broadcasted_iota(jnp.int32, (slots, number), 0).astype(f32) == slot_row
-    of_slot = lax.broadcasted_iota(jnp.int32, (number, slots), 1).astype(f32) == slot_col
-    slot_ref[...] = jnp.where(of_slot, 1.0, 0.0)
-    out_ref[...] = jnp.dot(
-        jnp.where(to_slot, 1.0, 0.0), row, precision=exact, preferred_element_type=f32
-    )
+    return row
+
+
+def products(stiff_ref, drift_ref, out_ref, begin, end):
+    group = 16
+    for g in range(begin // group * group, end, group):
+        rounded = drift_ref[g : g + group, :].astype(jnp.bfloat16)
+        row = lax.broadcasted_iota(jnp.int32, rounded.shape, 0)
+        low, high = max(g, begin), min(g + group, end)
+        total = out_ref[g : g + group, :]
+        for b in range(low, high):
+            part = lax.dot_general(
+                rounded, stiff_ref[b], (((1,), (1,)), ((), ())), preferred_element_type=f32
+            )
+            total = jnp.where(row == b - g, part, total)
+        out_ref[g : g + group, :] = total
+
+
+def pull_kernel(
+    stiff_ref,
+    raw_ref,
+    rate_ref,
+    coupling_ref,
+    counts_ref,
+    owner_ref,
+    base_ref,
+    drift_out,
+    next_ref,
+    pull,
+):
+    number = drift_out.shape[0]
+    mask = counted(counts_ref, drift_out.shape)
+    drift_out[...] = jnp.where(mask, raw_ref[...], 0.0)
+    pull[...] = jnp.zeros(pull.shape, f32)
+    products(stiff_ref, drift_out, pull, 0, number)
+    rate = jnp.where(mask, rate_ref[...], 0.0)
+    coupling = jnp.where(mask, coupling_ref[...], 0.0)
+    base = rate - time_step * pull[...] - time_step * coupling * rate
+    base = jnp.where(mask, base, 0.0)
+    base_ref[...] = base
+    row = sums_by_third(jnp.zeros((number, 128), f32), ((AT_NEXT, coupling * base),))
+    to_slot, _ = slot_table(owner_ref, next_ref.shape[0])
+    next_ref[...] = jnp.dot(to_slot, row, precision=exact, preferred_element_type=f32)
 
 
 def motion(maps_ref, v_ref, layers):
@@ -442,57 +577,48 @@
     return [jnp.sum(t, axis=1, keepdims=True) for t in total]
 
 
-def spread(maps_ref, reaction, out_ref):
-    size_x = maps_ref.shape[0]
-    for x in range(size_x):
-        part = maps_ref[x]
+def spread(at, reaction, out_ref):
+    for x in range(out_ref.shape[1]):
+        part = at(x)
         for c in range(3):
             out_ref[c, x : x + 1, :] = jnp.sum(part * reaction[c], axis=0, keepdims=True)
 
 
-def surface_kernel(layers, table_ref, v_ref, maps_ref, moved_ref, push_ref):
-    size_x = maps_ref.shape[0]
-    table = table_ref[...]
+def footprints(table):
     lane = lanes_of(table)
     off_y = lane - table[:, AT_Y : AT_Y + 1].astype(jnp.int32)
-    start_x = table[:, AT_X : AT_X + 1]
+    start_x = jnp.broadcast_to(table[:, AT_X : AT_X + 1], table.shape)
     within = (off_y >= 0) & (off_y < FOOT)
     inside = jnp.where(within, off_y, 0)
     lines = []
     for a in range(FOOT):
         picked = jnp.take_along_axis(table, inside + a * FOOT, axis=1)
         lines.append(jnp.where(within, picked, 0.0))
-    for x in range(size_x):
+
+    def at(x):
         value = jnp.zeros(table.shape, f32)
         for a in range(FOOT):
             value = jnp.where(start_x == float(x - a), lines[a], value)
-        maps_ref[x] = value
+        return value
+
+    return at
+
+
+def surface_kernel(layers, table_ref, v_ref, maps_ref, moved_ref, push_ref):
+    table = table_ref[...]
+    lane = lanes_of(table)
+    at = footprints(table)
+    for x in range(maps_ref.shape[0]):
+        maps_ref[x] = at(x)
     moved = motion(maps_ref, v_ref, layers)
     reaction = []
     rows = jnp.zeros(table.shape, f32)
     for c in range(3):
         rest, slope = (table[:, at + c : at + c + 1] for at in (AT_RATE, AT_COUPLING))
         reaction.append(time_step * FOOT * (rest - slope * moved[c]))
-        rows = jnp.where(lane == c, moved[c], rows)
+        rows = jnp.where(lane == FIRST + c, moved[c], rows)
     moved_ref[...] = rows
-    spread(maps_ref, reaction, push_ref)
-
-
-def surface_again_kernel(layers, table_ref, v_ref, maps_ref, before_ref, moved_ref, push_ref):
-    table, before = table_ref[...], before_ref[...]
-    lane = lanes_of(table)
-    moved = motion(maps_ref, v_ref, layers)
-    reaction = []
-    rows = before
-    for c in range(3):
-        rest, square, slope = (
-            table[:, at + c : at + c + 1] for at in (AT_NEXT, AT_SQUARE, AT_COUPLING)
-        )
-        rest = rest + square * before[:, c : c + 1]
-        reaction.append(time_step * FOOT * (rest - slope * moved[c]))
-        rows = jnp.where(lane == 3 + c, moved[c], rows)
-    moved_ref[...] = rows
-    spread(maps_ref, reaction, push_ref)
+    spread(lambda x: maps_ref[x], reaction, push_ref)
 
 
 def spread_thirds(moved, at, value):
@@ -502,32 +628,62 @@
     return result
 
 
-def halfway_kernel(
-    moved_ref, slot_ref, base_ref, drift_ref, coupling_ref, counts_ref, rate_out, drift_out, m_out
+def motion_again_kernel(layers, v_ref, maps_ref, before_ref, next_ref, out_ref):
+    moved = motion(maps_ref, v_ref, layers)
+    rows = before_ref[...] + next_ref[...]
+    lane = lanes_of(rows)
+    for c in range(3):
+        rows = jnp.where(lane == SECOND + c, moved[c], rows)
+    out_ref[...] = rows
+
+
+def finish_kernel(
+    sent_ref,
+    back_ref,
+    table_ref,
+    base_ref,
+    drift_ref,
+    coupling_ref,
+    counts_ref,
+    owner_ref,
+    stiff_hbm,
+    push_ref,
+    drift_out,
+    rate_out,
+    half,
+    pull,
+    stiff_ref,
+    sems,
 ):
-    moved = jnp.dot(slot_ref[...], moved_ref[...], precision=exact, preferred_element_type=f32)
-    m_out[...] = moved
+    chunks = sems.shape[0]
+    size = half.shape[0] // chunks
+    strips = [pl.ds(c * size, size) for c in range(chunks)]
+    copies = fetch([stiff_hbm.at[c] for c in strips], [stiff_ref.at[c] for c in strips], sems)
+    table, sent, back = table_ref[...], sent_ref[...], back_ref[...]
+    reaction = []
+    for c in range(3):
+        rest = back[:, AT_NEXT + c : AT_NEXT + c + 1]
+        rest = rest + table[:, AT_SQUARE + c : AT_SQUARE + c + 1] * sent[:, FIRST + c : FIRST + c + 1]
+        slope = table[:, AT_COUPLING + c : AT_COUPLING + c + 1]
+        reaction.append(time_step * FOOT * (rest - slope * sent[:, SECOND + c : SECOND + c + 1]))
+    spread(footprints(table), reaction, push_ref)
+    _, of_slot = slot_table(owner_ref, back.shape[0])
+    moved = jnp.dot(of_slot, back, precision=exact, preferred_element_type=f32)
     coupling = coupling_ref[...]
-    counts = column(counts_ref[...].astype(f32))
-    mask = lanes_of(coupling).astype(f32) < counts
-    rate = base_ref[...] + time_step * coupling * spread_thirds(moved, 0, coupling)
+    mask = counted(counts_ref, coupling.shape)
+    rate = base_ref[...] + time_step * coupling * spread_thirds(moved, FIRST, coupling)
+    rate = jnp.where(mask, rate, 0.0)
+    drift = jnp.where(mask, drift_ref[...] + time_step * rate, 0.0)
+    half[...] = drift
+    pull[...] = jnp.zeros(pull.shape, f32)
+    for c in range(chunks):
+        copies[c].wait()
+        products(stiff_ref, half, pull, c * size, (c + 1) * size)
+    relative = rate - spread_thirds(moved, SECOND, coupling)
+    rate = rate - time_step * pull[...] - time_step * coupling * relative
     rate = jnp.where(mask, rate, 0.0)
     rate_out[...] = rate
-    drift_out[...] = jnp.where(mask, drift_ref[...] + time_step * rate, 0.0)
-
-
-def end_kernel(
-    moved_ref, rate_ref, drift_ref, pull_ref, coupling_ref, counts_ref, drift_out, rate_out
-):
-    coupling = coupling_ref[...]
-    counts = column(counts_ref[...].astype(f32))
-    mask = lanes_of(coupling).astype(f32) < counts
-    rate = rate_ref[...]
-    relative = rate - spread_thirds(moved_ref[...], 3, coupling)
-    rate = rate - time_step * pull_ref[...] - time_step * coupling * relative
-    rate = jnp.where(mask, rate, 0.0)
-    rate_out[...] = rate
-    drift_out[...] = jnp.where(mask, drift_ref[...] + time_step * rate, 0.0)
+    drift_out[...] = jnp.where(mask, drift + time_step * rate, 0.0)
 
 
 def trade(rows):
@@ -535,12 +691,6 @@
     blocks = rows.reshape(devices, CAP, rows.shape[1])
     blocks = lax.all_to_all(blocks, ("gx", "gy"), split_axis=0, concat_axis=0, tiled=True)
     return blocks.reshape(rows.shape)
-
-
-def pull_of(stiffness, drift):
-    return jnp.einsum(
-        "bij,bj->bi", stiffness, drift.astype(jnp.bfloat16), preferred_element_type=f32
-    )
 
 
 def body(
@@ -579,13 +729,25 @@
 
     field = vm(cells, size_y)
     tall = layers + 2 * PAD
-    vt, up, dn, col = call(
-        bind(first_kernel, layers),
-        "edges",
-        (shape(3, cells, size_y), shape(4, layers, size_y), shape(7, layers, size_y), shape(16, cells)),
-        (v, buoy, shear),
-        [field],
-    )
+    plane = near_by(number, width)
+    dma = pltpu.SemaphoreType.DMA
+    far = (v, buoy, shear, drift_rate, coupling, contact, counts, owner, corner)
+    outs = call(
+        bind(first_kernel, layers, span),
+        "first",
+        (
+            near_by(3, cells, size_y),
+            near_by(cells, size_y),
+            near_by(cells, size_y),
+            near_by(4, layers, size_y),
+            near_by(7, layers, size_y),
+            near_by(16, cells),
+            near_by(slots, 128),
+        ),
+        [Far(a) for a in far],
+        [pltpu.VMEM(a.shape, a.dtype) for a in far] + [field, dma((len(far),))],
+    )
+    vt, bt, mt, up, dn, col, rows = outs
 
     def exchange(up, dn, col):
         west = ring(up, "gx", 1)
@@ -595,43 +757,51 @@
         return west, east, south, north
 
     halo = exchange(up, dn, col)
-    corner_rows = diagonal(dn[6])
-    counted = jnp.arange(width)[None, :] < dof_counts[:, None]
-    pull = pull_of(stiffness, jnp.where(counted, storey_drift, 0.0))
-    table, of_slot, base = call(
-        bind(table_kernel, span),
-        "table",
-        (shape(slots, 128), shape(number, slots), shape(number, width)),
-        (pull, storey_drift, drift_rate, coupling, contact, counts, owner, corner),
-    )
-    table = trade(table)
+    rows = trade(rows)
+    parts = size_x // STRIP
+    st, lt = call(
+        bind(load_kernel, layers),
+        "load",
+        (near_by(6, cells, size_y), near_by(cells, size_y)),
+        (Far(s), Far(lame)),
+        [vm(6, cells, size_y), field, dma((7,))],
+    )
     (material,) = call(
         bind(material_kernel, layers),
         "material",
-        (shape(8, cells, size_y),),
-        (buoy, lame, shear, halo[1], halo[3], corner_rows),
+        (near_by(8, cells, size_y),),
+        (bt, lt, mt, halo[1], halo[3], rows),
         [vm(size_x + 1, tall, size_y) for _ in range(4)] + [field],
     )
 
-    def stress_step(first, v, s, halo):
+    def stress_step(first, v, s, material, halo):
+        outs = [
+            near_by(6, cells, size_y),
+            near_by(5, layers, size_y),
+            near_by(4, layers, size_y),
+            near_by(16, cells),
+        ]
+        scratch = [vm(3, size_x + 4, tall, size_y), field, field]
+        if first:
+            outs += [pltpu.HBM((8, cells, size_y), f32)]
+            scratch += [dma((1,))]
         return call(
             bind(stress_kernel, layers, first),
             "stress",
-            (
-                shape(6, cells, size_y),
-                shape(5, layers, size_y),
-                shape(4, layers, size_y),
-                shape(16, cells),
-            ),
+            tuple(outs),
             (v, s, material, *halo),
-            [vm(3, size_x + 4, tall, size_y), field, field],
+            scratch,
+            far_outs=(4,),
         )
 
-    def velocity_step(last, v, s, halo, push):
-        outs = [shape(3, cells, size_y)]
+    def velocity_step(last, v, s, material, halo, push):
         scratch = [vm(5, size_x + 4, tall, size_y), field]
-        if not last:
-            outs += [shape(4, layers, size_y), shape(5, layers, size_y), shape(16, cells)]
+        if last:
+            outs = [pltpu.HBM((3, layers, parts, STRIP, size_y), f32)]
+            scratch = [vm(parts, 3, layers, STRIP, size_y)] + scratch + [dma((parts,))]
+        else:
+            outs = [near_by(3, cells, size_y)]
+            outs += [near_by(4, layers, size_y), near_by(5, layers, size_y), near_by(16, cells)]
             scratch += [field]
         return call(
             bind(velocity_kernel, layers, last),
@@ -639,41 +809,52 @@
             tuple(outs),
             (v, s, material, *halo, push),
             scratch,
+            far_outs=(0,) if last else (),
         )
 
-    st, up, dn, col = stress_step(True, vt, s, halo)
+    st, up, dn, col, kept = stress_step(True, vt, st, material, halo)
     halo = exchange(up, dn, col)
     maps, moved, push = call(
         bind(surface_kernel, layers),
         "surface",
-        (shape(size_x, slots, size_y), shape(slots, 128), shape(3, size_x, size_y)),
-        (table, vt),
-    )
-    vt, up, dn, col = velocity_step(False, vt, st, halo, push)
+        (near_by(size_x, slots, size_y), near_by(slots, 128), near_by(3, size_x, size_y)),
+        (rows, vt),
+    )
+    base, drift, following = call(
+        pull_kernel,
+        "pull",
+        (plane, plane, near_by(slots, 128)),
+        (stiffness, storey_drift, drift_rate, coupling, counts, owner),
+        [vm(number, width)],
+    )
+    push, following = lax.optimization_barrier((push, following))
+    vt, up, dn, col = velocity_step(False, vt, st, material, halo, push)
     halo = exchange(up, dn, col)
-    moved, push = call(
-        bind(surface_again_kernel, layers),
-        "surface_again",
-        (shape(slots, 128), shape(3, size_x, size_y)),
-        (table, vt, maps, moved),
-    )
-    moved = trade(moved)
-    st, up, dn, col = stress_step(False, vt, st, halo)
+    (sent,) = call(
+        bind(motion_again_kernel, layers),
+        "motion_again",
+        (near_by(slots, 128),),
+        (vt, maps, moved, following),
+    )
+    vt, sent = lax.optimization_barrier((vt, sent))
+    back = trade(sent)
+    st, up, dn, col = stress_step(False, vt, st, kept, halo)
     halo = exchange(up, dn, col)
-    rate, drift, moved = call(
-        halfway_kernel,
-        "halfway",
-        (shape(number, width), shape(number, width), shape(number, 128)),
-        (moved, of_slot, base, storey_drift, coupling, counts),
-    )
-    pull = pull_of(stiffness, drift)
-    drift, rate = call(
-        end_kernel,
-        "end",
-        (shape(number, width), shape(number, width)),
-        (moved, rate, drift, pull, coupling, counts),
-    )
-    (v,) = velocity_step(True, vt, st, halo, push)
+    sent, st = lax.optimization_barrier((sent, st))
+    chunks = 8 if number % 8 == 0 else 1
+    push, drift, rate = call(
+        finish_kernel,
+        "finish",
+        (near_by(3, size_x, size_y), shape(number, width), shape(number, width)),
+        (sent, back, rows, base, drift, coupling, counts, owner, Far(stiffness)),
+        [
+            vm(number, width),
+            vm(number, width),
+            pltpu.VMEM(stiffness.shape, stiffness.dtype),
+            dma((chunks,)),
+        ],
+    )
+    (v,) = velocity_step(True, vt, st, kept, halo, push)
     return v.reshape(soil_velocity.shape), drift, rate
 
 

time: 93.7 us -> 73.2 us (0.78)
  matrix products: 11.3 us -> 0 us
  local copies, waits for them, and re-layouts: 12.4 us -> 4.62 us
  waiting for transfers between devices: 7.95 us -> 5.54 us
  Pallas kernels: 23.9 us -> 25.3 us
  starting transfers between devices: 35.5 us -> 36.6 us
    dot_general x2 -> x0, matrix products: 11.3 us -> none  [pull_of(): jnp.einsum('bij,bj->bi', stiffness, drift.astype(jnp.bfloat16), preferred...]
    unnamed x38 -> x22, local copies, waits for them, and re-layouts: 12.4 us -> 4.62 us
    all_to_all x2, starting transfers between devices: 8.77 us -> 12.3 us  [trade(): lax.all_to_all(blocks, ('gx', 'gy'), split_axis=0, concat_axis=0, tiled=T...]
    ppermute x1 -> x0, starting transfers between devices: 2.35 us -> none  [diagonal(): return lax.ppermute(block, ('gx', 'gy'), route)]
    all_to_all x2, waiting for transfers between devices: 4.74 us -> 3.32 us  [trade(): lax.all_to_all(blocks, ('gx', 'gy'), split_axis=0, concat_axis=0, tiled=T...]
    pallas_call x11, Pallas kernels: 23.9 us -> 25.3 us  [call(): pl.pallas_call(kernel, name=name, out_shape=outs, in_specs=specs, out_spe...]
  transfers between devices with their start and end apart: 19 -> 18, of which waited for: 5 -> 4; matrix products, arithmetic and copies ran while one was open for 13% -> 0% of each run, Pallas kernels for 5% -> 17%
where the time goes in v1:
time: 73.2 us; the launch traced here: 72.9 us
  starting transfers between devices  36.6 us (50%)
  Pallas kernels  25.3 us (35%)
  waiting for transfers between devices  5.54 us (8%)
  local copies, waits for them, and re-layouts  4.62 us (6%)
  between operations  0.89 us (1%)
    pallas_call x11, Pallas kernels, call(): pl.pallas_call(kernel, name=name, out_shape=outs, in_specs=specs, out_spe...  25.3 us
    ppermute x16, starting transfers between devices, ring(): lax.ppermute(block, axis, [(i, (i + step) % size) for i in range(size)])  24.2 us
    all_to_all x2, starting transfers between devices, trade(): lax.all_to_all(blocks, ('gx', 'gy'), split_axis=0, concat_axis=0, tiled=T...  12.3 us
    unnamed x22, local copies, waits for them, and re-layouts  4.62 us
    all_to_all x2, waiting for transfers between devices, trade(): lax.all_to_all(blocks, ('gx', 'gy'), split_axis=0, concat_axis=0, tiled=T...  3.32 us
    ppermute x16, waiting for transfers between devices, ring(): lax.ppermute(block, axis, [(i, (i + step) % size) for i in range(size)])  2.22 us
  transfers between devices with their start and end apart: 18, of which 4 were waited for; matrix products, arithmetic and copies ran while one was open for 0% of the time, Pallas kernels for 17%

profile of v1, /device:TPU:0, one launch (start us, length us, event | category | flops | bytes accessed | tf_op | source)
XLA Modules:
  0.0 72.9 jit_solution(2513907210138266138)
XLA Ops:
  0.6 3.0 %first.1 = (f32[3,512,128]{2,1,0:T(8,128)S(1)}, f32[512,128]{1,0:T(8,128)S(1)}, f32[512,128]{1,0:T(8,128)S(1)}, f32[4,32,128]{2,1,0:T(8,128)S(1)}, f32[7,32,128]...) custom-call(f32[3,512,128]{2,1,0:T(8,128)} %bitcast.24, f32[512,128]{1,0:T(8,128)} %bitcast.27, ...), custom_call_target="tpu_custom_call" | custom-call | flops 30000000 | bytes 30000000 | tf_op jit(solution)/shard_map/first/pallas_call | solution.py:49
  3.6 3.4 %collective-permute-start = (f32[7,32,128]{2,1,0:T(8,128)}, f32[7,32,128]{2,1,0:T(8,128)S(1)}, u32[]{:S(2)}, u32[]{:S(2)}) collective-permute-start(f32[7,32,128]{2,1,0:T(8,128)} %get-tuple-element.45), channel_id=1, source_target_pairs={{0,28},{4,0},{8,4},{12,8},{16,12},{20,16},{24,20},{28,24},{1,29},{... | collective-permute-start | bytes 344072 | tf_op jit(solution)/shard_map/ppermute | solution.py:84
  7.0 0.0 collective-permute-start.2
  7.0 6.0 %all-to-all-start = ((f32[32,2,128]{2,1,0:T(2,128)}), f32[32,2,128]{2,1,0:T(2,128)S(1)}, u32[]{:S(2)}, u32[]{:S(2)}) async-start(f32[32,2,128]{2,1,0:T(2,128)} %bitcast.8), calls=%async_computation | async-start | bytes 65536 | tf_op jit(solution)/shard_map/all_to_all | solution.py:692
  13.1 3.7 %collective-permute-start.1 = (f32[16,512]{1,0:T(8,128)S(1)}, f32[16,512]{1,0:T(8,128)S(1)}, u32[]{:S(2)}, u32[]{:S(2)}) collective-permute-start(f32[16,512]{1,0:T(8,128)S(1)} %get-tuple-element.46), channel_id=1, source_target_pairs={{0,3},{1,0},{2,1},{3,2},{4,7},{5,4},{6,5},{7,6},{8,11},{9,8},{10,9... | collective-permute-start | bytes 98312 | tf_op jit(solution)/shard_map/ppermute | solution.py:84
  16.8 0.0 collective-permute-start.3
  16.8 1.6 %load.1 = (f32[6,512,128]{2,1,0:T(8,128)S(1)}, f32[512,128]{1,0:T(8,128)S(1)}) custom-call(f32[6,512,128]{2,1,0:T(8,128)} %bitcast.23, f32[512,128]{1,0:T(8,128)} %bitcast.26), custom_call_target="tpu_custom_call" | custom-call | flops 20000000 | bytes 20000000 | tf_op jit(solution)/shard_map/load/pallas_call | solution.py:49
  18.4 0.0 collective-permute-done.1.refs_4_.refs_6_
  18.4 2.1 %all-to-all-done = f32[32,2,128]{2,1,0:T(2,128)S(1)} async-done(((f32[32,2,128]{2,1,0:T(2,128)}), f32[32,2,128]{2,1,0:T(2,128)S(1)}, u32[]{:S(2)}, u32[]{:S(2)}) %all-to-all-start) | async-done | bytes 32800 | tf_op jit(solution)/shard_map/all_to_all | solution.py:692
  20.5 0.0 collective-permute-done.refs_3_.refs_4_
  20.5 0.9 %material.1.refs_2_ = f32[8,512,128]{2,1,0:T(8,128)S(1)} custom-call(f32[512,128]{1,0:T(8,128)S(1)} %get-tuple-element.42.refs_0_, f32[512,128]{1,0:T(8,128)S(1)} %get-tuple-element.43.refs_1_, f32[512,128]{1,0:T(8,128)S(1)} %get-tuple-element.44.refs_2_, f32[7,32,128]{2,1,0:T(8,128)S(1)} %collective-permute-done.refs_3_.refs_4_, ...), custom_call_target="tpu_custom_call" | custom-call | flops 10000000 | bytes 10000000 | tf_op jit(solution)/shard_map/material/pallas_call | solution.py:49
  21.4 1.1 %collective-permute-done.3.refs_5_ = f32[16,512]{1,0:T(8,128)S(1)} collective-permute-done((f32[16,512]{1,0:T(8,128)S(1)}, f32[16,512]{1,0:T(8,128)S(1)}, u32[]{:S(2)}, u32[]{:S(2)}) %collective-permute-start.3) | collective-permute-done | bytes 32800 | tf_op jit(solution)/shard_map/ppermute | solution.py:84
  22.5 0.0 collective-permute-done.2.refs_3_
  22.5 0.0 copy-start.6
  22.5 0.0 copy-start.7
  22.5 0.0 copy-start.9
  22.5 0.0 copy-start.10
  22.5 2.3 %stress.2 = (f32[6,512,128]{2,1,0:T(8,128)S(1)}, f32[5,32,128]{2,1,0:T(8,128)S(1)}, f32[4,32,128]{2,1,0:T(8,128)S(1)}, f32[16,512]{1,0:T(8,128)S(1)}, f32[8,512,128]{2,1,0:T(8,128)}) custom-call(f32[3,512,128]{2,1,0:T(8,128)S(1)} %get-tuple-element.40.refs_0_.refs_1_, f32[6,512,128]{2,1,0:T(8,128)S(1)} %get-tuple-element.41.refs_1_, ...), custom_call_target="tpu_custom_call" | custom-call | flops 25000000 | bytes 25000000 | tf_op jit(solution)/shard_map/stress/pallas_call | solution.py:49
  24.8 0.1 collective-permute-start.4
  24.9 2.6 %collective-permute-start.5 = (f32[4,32,128]{2,1,0:T(8,128)S(1)}, f32[4,32,128]{2,1,0:T(8,128)S(1)}, u32[]{:S(2)}, u32[]{:S(2)}) collective-permute-start(f32[4,32,128]{2,1,0:T(8,128)S(1)} %get-tuple-element.51), channel_id=1, source_target_pairs={{0,28},{4,0},{8,4},{12,8},{16,12},{20,16},{24,20},{28,24},{1,29},{... | collective-permute-start | bytes 196616 | tf_op jit(solution)/shard_map/ppermute | solution.py:84
  27.5 0.0 collective-permute-start.6
  27.5 3.8 %collective-permute-start.7 = (f32[16,512]{1,0:T(8,128)S(1)}, f32[16,512]{1,0:T(8,128)S(1)}, u32[]{:S(2)}, u32[]{:S(2)}) collective-permute-start(f32[16,512]{1,0:T(8,128)S(1)} %get-tuple-element.52), channel_id=1, source_target_pairs={{0,3},{1,0},{2,1},{3,2},{4,7},{5,4},{6,5},{7,6},{8,11},{9,8},{10,9... | collective-permute-start | bytes 98312 | tf_op jit(solution)/shard_map/ppermute | solution.py:84
  31.4 0.0 copy-done.6
  31.4 0.0 copy-done.7
  31.4 0.0 copy-done.8
  31.4 0.0 copy-done.9
  31.4 0.0 copy-done.10
  31.4 0.0 copy-start
  31.4 3.4 %copy-done = bf16[64,256,256]{2,1,0:T(8,128)(2,1)S(1)} copy-done((bf16[64,256,256]{2,1,0:T(8,128)(2,1)S(1)}, bf16[64,256,256]{2,1,0:T(8,128)(2,1)}, u32[]{:S(2)}) %copy-start) | copy-done | bytes 8388632
  34.8 2.5 %pull.1 = (f32[64,256]{1,0:T(8,128)S(1)}, f32[64,256]{1,0:T(8,128)S(1)}, f32[64,128]{1,0:T(8,128)S(1)}) custom-call(bf16[64,256,256]{2,1,0:T(8,128)(2,1)S(1)} %copy-done, f32[64,256]{1,0:T(8,128)S(1)} %copy-done.8, f32[64,256]{1,0:T(8,128)S(1)} %copy-done.7, f32[64,256]{1,0:T(8,128)S(1)} %copy-done.6, s32[1,64]{1,0:T(1,128)S(1)} %bitcast.18, ...), custom_call_target="tpu_custom_call" | custom-call | flops 30000000 | bytes 30000000 | tf_op jit(solution)/shard_map/pull/pallas_call | solution.py:49
  37.3 0.8 %surface.1 = (f32[16,64,128]{2,1,0:T(8,128)S(1)}, f32[64,128]{1,0:T(8,128)S(1)}, f32[3,16,128]{2,1,0:T(8,128)S(1)}) custom-call(f32[64,128]{1,0:T(8,128)S(1)} %bitcast.14, f32[3,512,128]{2,1,0:T(8,128)S(1)} %get-tuple-element.40.refs_0_.refs_1_), custom_call_target="tpu_custom_call" | custom-call | flops 10000000 | bytes 10000000 | tf_op jit(solution)/shard_map/surface/pallas_call | solution.py:49
  38.2 0.0 collective-permute-done.6.refs_5_
  38.2 0.0 collective-permute-done.7.refs_6_
  38.2 0.0 collective-permute-done.5.refs_4_
  38.2 0.0 collective-permute-done.4.refs_3_
  38.2 0.0 copy-start.1
  38.2 2.3 %velocity.2 = (f32[3,512,128]{2,1,0:T(8,128)S(1)}, f32[4,32,128]{2,1,0:T(8,128)S(1)}, f32[5,32,128]{2,1,0:T(8,128)S(1)}, f32[16,512]{1,0:T(8,128)S(1)}) custom-call(f32[3,512,128]{2,1,0:T(8,128)S(1)} %get-tuple-element.40.refs_0_.refs_1_, f32[6,512,128]{2,1,0:T(8,128)S(1)} %get-tuple-element.49.refs_1_, f32[8,512,128]{2,1,0:T(8,128)S(1)} %material.1.refs_2_, ...), custom_call_target="tpu_custom_call" | custom-call | flops 25000000 | bytes 25000000 | tf_op jit(solution)/shard_map/velocity/pallas_call | solution.py:49
  40.5 0.0 collective-permute-start.9
  40.6 0.5 collective-permute-start.8
  41.1 0.0 collective-permute-start.10
  41.1 3.8 %collective-permute-start.11 = (f32[16,512]{1,0:T(8,128)S(1)}, f32[16,512]{1,0:T(8,128)S(1)}, u32[]{:S(2)}, u32[]{:S(2)}) collective-permute-start(f32[16,512]{1,0:T(8,128)S(1)} %get-tuple-element.65), channel_id=1, source_target_pairs={{0,3},{1,0},{2,1},{3,2},{4,7},{5,4},{6,5},{7,6},{8,11},{9,8},{10,9... | collective-permute-start | bytes 98312 | tf_op jit(solution)/shard_map/ppermute | solution.py:84
  44.9 0.8 %motion_again.1.sent_ref = f32[64,128]{1,0:T(8,128)} custom-call(f32[3,512,128]{2,1,0:T(8,128)S(1)} %get-tuple-element.60.refs_0_, f32[16,64,128]{2,1,0:T(8,128)S(1)} %get-tuple-element.57.refs_1_, f32[64,128]{1,0:T(8,128)S(1)} %get-tuple-element.58.refs_2_, f32[64,128]{1,0:T(8,128)S(1)} %get-tuple-element.59.refs_3_), custom_call_target="tpu_custom_call" | custom-call | flops 10000000 | bytes 10000000 | tf_op jit(solution)/shard_map/motion_again/pallas_call | solution.py:49
  45.7 1.1 %collective-permute-done.10.refs_5_ = f32[16,512]{1,0:T(8,128)S(1)} collective-permute-done((f32[16,512]{1,0:T(8,128)S(1)}, f32[16,512]{1,0:T(8,128)S(1)}, u32[]{:S(2)}, u32[]{:S(2)}) %collective-permute-start.10) | collective-permute-done | bytes 32800 | tf_op jit(solution)/shard_map/ppermute | solution.py:84
  46.8 0.0 collective-permute-done.11.refs_6_
  46.8 0.0 collective-permute-done.8.refs_3_
  46.8 0.0 collective-permute-done.9.refs_4_
  46.8 0.0 copy-done.1
  46.8 2.3 %stress.3 = (f32[6,512,128]{2,1,0:T(8,128)S(1)}, f32[5,32,128]{2,1,0:T(8,128)S(1)}, f32[4,32,128]{2,1,0:T(8,128)S(1)}, f32[16,512]{1,0:T(8,128)S(1)}) custom-call(f32[3,512,128]{2,1,0:T(8,128)S(1)} %get-tuple-element.60.refs_0_, f32[6,512,128]{2,1,0:T(8,128)S(1)} %get-tuple-element.49.refs_1_, f32[8,512,128]{2,1,0:T(8,128)S(1)} %copy-done.1, ...), custom_call_target="tpu_custom_call" | custom-call | flops 25000000 | bytes 25000000 | tf_op jit(solution)/shard_map/stress/pallas_call | solution.py:49
  49.1 0.0 copy-done.2
  49.1 1.2 %copy-done.4 = f32[6,512,128]{2,1,0:T(8,128)} copy-done((f32[6,512,128]{2,1,0:T(8,128)}, f32[6,512,128]{2,1,0:T(8,128)S(1)}, u32[]{:S(2)}) %copy-start.4) | copy-done | bytes 1572888
  50.3 0.0 collective-permute-start.12
  50.3 6.3 %all-to-all-start.1 = ((f32[32,2,128]{2,1,0:T(2,128)}), f32[32,2,128]{2,1,0:T(2,128)S(1)}, u32[]{:S(2)}, u32[]{:S(2)}) async-start(f32[32,2,128]{2,1,0:T(2,128)} %bitcast.10), calls=%async_computation.1 | async-start | bytes 65536 | tf_op jit(solution)/shard_map/all_to_all | solution.py:692
  56.6 2.5 %collective-permute-start.13 = (f32[4,32,128]{2,1,0:T(8,128)S(1)}, f32[4,32,128]{2,1,0:T(8,128)S(1)}, u32[]{:S(2)}, u32[]{:S(2)}) collective-permute-start(f32[4,32,128]{2,1,0:T(8,128)S(1)} %get-tuple-element.69), channel_id=1, source_target_pairs={{0,28},{4,0},{8,4},{12,8},{16,12},{20,16},{24,20},{28,24},{1,29},{... | collective-permute-start | bytes 196616 | tf_op jit(solution)/shard_map/ppermute | solution.py:84
  59.1 1.5 %collective-permute-start.14 = (f32[16,512]{1,0:T(8,128)S(1)}, f32[16,512]{1,0:T(8,128)S(1)}, u32[]{:S(2)}, u32[]{:S(2)}) collective-permute-start(f32[16,512]{1,0:T(8,128)S(1)} %get-tuple-element.70), channel_id=1, source_target_pairs={{0,1},{1,2},{2,3},{3,0},{4,5},{5,6},{6,7},{7,4},{8,9},{9,10},{10,1... | collective-permute-start | bytes 98312 | tf_op jit(solution)/shard_map/ppermute | solution.py:84
  60.6 2.4 %collective-permute-start.15 = (f32[16,512]{1,0:T(8,128)S(1)}, f32[16,512]{1,0:T(8,128)S(1)}, u32[]{:S(2)}, u32[]{:S(2)}) collective-permute-start(f32[16,512]{1,0:T(8,128)S(1)} %get-tuple-element.70), channel_id=1, source_target_pairs={{0,3},{1,0},{2,1},{3,2},{4,7},{5,4},{6,5},{7,6},{8,11},{9,8},{10,9... | collective-permute-start | bytes 98312 | tf_op jit(solution)/shard_map/ppermute | solution.py:84
  62.9 1.3 %all-to-all-done.1 = f32[32,2,128]{2,1,0:T(2,128)S(1)} async-done(((f32[32,2,128]{2,1,0:T(2,128)}), f32[32,2,128]{2,1,0:T(2,128)S(1)}, u32[]{:S(2)}, u32[]{:S(2)}) %all-to-all-start.1) | async-done | bytes 32800 | tf_op jit(solution)/shard_map/all_to_all | solution.py:692
  64.2 6.0 %finish.1 = (f32[3,16,128]{2,1,0:T(8,128)S(1)}, f32[64,256]{1,0:T(8,128)}, f32[64,256]{1,0:T(8,128)}) custom-call(f32[64,128]{1,0:T(8,128)} %motion_again.1.sent_ref, f32[64,128]{1,0:T(8,128)S(1)} %bitcast.16, f32[64,128]{1,0:T(8,128)S(1)} %bitcast.15, f32[64,256]{1,0:T(8,128)S(1)} %get-tuple-element.72.base_ref, f32[64,256]{1,0:T(8,128)S(1)} %get-tuple-element.73.drift_ref, ...), custom_call_target="tpu_custom_call" | custom-call | flops 60000000 | bytes 60000000 | tf_op jit(solution)/shard_map/finish/pallas_call | solution.py:49
  70.2 0.0 collective-permute-done.14.refs_5_
  70.2 0.0 collective-permute-done.15.refs_6_
  70.2 0.0 collective-permute-done.13.refs_4_
  70.2 0.0 collective-permute-done.12.refs_3_
  70.2 0.0 copy-done.3
  70.2 0.0 copy-done.5
  70.2 2.7 %velocity.3 = f32[3,32,2,8,128]{4,3,2,1,0:T(8,128)} custom-call(f32[3,512,128]{2,1,0:T(8,128)S(1)} %copy-done.3, f32[6,512,128]{2,1,0:T(8,128)S(1)} %copy-done.5, f32[8,512,128]{2,1,0:T(8,128)S(1)} %copy-done.1, f32[5,32,128]{2,1,0:T(8,128)S(1)} %collective-permute-done.12.refs_3_, f32[4,32,128]{2,1,0:T(8,128)S(1)} %collective-permute-done.13.refs_4_, ...), custom_call_target="tpu_custom_call" | custom-call | flops 25000000 | bytes 25000000 | tf_op jit(solution)/shard_map/velocity/pallas_call | solution.py:49
  (5 shorter events, 0.0 us)
Async XLA Ops:
  3.6 16.8 %collective-permute-start = (f32[7,32,128]{2,1,0:T(8,128)}, f32[7,32,128]{2,1,0:T(8,128)S(1)}, u32[]{:S(2)}, u32[]{:S(2)}) collective-permute-start(f32[7,32,128]{2,1,0:T(8,128)} %get-tuple-element.45), channel_id=1, source_target_pairs={{0,28},{4,0},{8,4},{12,8},{16,12},{20,16},{24,20},{28,24},{1,29},{... | collective-permute-start | bytes 344072 | tf_op jit(solution)/shard_map/ppermute | solution.py:84
  7.0 15.4 %collective-permute-start.2 = (f32[4,32,128]{2,1,0:T(8,128)S(1)}, f32[4,32,128]{2,1,0:T(8,128)S(1)}, u32[]{:S(2)}, u32[]{:S(2)}) collective-permute-start(f32[4,32,128]{2,1,0:T(8,128)S(1)} %get-tuple-element.48), channel_id=1, source_target_pairs={{0,4},{4,8},{8,12},{12,16},{16,20},{20,24},{24,28},{28,0},{1,5},{5... | collective-permute-start | bytes 196616 | tf_op jit(solution)/shard_map/ppermute | solution.py:84
  7.0 13.4 %all-to-all-start = ((f32[32,2,128]{2,1,0:T(2,128)}), f32[32,2,128]{2,1,0:T(2,128)S(1)}, u32[]{:S(2)}, u32[]{:S(2)}) async-start(f32[32,2,128]{2,1,0:T(2,128)} %bitcast.8), calls=%async_computation | async-start | bytes 65536 | tf_op jit(solution)/shard_map/all_to_all | solution.py:692
  13.1 5.3 %collective-permute-start.1 = (f32[16,512]{1,0:T(8,128)S(1)}, f32[16,512]{1,0:T(8,128)S(1)}, u32[]{:S(2)}, u32[]{:S(2)}) collective-permute-start(f32[16,512]{1,0:T(8,128)S(1)} %get-tuple-element.46), channel_id=1, source_target_pairs={{0,3},{1,0},{2,1},{3,2},{4,7},{5,4},{6,5},{7,6},{8,11},{9,8},{10,9... | collective-permute-start | bytes 98312 | tf_op jit(solution)/shard_map/ppermute | solution.py:84
  16.8 5.7 %collective-permute-start.3 = (f32[16,512]{1,0:T(8,128)S(1)}, f32[16,512]{1,0:T(8,128)S(1)}, u32[]{:S(2)}, u32[]{:S(2)}) collective-permute-start(f32[16,512]{1,0:T(8,128)S(1)} %get-tuple-element.46), channel_id=1, source_target_pairs={{0,1},{1,2},{2,3},{3,0},{4,5},{5,6},{6,7},{7,4},{8,9},{9,10},{10,1... | collective-permute-start | bytes 98312 | tf_op jit(solution)/shard_map/ppermute | solution.py:84
  22.5 8.9 %copy-start.6 = (f32[64,256]{1,0:T(8,128)S(1)}, f32[64,256]{1,0:T(8,128)}, u32[]{:S(2)}) copy-start(f32[64,256]{1,0:T(8,128)} %coupling_ref.3) | copy-start | bytes 196612
  22.5 8.9 %copy-start.7 = (f32[64,256]{1,0:T(8,128)S(1)}, f32[64,256]{1,0:T(8,128)}, u32[]{:S(2)}) copy-start(f32[64,256]{1,0:T(8,128)} %rate_ref.1) | copy-start | bytes 196612
  22.5 8.9 %copy-start.8 = (f32[64,256]{1,0:T(8,128)S(1)}, f32[64,256]{1,0:T(8,128)}, u32[]{:S(2)}) copy-start(f32[64,256]{1,0:T(8,128)} %raw_ref.1) | copy-start | bytes 196612
  22.5 8.9 %copy-start.9 = (s32[64]{0:T(128)S(1)}, s32[64]{0:T(128)}, u32[]{:S(2)}) copy-start(s32[64]{0:T(128)} %param.23) | copy-start | bytes 772
  22.5 8.9 %copy-start.10 = (s32[64,1]{0,1:T(1,128)S(1)}, s32[64,1]{0,1:T(1,128)}, u32[]{:S(2)}) copy-start(s32[64,1]{0,1:T(1,128)} %param.24) | copy-start | bytes 772
  24.8 13.4 %collective-permute-start.4 = (f32[5,32,128]{2,1,0:T(8,128)S(1)}, f32[5,32,128]{2,1,0:T(8,128)S(1)}, u32[]{:S(2)}, u32[]{:S(2)}) collective-permute-start(f32[5,32,128]{2,1,0:T(8,128)S(1)} %get-tuple-element.50), channel_id=1, source_target_pairs={{0,4},{4,8},{8,12},{12,16},{16,20},{20,24},{24,28},{28,0},{1,5},{5... | collective-permute-start | bytes 245768 | tf_op jit(solution)/shard_map/ppermute | solution.py:84
  24.9 13.3 %collective-permute-start.5 = (f32[4,32,128]{2,1,0:T(8,128)S(1)}, f32[4,32,128]{2,1,0:T(8,128)S(1)}, u32[]{:S(2)}, u32[]{:S(2)}) collective-permute-start(f32[4,32,128]{2,1,0:T(8,128)S(1)} %get-tuple-element.51), channel_id=1, source_target_pairs={{0,28},{4,0},{8,4},{12,8},{16,12},{20,16},{24,20},{28,24},{1,29},{... | collective-permute-start | bytes 196616 | tf_op jit(solution)/shard_map/ppermute | solution.py:84
  27.5 10.6 %collective-permute-start.6 = (f32[16,512]{1,0:T(8,128)S(1)}, f32[16,512]{1,0:T(8,128)S(1)}, u32[]{:S(2)}, u32[]{:S(2)}) collective-permute-start(f32[16,512]{1,0:T(8,128)S(1)} %get-tuple-element.52), channel_id=1, source_target_pairs={{0,1},{1,2},{2,3},{3,0},{4,5},{5,6},{6,7},{7,4},{8,9},{9,10},{10,1... | collective-permute-start | bytes 98312 | tf_op jit(solution)/shard_map/ppermute | solution.py:84
  27.5 10.6 %collective-permute-start.7 = (f32[16,512]{1,0:T(8,128)S(1)}, f32[16,512]{1,0:T(8,128)S(1)}, u32[]{:S(2)}, u32[]{:S(2)}) collective-permute-start(f32[16,512]{1,0:T(8,128)S(1)} %get-tuple-element.52), channel_id=1, source_target_pairs={{0,3},{1,0},{2,1},{3,2},{4,7},{5,4},{6,5},{7,6},{8,11},{9,8},{10,9... | collective-permute-start | bytes 98312 | tf_op jit(solution)/shard_map/ppermute | solution.py:84
  31.4 3.4 %copy-start = (bf16[64,256,256]{2,1,0:T(8,128)(2,1)S(1)}, bf16[64,256,256]{2,1,0:T(8,128)(2,1)}, u32[]{:S(2)}) copy-start(bf16[64,256,256]{2,1,0:T(8,128)(2,1)} %stiff_hbm.1) | copy-start | bytes 25165828
  38.2 8.6 %copy-start.1 = (f32[8,512,128]{2,1,0:T(8,128)S(1)}, f32[8,512,128]{2,1,0:T(8,128)}, u32[]{:S(2)}) copy-start(f32[8,512,128]{2,1,0:T(8,128)} %get-tuple-element.62.refs_2_) | copy-start | bytes 6291460
  40.5 8.6 %copy-start.2 = (f32[3,512,128]{2,1,0:T(8,128)}, f32[3,512,128]{2,1,0:T(8,128)S(1)}, u32[]{:S(2)}) copy-start(f32[3,512,128]{2,1,0:T(8,128)S(1)} %get-tuple-element.60.refs_0_) | copy-start | bytes 2359300
  40.5 6.3 %collective-permute-start.9 = (f32[5,32,128]{2,1,0:T(8,128)S(1)}, f32[5,32,128]{2,1,0:T(8,128)S(1)}, u32[]{:S(2)}, u32[]{:S(2)}) collective-permute-start(f32[5,32,128]{2,1,0:T(8,128)S(1)} %get-tuple-element.64), channel_id=1, source_target_pairs={{0,28},{4,0},{8,4},{12,8},{16,12},{20,16},{24,20},{28,24},{1,29},{... | collective-permute-start | bytes 245768 | tf_op jit(solution)/shard_map/ppermute | solution.py:84
  40.6 6.2 %collective-permute-start.8 = (f32[4,32,128]{2,1,0:T(8,128)S(1)}, f32[4,32,128]{2,1,0:T(8,128)S(1)}, u32[]{:S(2)}, u32[]{:S(2)}) collective-permute-start(f32[4,32,128]{2,1,0:T(8,128)S(1)} %get-tuple-element.63), channel_id=1, source_target_pairs={{0,4},{4,8},{8,12},{12,16},{16,20},{20,24},{24,28},{28,0},{1,5},{5... | collective-permute-start | bytes 196616 | tf_op jit(solution)/shard_map/ppermute | solution.py:84
  41.1 5.7 %collective-permute-start.10 = (f32[16,512]{1,0:T(8,128)S(1)}, f32[16,512]{1,0:T(8,128)S(1)}, u32[]{:S(2)}, u32[]{:S(2)}) collective-permute-start(f32[16,512]{1,0:T(8,128)S(1)} %get-tuple-element.65), channel_id=1, source_target_pairs={{0,1},{1,2},{2,3},{3,0},{4,5},{5,6},{6,7},{7,4},{8,9},{9,10},{10,1... | collective-permute-start | bytes 98312 | tf_op jit(solution)/shard_map/ppermute | solution.py:84
  41.1 5.7 %collective-permute-start.11 = (f32[16,512]{1,0:T(8,128)S(1)}, f32[16,512]{1,0:T(8,128)S(1)}, u32[]{:S(2)}, u32[]{:S(2)}) collective-permute-start(f32[16,512]{1,0:T(8,128)S(1)} %get-tuple-element.65), channel_id=1, source_target_pairs={{0,3},{1,0},{2,1},{3,2},{4,7},{5,4},{6,5},{7,6},{8,11},{9,8},{10,9... | collective-permute-start | bytes 98312 | tf_op jit(solution)/shard_map/ppermute | solution.py:84
  49.1 1.2 %copy-start.4 = (f32[6,512,128]{2,1,0:T(8,128)}, f32[6,512,128]{2,1,0:T(8,128)S(1)}, u32[]{:S(2)}) copy-start(f32[6,512,128]{2,1,0:T(8,128)S(1)} %get-tuple-element.67.refs_1_) | copy-start | bytes 4718596
  50.3 19.9 %collective-permute-start.12 = (f32[5,32,128]{2,1,0:T(8,128)S(1)}, f32[5,32,128]{2,1,0:T(8,128)S(1)}, u32[]{:S(2)}, u32[]{:S(2)}) collective-permute-start(f32[5,32,128]{2,1,0:T(8,128)S(1)} %get-tuple-element.68), channel_id=1, source_target_pairs={{0,4},{4,8},{8,12},{12,16},{16,20},{20,24},{24,28},{28,0},{1,5},{5... | collective-permute-start | bytes 245768 | tf_op jit(solution)/shard_map/ppermute | solution.py:84
  50.3 13.9 %all-to-all-start.1 = ((f32[32,2,128]{2,1,0:T(2,128)}), f32[32,2,128]{2,1,0:T(2,128)S(1)}, u32[]{:S(2)}, u32[]{:S(2)}) async-start(f32[32,2,128]{2,1,0:T(2,128)} %bitcast.10), calls=%async_computation.1 | async-start | bytes 65536 | tf_op jit(solution)/shard_map/all_to_all | solution.py:692
  56.6 13.6 %collective-permute-start.13 = (f32[4,32,128]{2,1,0:T(8,128)S(1)}, f32[4,32,128]{2,1,0:T(8,128)S(1)}, u32[]{:S(2)}, u32[]{:S(2)}) collective-permute-start(f32[4,32,128]{2,1,0:T(8,128)S(1)} %get-tuple-element.69), channel_id=1, source_target_pairs={{0,28},{4,0},{8,4},{12,8},{16,12},{20,16},{24,20},{28,24},{1,29},{... | collective-permute-start | bytes 196616 | tf_op jit(solution)/shard_map/ppermute | solution.py:84
  59.1 11.1 %collective-permute-start.14 = (f32[16,512]{1,0:T(8,128)S(1)}, f32[16,512]{1,0:T(8,128)S(1)}, u32[]{:S(2)}, u32[]{:S(2)}) collective-permute-start(f32[16,512]{1,0:T(8,128)S(1)} %get-tuple-element.70), channel_id=1, source_target_pairs={{0,1},{1,2},{2,3},{3,0},{4,5},{5,6},{6,7},{7,4},{8,9},{9,10},{10,1... | collective-permute-start | bytes 98312 | tf_op jit(solution)/shard_map/ppermute | solution.py:84
  60.6 9.6 %collective-permute-start.15 = (f32[16,512]{1,0:T(8,128)S(1)}, f32[16,512]{1,0:T(8,128)S(1)}, u32[]{:S(2)}, u32[]{:S(2)}) collective-permute-start(f32[16,512]{1,0:T(8,128)S(1)} %get-tuple-element.70), channel_id=1, source_target_pairs={{0,3},{1,0},{2,1},{3,2},{4,7},{5,4},{6,5},{7,6},{8,11},{9,8},{10,9... | collective-permute-start | bytes 98312 | tf_op jit(solution)/shard_map/ppermute | solution.py:84
  64.2 6.0 %copy-start.3 = (f32[3,512,128]{2,1,0:T(8,128)S(1)}, f32[3,512,128]{2,1,0:T(8,128)}, u32[]{:S(2)}) copy-start(f32[3,512,128]{2,1,0:T(8,128)} %copy-done.2) | copy-start | bytes 2359300
  64.2 6.0 %copy-start.5 = (f32[6,512,128]{2,1,0:T(8,128)S(1)}, f32[6,512,128]{2,1,0:T(8,128)}, u32[]{:S(2)}) copy-start(f32[6,512,128]{2,1,0:T(8,128)} %copy-done.4) | copy-start | bytes 4718596

commit v2 on v1

--- a/solution.py
+++ b/solution.py
@@ -8,7 +8,8 @@
 FOOT = 8
 CAP = 2
 PAD = 8
-STRIP = 8
+STRIP = 4
+TILE = 8
 
 near = 9.0 / 8.0
 far = 1.0 / 24.0
@@ -22,8 +23,7 @@
 
 COSTS = {
     "first": 30_000_000,
-    "load": 20_000_000,
-    "material": 10_000_000,
+    "begin": 40_000_000,
     "stress": 25_000_000,
     "surface": 10_000_000,
     "pull": 30_000_000,
@@ -56,7 +56,7 @@
             for i in range(len(outs))
         ),
         scratch_shapes=list(scratch),
-        cost_estimate=pl.CostEstimate(flops=cost, bytes_accessed=cost, transcendentals=0),
+        cost_estimate=pl.CostEstimate(flops=1000*cost, bytes_accessed=cost, transcendentals=0),
         compiler_params=pltpu.CompilerParams(vmem_limit_bytes=16 * 2**20),
     )(*values)
 
@@ -79,9 +79,36 @@
     return copies
 
 
-def ring(block, axis, step):
+def swap(block, axis, odd):
     size = lax.axis_size(axis)
-    return lax.ppermute(block, axis, [(i, (i + step) % size) for i in range(size)])
+    pairs = [(i % size, (i + 1) % size) for i in range(odd, size + odd, 2)]
+    return lax.ppermute(block, axis, pairs + [(b, a) for a, b in pairs])
+
+
+def even(axis):
+    return lax.rem(lax.axis_index(axis), 2) == 0
+
+
+def two_ways(up, down, even_ref, odd_ref):
+    lead = even("gx")
+    blank = jnp.zeros(even_ref.shape[1:], f32)
+    for row in range(even_ref.shape[0]):
+        a = up[row] if row < len(up) else blank
+        b = down[row] if row < len(down) else blank
+        even_ref[row] = jnp.where(lead, a, b)
+        odd_ref[row] = jnp.where(lead, b, a)
+
+
+def below_above(axis, even_ref, odd_ref):
+    lead = even(axis)
+
+    def below(index):
+        return jnp.where(lead, odd_ref[index], even_ref[index])
+
+    def above(index):
+        return jnp.where(lead, even_ref[index], odd_ref[index])
+
+    return below, above
 
 
 def lanes_of(value):
@@ -111,12 +138,13 @@
         out_ref[:, block * 128 : (block + 1) * 128] = part.T[:rows]
 
 
-def receive_columns(south_ref, north_ref, from_south, south_ok, north_ok, out_ref):
-    rows, width = south_ref.shape
+def receive_columns(even_ref, odd_ref, from_south, south_ok, north_ok, out_ref):
+    rows, width = even_ref.shape
+    below, above = below_above("gy", even_ref, odd_ref)
     for block in range(width // 128):
         cut = slice(block * 128, (block + 1) * 128)
-        south = jnp.where(south_ok, south_ref[:, cut], 0.0)
-        north = jnp.where(north_ok, north_ref[:, cut], 0.0)
+        south = jnp.where(south_ok, below((slice(None), cut)), 0.0)
+        north = jnp.where(north_ok, above((slice(None), cut)), 0.0)
         row = lax.broadcasted_iota(jnp.int32, south.shape, 0)
         taken = row == from_south[0]
         for other in from_south[1:]:
@@ -169,66 +197,35 @@
         ext[c, x + 2, PAD + layers : PAD + layers + PAD, :] = jnp.zeros((PAD, 128), f32)
 
 
-def edges(layers, v_ref, b_ref, m_ref, vt_ref, bt_ref, mt_ref, up_ref, dn_ref, col_ref, pack):
-    size_x = v_ref.shape[1] // layers
+def edges(layers, arrived, vt_ref, bt_ref, mt_ref, even_ref, odd_ref, col_ref, pack):
+    size_x = vt_ref.shape[1] // layers
+
+    def slab(ref, x):
+        return ref[x * layers : (x + 1) * layers, :]
+
     for x in range(size_x):
-        cut = pl.ds(x * layers, layers)
-        slab = [v_ref[c, pl.ds(x, layers, stride=size_x), :] for c in range(3)]
-        buoy = b_ref[pl.ds(x, layers, stride=size_x), :]
-        shear = m_ref[pl.ds(x, layers, stride=size_x), :]
-        for c in range(3):
-            vt_ref[c, cut, :] = slab[c]
-        bt_ref[cut, :] = buoy
-        mt_ref[cut, :] = shear
-        pack[cut, :] = packed(
+        arrived(x)
+        pack[x * layers : (x + 1) * layers, :] = packed(
             [
-                (slab[0], 0, 3, 1),
-                (slab[1], 3, 3, 5),
-                (slab[2], 6, 3, 7),
-                (buoy, 9, 1, 9),
-                (shear, 10, 1, 10),
+                (slab(vt_ref.at[0], x), 0, 3, 1),
+                (slab(vt_ref.at[1], x), 3, 3, 5),
+                (slab(vt_ref.at[2], x), 6, 3, 7),
+                (slab(bt_ref, x), 9, 1, 9),
+                (slab(mt_ref, x), 10, 1, 10),
             ]
         )
-        if x == 0:
-            dn_ref[0] = slab[0]
-            dn_ref[1] = slab[1]
-            dn_ref[3] = slab[2]
-            dn_ref[5] = buoy
-            dn_ref[6] = shear
-        if x == 1:
-            dn_ref[2] = slab[1]
-            dn_ref[4] = slab[2]
-        if x == size_x - 2:
-            up_ref[0] = slab[0]
-        if x == size_x - 1:
-            for c in range(3):
-                up_ref[1 + c] = slab[c]
+    last = size_x - 1
+    up = [slab(vt_ref.at[c], x) for c, x in ((0, last - 1), (0, last), (1, last), (2, last))]
+    down = [slab(vt_ref.at[c], x) for c, x in ((0, 0), (1, 0), (1, 1), (2, 0), (2, 1))]
+    two_ways(up, down + [slab(bt_ref, 0), slab(mt_ref, 0)], even_ref, odd_ref)
     send_columns(pack, col_ref)
 
 
-def load_kernel(layers, s_hbm, l_hbm, st_ref, lt_ref, s_ref, l_ref, sems):
-    size_x = l_ref.shape[0] // layers
-    sources = [s_hbm.at[c] for c in range(6)] + [l_hbm]
-    targets = [s_ref.at[c] for c in range(6)] + [l_ref]
-    copies = fetch(sources, targets, sems)
-    for c, copy in enumerate(copies):
-        copy.wait()
-        for x in range(size_x):
-            cut = pl.ds(x * layers, layers)
-            if c < 6:
-                st_ref[c, cut, :] = s_ref[c, pl.ds(x, layers, stride=size_x), :]
-            else:
-                lt_ref[cut, :] = l_ref[pl.ds(x, layers, stride=size_x), :]
-
-
-def material_kernel(
-    layers, b_ref, l_ref, m_ref, east_ref, north_ref, table_ref, out_ref, bs, ms, tb, tm, cols
-):
+def materials(layers, b_ref, l_ref, m_ref, above, cols, table_ref, mat_ref, buoy_ref, bs, ms, tb, tm):
     size_x = b_ref.shape[0] // layers
     _, east_ok, _, north_ok = place()
     nx, ny = lax.axis_size("gx"), lax.axis_size("gy")
     beyond = lax.rem(lax.axis_index("gx") + 1, nx) * ny + lax.rem(lax.axis_index("gy") + 1, ny)
-    receive_columns(north_ref, north_ref, (0,), north_ok, north_ok, cols)
     inner = slice(PAD, PAD + layers)
     for x in range(size_x):
         cut = slice(x * layers, (x + 1) * layers)
@@ -237,8 +234,8 @@
         part = cols[cut, :]
         tb[x, inner, :] = roll(part, -9)
         tm[x, inner, :] = roll(part, -10)
-    bs[size_x, inner, :] = east_ref[5]
-    ms[size_x, inner, :] = east_ref[6]
+    bs[size_x, inner, :] = above(5)
+    ms[size_x, inner, :] = above(6)
     line = jnp.broadcast_to(table_ref[pl.ds(beyond * CAP, 1), :], (layers, 128))
     own = lanes_of(line) - AT_CORNER == lax.broadcasted_iota(jnp.int32, line.shape, 0)
     corner = jnp.sum(jnp.where(own, line, 0.0), axis=1, keepdims=True)
@@ -271,76 +268,56 @@
         m_en = jnp.where(in_y & in_x, north(ms[x + 1, inner, :], tm[x + 1, inner, :]), m)
         m_ez = jnp.where(in_z & in_x, ms[x + 1, below, :], m)
         m_nz = jnp.where(in_z & in_y, north(ms[x, below, :], tm[x, below, :]), m)
-        out_ref[0, cut, :] = time_step * l_ref[cut, :]
-        out_ref[1, cut, :] = (2.0 * time_step) * m
-        out_ref[2, cut, :] = (0.25 * time_step) * (m + m_e + m_n + m_en)
-        out_ref[3, cut, :] = (0.25 * time_step) * (m + m_e + m_z + m_ez)
-        out_ref[4, cut, :] = (0.25 * time_step) * (m + m_n + m_z + m_nz)
-        out_ref[5, cut, :] = (0.5 * time_step) * (b + b_e)
-        out_ref[6, cut, :] = (0.5 * time_step) * (b + b_n)
-        out_ref[7, cut, :] = (0.5 * time_step) * (b + b_z)
+        mat_ref[0, cut, :] = time_step * l_ref[x]
+        mat_ref[1, cut, :] = (2.0 * time_step) * m
+        mat_ref[2, cut, :] = (0.25 * time_step) * (m + m_e + m_n + m_en)
+        mat_ref[3, cut, :] = (0.25 * time_step) * (m + m_e + m_z + m_ez)
+        mat_ref[4, cut, :] = (0.25 * time_step) * (m + m_n + m_z + m_nz)
+        buoy_ref[0, cut, :] = (0.5 * time_step) * (b + b_e)
+        buoy_ref[1, cut, :] = (0.5 * time_step) * (b + b_n)
+        buoy_ref[2, cut, :] = (0.5 * time_step) * (b + b_z)
         return carry
 
     lax.fori_loop(0, size_x, step, 0, unroll=4)
 
 
-def stress_kernel(
-    layers,
-    first,
-    v_ref,
-    s_ref,
-    mat_ref,
-    west_ref,
-    east_ref,
-    south_ref,
-    north_ref,
-    out_ref,
-    up_ref,
-    dn_ref,
-    col_ref,
-    *refs,
-):
-    if first:
-        kept_hbm, ext, cols, pack, sems = refs
-        keep = pltpu.make_async_copy(mat_ref, kept_hbm, sems.at[0])
-        keep.start()
-    else:
-        ext, cols, pack = refs
+def extend(ext, rows, at, ok, layers):
+    for row, c, x in rows:
+        ext[c, x, PAD : PAD + layers, :] = jnp.where(ok, at(row), 0.0)
+
+
+def stresses(layers, v_ref, old, ready, mat_ref, below, above, cols, out_ref, refs, ext, pack):
+    even_ref, odd_ref, col_ref = refs
     size_x = v_ref.shape[1] // layers
-    west_ok, east_ok, south_ok, north_ok = place()
-    receive_columns(south_ref, north_ref, (0, 3, 4, 6), south_ok, north_ok, cols)
+    west_ok, east_ok, _, _ = place()
     for c in range(3):
         fill(ext, c, v_ref, c, size_x, layers)
     inner = slice(PAD, PAD + layers)
-    for row, c, x in ((0, 0, 0), (1, 0, 1), (2, 1, 1), (3, 2, 1)):
-        ext[c, x, inner, :] = jnp.where(west_ok, west_ref[row], 0.0)
-    for row, c, x in ((0, 0, 0), (1, 1, 0), (2, 1, 1), (3, 2, 0), (4, 2, 1)):
-        ext[c, size_x + 2 + x, inner, :] = jnp.where(east_ok, east_ref[row], 0.0)
+    extend(ext, ((0, 0, 0), (1, 0, 1), (2, 1, 1), (3, 2, 1)), below, west_ok, layers)
+    over = size_x + 2
+    rows = ((0, 0, over), (1, 1, over), (2, 1, over + 1), (3, 2, over), (4, 2, over + 1))
+    extend(ext, rows, above, east_ok, layers)
 
     def step(x, carry):
         cut = pl.ds(pl.multiple_of(x * layers, layers), layers)
         ghost = cols[cut, :]
         vx, vy, vz = [ext[c, x + 2, inner, :] for c in range(3)]
         gx, gy, gz = roll(ghost, -1), roll(ghost, -5), roll(ghost, -7)
-
-        def old(c):
-            return s_ref[c, cut, :]
-
         dx = across(ext, 0, x, False, layers)
         dy = slopes(vy, gy, False)
         dz = down(ext, 2, x, False, layers)
         both = mat_ref[0, cut, :] * (dx + dy + dz)
         twice = mat_ref[1, cut, :]
-        xx = old(0) + (both + twice * dx)
-        yy = old(1) + (both + twice * dy)
-        zz = old(2) + (both + twice * dz)
-        xy = old(3) + mat_ref[2, cut, :] * (
+        xx = old(0, x, cut) + (both + twice * dx)
+        yy = old(1, x, cut) + (both + twice * dy)
+        zz = old(2, x, cut) + (both + twice * dz)
+        xy = old(3, x, cut) + mat_ref[2, cut, :] * (
             slopes(vx, gx, True) + across(ext, 1, x, True, layers)
         )
-        xz = old(4) + mat_ref[3, cut, :] * (
+        xz = old(4, x, cut) + mat_ref[3, cut, :] * (
             down(ext, 0, x, True, layers) + across(ext, 2, x, True, layers)
         )
-        yz = old(5) + mat_ref[4, cut, :] * (
+        yz = old(5, x, cut) + mat_ref[4, cut, :] * (
             down(ext, 1, x, True, layers) + slopes(vz, gz, True)
         )
         for c, value in enumerate((xx, yy, zz, xy, xz, yz)):
@@ -348,48 +325,142 @@
         pack[cut, :] = packed([(yy, 0, 3, 1), (xy, 3, 3, 5), (yz, 6, 3, 8)])
         return carry
 
-    lax.fori_loop(0, size_x, step, 0, unroll=4)
+    for strip in range(size_x // STRIP):
+        ready(strip)
+        lax.fori_loop(strip * STRIP, (strip + 1) * STRIP, step, 0, unroll=4)
     send_columns(pack, col_ref)
 
     def slab(c, x):
         return out_ref[c, x * layers : (x + 1) * layers, :]
 
-    for row, (c, x) in enumerate(((0, 1), (3, 2), (3, 1), (4, 2), (4, 1))):
-        up_ref[row] = slab(c, size_x - x)
-    for row, (c, x) in enumerate(((0, 0), (0, 1), (3, 0), (4, 0))):
-        dn_ref[row] = slab(c, x)
-    if first:
-        keep.wait()
-
-
-def velocity_kernel(
+    up = [slab(c, size_x - x) for c, x in ((0, 1), (3, 2), (3, 1), (4, 2), (4, 1))]
+    two_ways(up, [slab(c, x) for c, x in ((0, 0), (0, 1), (3, 0), (4, 0))], even_ref, odd_ref)
+
+
+def begin_kernel(
     layers,
-    last,
     v_ref,
+    b_ref,
+    m_ref,
+    s_hbm,
+    l_hbm,
+    stiff_hbm,
+    x_even,
+    x_odd,
+    y_even,
+    y_odd,
+    table_ref,
+    out_ref,
+    even_ref,
+    odd_ref,
+    col_ref,
+    buoy_ref,
+    stiff_ref,
+    mat_hbm,
+    buoy_hbm,
+    s_ref,
+    l_ref,
+    mat_ref,
+    bs,
+    ms,
+    tb,
+    tm,
+    ext,
+    cols,
+    pack,
+    sems,
+):
+    size_x = v_ref.shape[1] // layers
+    own = range(size_x)
+    sources = [l_hbm.at[:, x] for x in own] + [s_hbm.at[:, :, x] for x in own]
+    targets = [l_ref.at[x] for x in own] + [s_ref.at[:, x] for x in own]
+    half = stiff_ref.shape[0]
+    copies = fetch(
+        sources + [stiff_hbm.at[pl.ds(0, half)]], targets + [stiff_ref.at[...]], sems
+    )
+    _, _, south_ok, north_ok = place()
+    below, above = below_above("gx", x_even, x_odd)
+    receive_columns(y_even, y_odd, (0, 3, 4, 6), south_ok, north_ok, cols)
+    for x in own:
+        copies[x].wait()
+    materials(layers, b_ref, l_ref, m_ref, above, cols, table_ref, mat_ref, buoy_ref, bs, ms, tb, tm)
+    leaving = fetch([mat_ref, buoy_ref], [mat_hbm, buoy_hbm], sems.at[pl.ds(2 * size_x + 1, 2)])
+
+    def ready(strip):
+        for x in range(strip * STRIP, (strip + 1) * STRIP):
+            copies[size_x + x].wait()
+
+    def old(c, x, cut):
+        return s_ref[c, x]
+
+    refs = (even_ref, odd_ref, col_ref)
+    stresses(layers, v_ref, old, ready, mat_ref, below, above, cols, out_ref, refs, ext, pack)
+    for copy in leaving + copies[2 * size_x :]:
+        copy.wait()
+
+
+def stress_kernel(
+    layers,
+    v_ref,
+    s_hbm,
+    mat_hbm,
+    x_even,
+    x_odd,
+    y_even,
+    y_odd,
+    out_ref,
+    even_ref,
+    odd_ref,
+    col_ref,
     s_ref,
     mat_ref,
-    west_ref,
-    east_ref,
-    south_ref,
-    north_ref,
-    push_ref,
-    *refs,
+    ext,
+    cols,
+    pack,
+    sems,
+):
+    strips = v_ref.shape[1] // layers // STRIP
+    cuts = [pl.ds(strip * STRIP * layers, STRIP * layers) for strip in range(strips)]
+    sources, targets = [], []
+    for cut in cuts:
+        sources += [s_hbm.at[:, cut], mat_hbm.at[:, cut]]
+        targets += [s_ref.at[:, cut], mat_ref.at[:, cut]]
+    copies = fetch(sources, targets, sems)
+    _, _, south_ok, north_ok = place()
+    below, above = below_above("gx", x_even, x_odd)
+    receive_columns(y_even, y_odd, (0, 3, 4, 6), south_ok, north_ok, cols)
+
+    def ready(strip):
+        copies[2 * strip].wait()
+        copies[2 * strip + 1].wait()
+
+    def old(c, x, cut):
+        return s_ref[c, cut, :]
+
+    refs = (even_ref, odd_ref, col_ref)
+    stresses(layers, v_ref, old, ready, mat_ref, below, above, cols, out_ref, refs, ext, pack)
+
+
+def velocity_kernel(
+    layers, last, v_ref, s_ref, buoy_ref, x_even, x_odd, y_even, y_odd, push_ref, *refs
 ):
     if last:
         out_hbm, out_ref, ext, cols, sems = refs
     else:
-        out_ref, up_ref, dn_ref, col_ref, ext, cols, pack = refs
+        out_ref, even_ref, odd_ref, col_ref, kept_hbm, ext, cols, pack, sems = refs
+        keep = pltpu.make_async_copy(s_ref, kept_hbm, sems.at[0])
+        keep.start()
     size_x = v_ref.shape[1] // layers
-    parts = size_x // STRIP
     west_ok, east_ok, south_ok, north_ok = place()
-    receive_columns(south_ref, north_ref, (0, 3, 4, 6, 7), south_ok, north_ok, cols)
+    below, above = below_above("gx", x_even, x_odd)
+    receive_columns(y_even, y_odd, (0, 3, 4, 6, 7), south_ok, north_ok, cols)
     for c, src in enumerate((0, 3, 4, 5, 2)):
         fill(ext, c, s_ref, src, size_x, layers)
     inner = slice(PAD, PAD + layers)
-    for row, c, x in ((0, 0, 1), (1, 1, 0), (2, 1, 1), (3, 2, 0), (4, 2, 1)):
-        ext[c, x, inner, :] = jnp.where(west_ok, west_ref[row], 0.0)
-    for row, c, x in ((0, 0, 0), (1, 0, 1), (2, 1, 0), (3, 2, 0)):
-        ext[c, size_x + 2 + x, inner, :] = jnp.where(east_ok, east_ref[row], 0.0)
+    rows = ((0, 0, 1), (1, 1, 0), (2, 1, 1), (3, 2, 0), (4, 2, 1))
+    extend(ext, rows, below, west_ok, layers)
+    over = size_x + 2
+    extend(ext, ((0, 0, over), (1, 0, over + 1), (2, 1, over), (3, 2, over)), above, east_ok, layers)
 
     def step(x, carry):
         cut = pl.ds(pl.multiple_of(x * layers, layers), layers)
@@ -403,36 +474,36 @@
         fresh = []
         for c, accel in enumerate((ax, ay, az)):
             pushed = jnp.where(layer == 0, push_ref[c, pl.ds(x, 1), :], 0.0)
-            fresh.append(v_ref[c, cut, :] + mat_ref[5 + c, cut, :] * accel + pushed)
+            fresh.append(v_ref[c, cut, :] + buoy_ref[c, cut, :] * accel + pushed)
         if last:
             for c in range(3):
-                out_ref[x // STRIP, c, :, lax.rem(x, STRIP), :] = fresh[c]
+                out_ref[x // TILE, c, :, lax.rem(x, TILE), :] = fresh[c]
         else:
             for c in range(3):
                 out_ref[c, cut, :] = fresh[c]
             pack[cut, :] = packed([(fresh[0], 0, 3, 1), (fresh[1], 3, 3, 5), (fresh[2], 6, 3, 7)])
         return carry
 
-    leaving = []
-    for part in range(parts):
-        lax.fori_loop(part * STRIP, (part + 1) * STRIP, step, 0, unroll=4)
-        if last:
+    if last:
+        leaving = []
+        for tile in range(size_x // TILE):
+            lax.fori_loop(tile * TILE, (tile + 1) * TILE, step, 0, unroll=4)
             leaving += fetch(
-                [out_ref.at[part]], [out_hbm.at[:, :, part]], sems.at[pl.ds(part, 1)]
+                [out_ref.at[tile]], [out_hbm.at[:, :, tile]], sems.at[pl.ds(tile, 1)]
             )
-    for copy in leaving:
-        copy.wait()
-    if last:
+        for copy in leaving:
+            copy.wait()
         return
+    lax.fori_loop(0, size_x, step, 0, unroll=4)
     send_columns(pack, col_ref)
 
     def slab(c, x):
         return out_ref[c, x * layers : (x + 1) * layers, :]
 
-    for row, (c, x) in enumerate(((0, 2), (0, 1), (1, 1), (2, 1))):
-        up_ref[row] = slab(c, size_x - x)
-    for row, (c, x) in enumerate(((0, 0), (1, 0), (1, 1), (2, 0), (2, 1))):
-        dn_ref[row] = slab(c, x)
+    up = [slab(c, size_x - x) for c, x in ((0, 2), (0, 1), (1, 1), (2, 1))]
+    down_rows = [slab(c, x) for c, x in ((0, 0), (1, 0), (1, 1), (2, 0), (2, 1))]
+    two_ways(up, down_rows, even_ref, odd_ref)
+    keep.wait()
 
 
 def third(value, e):
@@ -502,15 +573,25 @@
 
 def first_kernel(layers, span, *refs):
     far, outs, scratch = refs[:9], refs[9:16], refs[16:]
-    near, pack, sems = scratch[:9], scratch[9], scratch[10]
-    copies = fetch(far, near, sems)
-    for copy in copies[3:]:
+    small, pack, sems = scratch[:6], scratch[6], scratch[7]
+    vt, bt, mt = outs[:3]
+    size_x = vt.shape[1] // layers
+    cuts = [pl.ds(x * layers, layers) for x in range(size_x)]
+    sources, targets = list(far[3:]), list(small)
+    for x, cut in enumerate(cuts):
+        sources += [far[0].at[:, :, x], far[1].at[:, x], far[2].at[:, x]]
+        targets += [vt.at[:, cut], bt.at[cut], mt.at[cut]]
+    copies = fetch(sources, targets, sems)
+    for copy in copies[:6]:
         copy.wait()
-    table(span, *near[3:], outs[6])
-    for copy in copies[:3]:
-        copy.wait()
-    edges(layers, *near[:3], *outs[:6], pack)
-    first = outs[2][pl.ds(0, layers), 0:1]
+    table(span, *small, outs[6])
+
+    def arrived(x):
+        for copy in copies[6 + 3 * x : 9 + 3 * x]:
+            copy.wait()
+
+    edges(layers, arrived, *outs[:6], pack)
+    first = mt[pl.ds(0, layers), 0:1]
     spot = lax.broadcasted_iota(jnp.int32, (layers, 128), 1) - AT_CORNER
     own = spot == lax.broadcasted_iota(jnp.int32, (layers, 128), 0)
     outs[6][...] += jnp.sum(jnp.where(own, first, 0.0), axis=0, keepdims=True)
@@ -525,7 +606,17 @@
     return row
 
 
-def products(stiff_ref, drift_ref, out_ref, begin, end):
+def fetch_strips(stiff_hbm, begin, stiff_ref, sems):
+    size = stiff_ref.shape[0] // sems.shape[0]
+    strips = range(sems.shape[0])
+    return fetch(
+        [stiff_hbm.at[pl.ds(begin + c * size, size)] for c in strips],
+        [stiff_ref.at[pl.ds(c * size, size)] for c in strips],
+        sems,
+    )
+
+
+def products(stiff_ref, at, drift_ref, out_ref, begin, end):
     group = 16
     for g in range(begin // group * group, end, group):
         rounded = drift_ref[g : g + group, :].astype(jnp.bfloat16)
@@ -534,7 +625,7 @@
         total = out_ref[g : g + group, :]
         for b in range(low, high):
             part = lax.dot_general(
-                rounded, stiff_ref[b], (((1,), (1,)), ((), ())), preferred_element_type=f32
+                rounded, stiff_ref[b - at], (((1,), (1,)), ((), ())), preferred_element_type=f32
             )
             total = jnp.where(row == b - g, part, total)
         out_ref[g : g + group, :] = total
@@ -542,6 +633,7 @@
 
 def pull_kernel(
     stiff_ref,
+    stiff_hbm,
     raw_ref,
     rate_ref,
     coupling_ref,
@@ -551,12 +643,19 @@
     drift_out,
     next_ref,
     pull,
+    rest_ref,
+    sems,
 ):
-    number = drift_out.shape[0]
+    number, half = drift_out.shape[0], stiff_ref.shape[0]
+    copies = fetch_strips(stiff_hbm, half, rest_ref, sems)
     mask = counted(counts_ref, drift_out.shape)
     drift_out[...] = jnp.where(mask, raw_ref[...], 0.0)
     pull[...] = jnp.zeros(pull.shape, f32)
-    products(stiff_ref, drift_out, pull, 0, number)
+    products(stiff_ref, 0, drift_out, pull, 0, half)
+    size = (number - half) // len(copies)
+    for c, copy in enumerate(copies):
+        copy.wait()
+        products(rest_ref, half, drift_out, pull, half + c * size, half + (c + 1) * size)
     rate = jnp.where(mask, rate_ref[...], 0.0)
     coupling = jnp.where(mask, coupling_ref[...], 0.0)
     base = rate - time_step * pull[...] - time_step * coupling * rate
@@ -655,10 +754,7 @@
     stiff_ref,
     sems,
 ):
-    chunks = sems.shape[0]
-    size = half.shape[0] // chunks
-    strips = [pl.ds(c * size, size) for c in range(chunks)]
-    copies = fetch([stiff_hbm.at[c] for c in strips], [stiff_ref.at[c] for c in strips], sems)
+    copies = fetch_strips(stiff_hbm, 0, stiff_ref, sems)
     table, sent, back = table_ref[...], sent_ref[...], back_ref[...]
     reaction = []
     for c in range(3):
@@ -676,9 +772,10 @@
     drift = jnp.where(mask, drift_ref[...] + time_step * rate, 0.0)
     half[...] = drift
     pull[...] = jnp.zeros(pull.shape, f32)
-    for c in range(chunks):
-        copies[c].wait()
-        products(stiff_ref, half, pull, c * size, (c + 1) * size)
+    size = half.shape[0] // len(copies)
+    for c, copy in enumerate(copies):
+        copy.wait()
+        products(stiff_ref, 0, half, pull, c * size, (c + 1) * size)
     relative = rate - spread_thirds(moved, SECOND, coupling)
     rate = rate - time_step * pull[...] - time_step * coupling * relative
     rate = jnp.where(mask, rate, 0.0)
@@ -713,9 +810,6 @@
     number, width = storey_drift.shape
     slots = lax.axis_size("gx") * lax.axis_size("gy") * CAP
     span = size_y - FOOT + 1
-    v = soil_velocity.reshape(3, cells, size_y)
-    s = soil_stress.reshape(6, cells, size_y)
-    buoy, lame, shear = (a.reshape(cells, size_y) for a in (buoyancy, lame_first, shear_modulus))
     counts, owner, corner = (a.reshape(1, number) for a in (dof_counts, owner_tile, corner_cell))
 
     def bind(kernel, *fixed):
@@ -731,7 +825,7 @@
     tall = layers + 2 * PAD
     plane = near_by(number, width)
     dma = pltpu.SemaphoreType.DMA
-    far = (v, buoy, shear, drift_rate, coupling, contact, counts, owner, corner)
+    far = (soil_velocity, buoyancy, shear_modulus, drift_rate, coupling, contact, counts, owner, corner)
     outs = call(
         bind(first_kernel, layers, span),
         "first",
@@ -739,97 +833,93 @@
             near_by(3, cells, size_y),
             near_by(cells, size_y),
             near_by(cells, size_y),
-            near_by(4, layers, size_y),
+            near_by(7, layers, size_y),
             near_by(7, layers, size_y),
             near_by(16, cells),
             near_by(slots, 128),
         ),
         [Far(a) for a in far],
-        [pltpu.VMEM(a.shape, a.dtype) for a in far] + [field, dma((len(far),))],
-    )
-    vt, bt, mt, up, dn, col, rows = outs
-
-    def exchange(up, dn, col):
-        west = ring(up, "gx", 1)
-        east = ring(dn, "gx", -1)
-        south = ring(col, "gy", 1)
-        north = ring(col, "gy", -1)
-        return west, east, south, north
-
-    halo = exchange(up, dn, col)
+        [pltpu.VMEM(a.shape, a.dtype) for a in far[3:]] + [field, dma((6 + 3 * size_x,))],
+    )
+    vt, bt, mt, one, two, col, rows = outs
+
+    def exchange(one, two, col):
+        return swap(one, "gx", 0), swap(two, "gx", 1), swap(col, "gy", 0), swap(col, "gy", 1)
+
+    halo = exchange(one, two, col)
     rows = trade(rows)
-    parts = size_x // STRIP
-    st, lt = call(
-        bind(load_kernel, layers),
-        "load",
-        (near_by(6, cells, size_y), near_by(cells, size_y)),
-        (Far(s), Far(lame)),
-        [vm(6, cells, size_y), field, dma((7,))],
-    )
-    (material,) = call(
-        bind(material_kernel, layers),
-        "material",
-        (near_by(8, cells, size_y),),
-        (bt, lt, mt, halo[1], halo[3], rows),
-        [vm(size_x + 1, tall, size_y) for _ in range(4)] + [field],
-    )
-
-    def stress_step(first, v, s, material, halo):
-        outs = [
+    half = number // 2
+    payload = (near_by(5, layers, size_y), near_by(5, layers, size_y), near_by(16, cells))
+    ext = vm(3, size_x + 4, tall, size_y)
+    stack = vm(size_x + 1, tall, size_y)
+    st, one, two, col, buoys, stiff, mat_kept, buoy_kept = call(
+        bind(begin_kernel, layers),
+        "begin",
+        (
             near_by(6, cells, size_y),
-            near_by(5, layers, size_y),
-            near_by(4, layers, size_y),
-            near_by(16, cells),
-        ]
-        scratch = [vm(3, size_x + 4, tall, size_y), field, field]
-        if first:
-            outs += [pltpu.HBM((8, cells, size_y), f32)]
-            scratch += [dma((1,))]
-        return call(
-            bind(stress_kernel, layers, first),
-            "stress",
-            tuple(outs),
-            (v, s, material, *halo),
-            scratch,
-            far_outs=(4,),
-        )
-
-    def velocity_step(last, v, s, material, halo, push):
+            *payload,
+            near_by(3, cells, size_y),
+            near_by(half, width, width, dtype=stiffness.dtype),
+            pltpu.HBM((5, cells, size_y), f32),
+            pltpu.HBM((3, cells, size_y), f32),
+        ),
+        (vt, bt, mt, Far(soil_stress), Far(lame_first), Far(stiffness), *halo, rows),
+        [
+            vm(6, size_x, layers, size_y),
+            vm(size_x, layers, size_y),
+            vm(5, cells, size_y),
+            stack,
+            stack,
+            stack,
+            stack,
+            ext,
+            field,
+            field,
+            dma((2 * size_x + 3,)),
+        ],
+        far_outs=(6, 7),
+    )
+
+    def velocity_step(last, v, s, buoys, halo, push):
         scratch = [vm(5, size_x + 4, tall, size_y), field]
+        tiles = size_x // TILE
         if last:
-            outs = [pltpu.HBM((3, layers, parts, STRIP, size_y), f32)]
-            scratch = [vm(parts, 3, layers, STRIP, size_y)] + scratch + [dma((parts,))]
+            outs = [pltpu.HBM((3, layers, tiles, TILE, size_y), f32)]
+            scratch = [vm(tiles, 3, layers, TILE, size_y)] + scratch + [dma((tiles,))]
         else:
-            outs = [near_by(3, cells, size_y)]
-            outs += [near_by(4, layers, size_y), near_by(5, layers, size_y), near_by(16, cells)]
-            scratch += [field]
+            outs = [near_by(3, cells, size_y), *payload, pltpu.HBM((6, cells, size_y), f32)]
+            scratch += [field, dma((1,))]
         return call(
             bind(velocity_kernel, layers, last),
             "velocity",
             tuple(outs),
-            (v, s, material, *halo, push),
+            (v, s, buoys, *halo, push),
             scratch,
-            far_outs=(0,) if last else (),
+            far_outs=(0,) if last else (4,),
         )
 
-    st, up, dn, col, kept = stress_step(True, vt, st, material, halo)
-    halo = exchange(up, dn, col)
+    halo = exchange(one, two, col)
     maps, moved, push = call(
         bind(surface_kernel, layers),
         "surface",
         (near_by(size_x, slots, size_y), near_by(slots, 128), near_by(3, size_x, size_y)),
         (rows, vt),
     )
+    chunks = 4 if number % 8 == 0 else 1
     base, drift, following = call(
         pull_kernel,
         "pull",
         (plane, plane, near_by(slots, 128)),
-        (stiffness, storey_drift, drift_rate, coupling, counts, owner),
-        [vm(number, width)],
+        (stiff, Far(stiffness), storey_drift, drift_rate, coupling, counts, owner),
+        [
+            vm(number, width),
+            pltpu.VMEM((number - half, width, width), stiffness.dtype),
+            dma((chunks,)),
+        ],
     )
     push, following = lax.optimization_barrier((push, following))
-    vt, up, dn, col = velocity_step(False, vt, st, material, halo, push)
-    halo = exchange(up, dn, col)
+    vt, one, two, col, kept = velocity_step(False, vt, st, buoys, halo, push)
+    halo = exchange(one, two, col)
     (sent,) = call(
         bind(motion_again_kernel, layers),
         "motion_again",
@@ -838,10 +928,23 @@
     )
     vt, sent = lax.optimization_barrier((vt, sent))
     back = trade(sent)
-    st, up, dn, col = stress_step(False, vt, st, kept, halo)
-    halo = exchange(up, dn, col)
+    strips = size_x // STRIP
+    st, one, two, col = call(
+        bind(stress_kernel, layers),
+        "stress",
+        (near_by(6, cells, size_y), *payload),
+        (vt, Far(kept), Far(mat_kept), *halo),
+        [
+            vm(6, cells, size_y),
+            vm(5, cells, size_y),
+            ext,
+            field,
+            field,
+            dma((2 * strips,)),
+        ],
+    )
+    halo = exchange(one, two, col)
     sent, st = lax.optimization_barrier((sent, st))
-    chunks = 8 if number % 8 == 0 else 1
     push, drift, rate = call(
         finish_kernel,
         "finish",
@@ -851,10 +954,10 @@
             vm(number, width),
             vm(number, width),
             pltpu.VMEM(stiffness.shape, stiffness.dtype),
-            dma((chunks,)),
+            dma((2 * chunks,)),
         ],
     )
-    (v,) = velocity_step(True, vt, st, kept, halo, push)
+    (v,) = velocity_step(True, vt, st, buoy_kept, halo, push)
     return v.reshape(soil_velocity.shape), drift, rate
 
 

time: 73.2 us -> 63.2 us (0.86)
  local copies, waits for them, and re-layouts: 4.62 us -> 0.02 us
  starting transfers between devices: 36.6 us -> 32.4 us
  waiting for transfers between devices: 5.54 us -> 2.34 us
  Pallas kernels: 25.3 us -> 27.3 us
    unnamed x22 -> x12, local copies, waits for them, and re-layouts: 4.62 us -> 0.02 us
    all_to_all x2, waiting for transfers between devices: 3.32 us -> 0.66 us  [trade(): lax.all_to_all(blocks, ('gx', 'gy'), split_axis=0, concat_axis=0, tiled=T...]
    ppermute x16, starting transfers between devices: 24.2 us -> 22.1 us  [swap(): return lax.ppermute(block, axis, pairs + [(b, a) for a, b in pairs])]
    all_to_all x2, starting transfers between devices: 12.3 us -> 10.3 us  [trade(): lax.all_to_all(blocks, ('gx', 'gy'), split_axis=0, concat_axis=0, tiled=T...]
    pallas_call x11 -> x9, Pallas kernels: 25.3 us -> 27.3 us  [call(): pl.pallas_call(kernel, name=name, out_shape=outs, in_specs=specs, out_spe...]
  transfers between devices with their start and end apart: 18 -> 18, of which waited for: 4 -> 2; matrix products, arithmetic and copies ran while one was open for 0% -> 0% of each run, Pallas kernels for 17% -> 22%
where the time goes in v2:
time: 63.2 us; the launch traced here: 62.9 us
  starting transfers between devices  32.4 us (51%)
  Pallas kernels  27.3 us (43%)
  waiting for transfers between devices  2.34 us (4%)
  between operations  0.86 us (1%)
    pallas_call x9, Pallas kernels, call(): pl.pallas_call(kernel, name=name, out_shape=outs, in_specs=specs, out_spe...  27.3 us
    ppermute x16, starting transfers between devices, swap(): return lax.ppermute(block, axis, pairs + [(b, a) for a, b in pairs])  22.1 us
    all_to_all x2, starting transfers between devices, trade(): lax.all_to_all(blocks, ('gx', 'gy'), split_axis=0, concat_axis=0, tiled=T...  10.3 us
    ppermute x16, waiting for transfers between devices, swap(): return lax.ppermute(block, axis, pairs + [(b, a) for a, b in pairs])  1.68 us
  transfers between devices with their start and end apart: 18, of which 2 were waited for; matrix products, arithmetic and copies ran while one was open for 0% of the time, Pallas kernels for 22%

profile of v2, /device:TPU:0, one launch (start us, length us, event | category | flops | bytes accessed | tf_op | source)
XLA Modules:
  0.0 62.9 jit_solution(7652292513358529103)
XLA Ops:
  0.6 3.9 %first.1 = (f32[3,512,128]{2,1,0:T(8,128)S(1)}, f32[512,128]{1,0:T(8,128)S(1)}, f32[512,128]{1,0:T(8,128)S(1)}, f32[7,32,128]{2,1,0:T(8,128)S(1)}, f32[7,32,128]...) custom-call(f32[3,32,16,128]{3,2,1,0:T(8,128)} %refs_0_.1, f32[32,16,128]{2,1,0:T(8,128)} %refs_1_.1, ...), custom_call_target="tpu_custom_call" | custom-call | flops 30000001024 | bytes 30000000 | tf_op jit(solution)/shard_map/first/pallas_call | solution.py:49
  4.5 7.3 %all-to-all-start = ((f32[32,2,128]{2,1,0:T(2,128)}), f32[32,2,128]{2,1,0:T(2,128)S(1)}, u32[]{:S(2)}, u32[]{:S(2)}) async-start(f32[32,2,128]{2,1,0:T(2,128)} %bitcast.3), calls=%async_computation | async-start | bytes 65536 | tf_op jit(solution)/shard_map/all_to_all | solution.py:789
  11.8 1.8 %collective-permute-start.2 = (f32[16,512]{1,0:T(8,128)S(1)}, f32[16,512]{1,0:T(8,128)S(1)}, u32[]{:S(2)}, u32[]{:S(2)}) collective-permute-start(f32[16,512]{1,0:T(8,128)S(1)} %get-tuple-element.47), channel_id=1, source_target_pairs={{0,1},{2,3},{1,0},{3,2},{4,5},{6,7},{5,4},{7,6},{8,9},{10,11},{9,8... | collective-permute-start | bytes 98312 | tf_op jit(solution)/shard_map/ppermute | solution.py:85
  13.6 2.4 %collective-permute-start.3 = (f32[16,512]{1,0:T(8,128)S(1)}, f32[16,512]{1,0:T(8,128)S(1)}, u32[]{:S(2)}, u32[]{:S(2)}) collective-permute-start(f32[16,512]{1,0:T(8,128)S(1)} %get-tuple-element.47), channel_id=1, source_target_pairs={{1,2},{3,0},{2,1},{0,3},{5,6},{7,4},{6,5},{4,7},{9,10},{11,8},{10,... | collective-permute-start | bytes 98312 | tf_op jit(solution)/shard_map/ppermute | solution.py:85
  16.0 0.0 collective-permute-start
  16.0 2.5 %collective-permute-start.1 = (f32[7,32,128]{2,1,0:T(8,128)S(1)}, f32[7,32,128]{2,1,0:T(8,128)S(1)}, u32[]{:S(2)}, u32[]{:S(2)}) collective-permute-start(f32[7,32,128]{2,1,0:T(8,128)S(1)} %get-tuple-element.46), channel_id=1, source_target_pairs={{4,8},{12,16},{20,24},{28,0},{8,4},{16,12},{24,20},{0,28},{5,9},{1... | collective-permute-start | bytes 344072 | tf_op jit(solution)/shard_map/ppermute | solution.py:85
  18.5 0.7 %all-to-all-done = f32[32,2,128]{2,1,0:T(2,128)S(1)} async-done(((f32[32,2,128]{2,1,0:T(2,128)}), f32[32,2,128]{2,1,0:T(2,128)S(1)}, u32[]{:S(2)}, u32[]{:S(2)}) %all-to-all-start) | async-done | bytes 32800 | tf_op jit(solution)/shard_map/all_to_all | solution.py:789
  19.2 0.8 %surface.1 = (f32[16,64,128]{2,1,0:T(8,128)S(1)}, f32[64,128]{1,0:T(8,128)S(1)}, f32[3,16,128]{2,1,0:T(8,128)S(1)}) custom-call(f32[64,128]{1,0:T(8,128)S(1)} %bitcast.8, f32[3,512,128]{2,1,0:T(8,128)S(1)} %get-tuple-element.42.refs_0_.refs_1_), custom_call_target="tpu_custom_call" | custom-call | flops 10000000000 | bytes 10000000 | tf_op jit(solution)/shard_map/surface/pallas_call | solution.py:49
  20.0 0.0 collective-permute-done.2.refs_8_
  20.0 0.0 collective-permute-done.3.refs_9_
  20.1 0.0 collective-permute-done.refs_6_
  20.1 1.6 %collective-permute-done.1.refs_7_ = f32[7,32,128]{2,1,0:T(8,128)S(1)} collective-permute-done((f32[7,32,128]{2,1,0:T(8,128)S(1)}, f32[7,32,128]{2,1,0:T(8,128)S(1)}, u32[]{:S(2)}, u32[]{:S(2)}) %collective-permute-start.1) | collective-permute-done | bytes 114720 | tf_op jit(solution)/shard_map/ppermute | solution.py:85
  21.7 0.0 copy-start
  21.7 0.0 copy-start.1
  21.7 0.0 copy-start.2
  21.7 0.0 copy-start.3
  21.7 0.0 copy-start.4
  21.7 4.3 %begin.1 = (f32[6,512,128]{2,1,0:T(8,128)S(1)}, f32[5,32,128]{2,1,0:T(8,128)S(1)}, f32[5,32,128]{2,1,0:T(8,128)S(1)}, f32[16,512]{1,0:T(8,128)S(1)}, f32[3,512,1...) custom-call(f32[3,512,128]{2,1,0:T(8,128)S(1)} %get-tuple-element.42.refs_, ...), custom_call_target="tpu_custom_call" | custom-call | flops 40000000000 | bytes 40000000 | tf_op jit(solution)/shard_map/begin/pallas_call | solution.py:49
  26.1 0.7 %collective-permute-start.6 = (f32[16,512]{1,0:T(8,128)S(1)}, f32[16,512]{1,0:T(8,128)S(1)}, u32[]{:S(2)}, u32[]{:S(2)}) collective-permute-start(f32[16,512]{1,0:T(8,128)S(1)} %get-tuple-element.53), channel_id=1, source_target_pairs={{0,1},{2,3},{1,0},{3,2},{4,5},{6,7},{5,4},{7,6},{8,9},{10,11},{9,8... | collective-permute-start | bytes 98312 | tf_op jit(solution)/shard_map/ppermute | solution.py:85
  26.7 1.0 %collective-permute-start.7 = (f32[16,512]{1,0:T(8,128)S(1)}, f32[16,512]{1,0:T(8,128)S(1)}, u32[]{:S(2)}, u32[]{:S(2)}) collective-permute-start(f32[16,512]{1,0:T(8,128)S(1)} %get-tuple-element.53), channel_id=1, source_target_pairs={{1,2},{3,0},{2,1},{0,3},{5,6},{7,4},{6,5},{4,7},{9,10},{11,8},{10,... | collective-permute-start | bytes 98312 | tf_op jit(solution)/shard_map/ppermute | solution.py:85
  27.7 0.0 collective-permute-start.4
  27.7 1.6 %collective-permute-start.5 = (f32[5,32,128]{2,1,0:T(8,128)S(1)}, f32[5,32,128]{2,1,0:T(8,128)S(1)}, u32[]{:S(2)}, u32[]{:S(2)}) collective-permute-start(f32[5,32,128]{2,1,0:T(8,128)S(1)} %get-tuple-element.52), channel_id=1, source_target_pairs={{4,8},{12,16},{20,24},{28,0},{8,4},{16,12},{24,20},{0,28},{5,9},{1... | collective-permute-start | bytes 245768 | tf_op jit(solution)/shard_map/ppermute | solution.py:85
  29.3 0.0 copy-done
  29.3 0.0 copy-done.1
  29.3 0.0 copy-done.2
  29.3 0.0 copy-done.3
  29.4 0.0 copy-done.4
  29.4 3.1 %pull.1 = (f32[64,256]{1,0:T(8,128)S(1)}, f32[64,256]{1,0:T(8,128)S(1)}, f32[64,128]{1,0:T(8,128)S(1)}) custom-call(bf16[32,256,256]{2,1,0:T(8,128)(2,1)S(1)} %get-tuple-element.55.stiff_ref, bf16[64,256,256]{2,1,0:T(8,128)(2,1)} %stiff_hbm.3, f32[64,256]{1,0:T(8,128)S(1)} %copy-done.1, f32[64,256]{1,0:T(8,128)S(1)} %copy-done, f32[64,256]{1,0:T(8,128)S(1)} %copy-done.2, ...), custom_call_target="tpu_custom_call" | custom-call | flops 30000001024 | bytes 30000000 | tf_op jit(solution)/shard_map/pull/pallas_call | solution.py:49
  32.4 0.0 collective-permute-done.6.refs_5_
  32.5 0.0 collective-permute-done.7.refs_6_
  32.5 0.0 collective-permute-done.4.refs_3_
  32.5 0.0 collective-permute-done.5.refs_4_
  32.5 2.4 %velocity.2 = (f32[3,512,128]{2,1,0:T(8,128)S(1)}, f32[5,32,128]{2,1,0:T(8,128)S(1)}, f32[5,32,128]{2,1,0:T(8,128)S(1)}, f32[16,512]{1,0:T(8,128)S(1)}, f32[6,512,128]{2,1,0:T(8,128)}) custom-call(f32[3,512,128]{2,1,0:T(8,128)S(1)} %get-tuple-element.42.refs_0_.refs_1_, f32[6,512,128]{2,1,0:T(8,128)S(1)} %get-tuple-element.49.refs_1_, ...), custom_call_target="tpu_custom_call" | custom-call | flops 24999999488 | bytes 25000000 | tf_op jit(solution)/shard_map/velocity/pallas_call | solution.py:49
  34.9 1.1 %collective-permute-start.10 = (f32[16,512]{1,0:T(8,128)S(1)}, f32[16,512]{1,0:T(8,128)S(1)}, u32[]{:S(2)}, u32[]{:S(2)}) collective-permute-start(f32[16,512]{1,0:T(8,128)S(1)} %get-tuple-element.68), channel_id=1, source_target_pairs={{0,1},{2,3},{1,0},{3,2},{4,5},{6,7},{5,4},{7,6},{8,9},{10,11},{9,8... | collective-permute-start | bytes 98312 | tf_op jit(solution)/shard_map/ppermute | solution.py:85
  35.9 2.4 %collective-permute-start.11 = (f32[16,512]{1,0:T(8,128)S(1)}, f32[16,512]{1,0:T(8,128)S(1)}, u32[]{:S(2)}, u32[]{:S(2)}) collective-permute-start(f32[16,512]{1,0:T(8,128)S(1)} %get-tuple-element.68), channel_id=1, source_target_pairs={{1,2},{3,0},{2,1},{0,3},{5,6},{7,4},{6,5},{4,7},{9,10},{11,8},{10,... | collective-permute-start | bytes 98312 | tf_op jit(solution)/shard_map/ppermute | solution.py:85
  38.3 0.0 collective-permute-start.8
  38.3 1.9 %collective-permute-start.9 = (f32[5,32,128]{2,1,0:T(8,128)S(1)}, f32[5,32,128]{2,1,0:T(8,128)S(1)}, u32[]{:S(2)}, u32[]{:S(2)}) collective-permute-start(f32[5,32,128]{2,1,0:T(8,128)S(1)} %get-tuple-element.67), channel_id=1, source_target_pairs={{4,8},{12,16},{20,24},{28,0},{8,4},{16,12},{24,20},{0,28},{5,9},{1... | collective-permute-start | bytes 245768 | tf_op jit(solution)/shard_map/ppermute | solution.py:85
  40.3 0.8 %motion_again.1.sent_ref = f32[64,128]{1,0:T(8,128)} custom-call(f32[3,512,128]{2,1,0:T(8,128)S(1)} %get-tuple-element.62.refs_0_, f32[16,64,128]{2,1,0:T(8,128)S(1)} %get-tuple-element.59.refs_1_, f32[64,128]{1,0:T(8,128)S(1)} %get-tuple-element.60.refs_2_, f32[64,128]{1,0:T(8,128)S(1)} %get-tuple-element.61.refs_3_), custom_call_target="tpu_custom_call" | custom-call | flops 10000000000 | bytes 10000000 | tf_op jit(solution)/shard_map/motion_again/pallas_call | solution.py:49
  41.1 3.0 %all-to-all-start.1 = ((f32[32,2,128]{2,1,0:T(2,128)}), f32[32,2,128]{2,1,0:T(2,128)S(1)}, u32[]{:S(2)}, u32[]{:S(2)}) async-start(f32[32,2,128]{2,1,0:T(2,128)} %bitcast.5), calls=%async_computation.1 | async-start | bytes 65536 | tf_op jit(solution)/shard_map/all_to_all | solution.py:789
  44.1 0.0 collective-permute-done.10.refs_5_
  44.1 0.0 collective-permute-done.11.refs_6_
  44.1 0.0 collective-permute-done.8.refs_3_
  44.1 0.0 collective-permute-done.9.refs_4_
  44.1 3.4 %stress.1 = (f32[6,512,128]{2,1,0:T(8,128)S(1)}, f32[5,32,128]{2,1,0:T(8,128)S(1)}, f32[5,32,128]{2,1,0:T(8,128)S(1)}, f32[16,512]{1,0:T(8,128)S(1)}) custom-call(f32[3,512,128]{2,1,0:T(8,128)S(1)} %get-tuple-element.62.refs_0_, f32[6,512,128]{2,1,0:T(8,128)} %get-tuple-element.64.refs_1_, f32[5,512,128]{2,1,0:T(8,128)} %get-tuple-element.65.refs_2_, ...), custom_call_target="tpu_custom_call" | custom-call | flops 24999999488 | bytes 25000000 | tf_op jit(solution)/shard_map/stress/pallas_call | solution.py:49
  47.5 1.8 %collective-permute-start.14 = (f32[16,512]{1,0:T(8,128)S(1)}, f32[16,512]{1,0:T(8,128)S(1)}, u32[]{:S(2)}, u32[]{:S(2)}) collective-permute-start(f32[16,512]{1,0:T(8,128)S(1)} %get-tuple-element.74), channel_id=1, source_target_pairs={{0,1},{2,3},{1,0},{3,2},{4,5},{6,7},{5,4},{7,6},{8,9},{10,11},{9,8... | collective-permute-start | bytes 98312 | tf_op jit(solution)/shard_map/ppermute | solution.py:85
  49.3 2.4 %collective-permute-start.15 = (f32[16,512]{1,0:T(8,128)S(1)}, f32[16,512]{1,0:T(8,128)S(1)}, u32[]{:S(2)}, u32[]{:S(2)}) collective-permute-start(f32[16,512]{1,0:T(8,128)S(1)} %get-tuple-element.74), channel_id=1, source_target_pairs={{1,2},{3,0},{2,1},{0,3},{5,6},{7,4},{6,5},{4,7},{9,10},{11,8},{10,... | collective-permute-start | bytes 98312 | tf_op jit(solution)/shard_map/ppermute | solution.py:85
  51.7 0.0 collective-permute-start.12
  51.7 2.5 %collective-permute-start.13 = (f32[5,32,128]{2,1,0:T(8,128)S(1)}, f32[5,32,128]{2,1,0:T(8,128)S(1)}, u32[]{:S(2)}, u32[]{:S(2)}) collective-permute-start(f32[5,32,128]{2,1,0:T(8,128)S(1)} %get-tuple-element.73), channel_id=1, source_target_pairs={{4,8},{12,16},{20,24},{28,0},{8,4},{16,12},{24,20},{0,28},{5,9},{1... | collective-permute-start | bytes 245768 | tf_op jit(solution)/shard_map/ppermute | solution.py:85
  54.2 0.0 all-to-all-done.1
  54.2 0.0 copy-start.5
  54.2 5.9 %finish.1 = (f32[3,16,128]{2,1,0:T(8,128)S(1)}, f32[64,256]{1,0:T(8,128)}, f32[64,256]{1,0:T(8,128)}) custom-call(f32[64,128]{1,0:T(8,128)} %motion_again.1.sent_ref, f32[64,128]{1,0:T(8,128)S(1)} %bitcast.11, f32[64,128]{1,0:T(8,128)S(1)} %bitcast.10, f32[64,256]{1,0:T(8,128)S(1)} %get-tuple-element.76.base_ref, f32[64,256]{1,0:T(8,128)S(1)} %get-tuple-element.77.drift_ref, ...), custom_call_target="tpu_custom_call" | custom-call | flops 60000002048 | bytes 60000000 | tf_op jit(solution)/shard_map/finish/pallas_call | solution.py:49
  60.1 0.0 collective-permute-done.14.refs_5_
  60.1 0.0 collective-permute-done.15.refs_6_
  60.1 0.0 collective-permute-done.12.refs_3_
  60.2 0.0 collective-permute-done.13.refs_4_
  60.2 0.0 copy-done.5
  60.2 2.8 %velocity.3 = f32[3,32,2,8,128]{4,3,2,1,0:T(8,128)} custom-call(f32[3,512,128]{2,1,0:T(8,128)S(1)} %get-tuple-element.62.refs_0_, f32[6,512,128]{2,1,0:T(8,128)S(1)} %get-tuple-element.70.refs_1_, f32[3,512,128]{2,1,0:T(8,128)S(1)} %copy-done.5, f32[5,32,128]{2,1,0:T(8,128)S(1)} %collective-permute-done.12.refs_3_, ...), custom_call_target="tpu_custom_call" | custom-call | flops 24999999488 | bytes 25000000 | tf_op jit(solution)/shard_map/velocity/pallas_call | solution.py:49
Async XLA Ops:
  4.5 14.7 %all-to-all-start = ((f32[32,2,128]{2,1,0:T(2,128)}), f32[32,2,128]{2,1,0:T(2,128)S(1)}, u32[]{:S(2)}, u32[]{:S(2)}) async-start(f32[32,2,128]{2,1,0:T(2,128)} %bitcast.3), calls=%async_computation | async-start | bytes 65536 | tf_op jit(solution)/shard_map/all_to_all | solution.py:789
  11.8 8.2 %collective-permute-start.2 = (f32[16,512]{1,0:T(8,128)S(1)}, f32[16,512]{1,0:T(8,128)S(1)}, u32[]{:S(2)}, u32[]{:S(2)}) collective-permute-start(f32[16,512]{1,0:T(8,128)S(1)} %get-tuple-element.47), channel_id=1, source_target_pairs={{0,1},{2,3},{1,0},{3,2},{4,5},{6,7},{5,4},{7,6},{8,9},{10,11},{9,8... | collective-permute-start | bytes 98312 | tf_op jit(solution)/shard_map/ppermute | solution.py:85
  13.6 6.4 %collective-permute-start.3 = (f32[16,512]{1,0:T(8,128)S(1)}, f32[16,512]{1,0:T(8,128)S(1)}, u32[]{:S(2)}, u32[]{:S(2)}) collective-permute-start(f32[16,512]{1,0:T(8,128)S(1)} %get-tuple-element.47), channel_id=1, source_target_pairs={{1,2},{3,0},{2,1},{0,3},{5,6},{7,4},{6,5},{4,7},{9,10},{11,8},{10,... | collective-permute-start | bytes 98312 | tf_op jit(solution)/shard_map/ppermute | solution.py:85
  16.0 4.0 %collective-permute-start = (f32[7,32,128]{2,1,0:T(8,128)S(1)}, f32[7,32,128]{2,1,0:T(8,128)S(1)}, u32[]{:S(2)}, u32[]{:S(2)}) collective-permute-start(f32[7,32,128]{2,1,0:T(8,128)S(1)} %get-tuple-element.45), channel_id=1, source_target_pairs={{0,4},{8,12},{16,20},{24,28},{4,0},{12,8},{20,16},{28,24},{1,5},{9... | collective-permute-start | bytes 344072 | tf_op jit(solution)/shard_map/ppermute | solution.py:85
  16.0 5.7 %collective-permute-start.1 = (f32[7,32,128]{2,1,0:T(8,128)S(1)}, f32[7,32,128]{2,1,0:T(8,128)S(1)}, u32[]{:S(2)}, u32[]{:S(2)}) collective-permute-start(f32[7,32,128]{2,1,0:T(8,128)S(1)} %get-tuple-element.46), channel_id=1, source_target_pairs={{4,8},{12,16},{20,24},{28,0},{8,4},{16,12},{24,20},{0,28},{5,9},{1... | collective-permute-start | bytes 344072 | tf_op jit(solution)/shard_map/ppermute | solution.py:85
  21.7 7.6 %copy-start = (f32[64,256]{1,0:T(8,128)S(1)}, f32[64,256]{1,0:T(8,128)}, u32[]{:S(2)}) copy-start(f32[64,256]{1,0:T(8,128)} %rate_ref.1) | copy-start | bytes 196612
  21.7 7.6 %copy-start.1 = (f32[64,256]{1,0:T(8,128)S(1)}, f32[64,256]{1,0:T(8,128)}, u32[]{:S(2)}) copy-start(f32[64,256]{1,0:T(8,128)} %raw_ref.1) | copy-start | bytes 196612
  21.7 7.6 %copy-start.2 = (f32[64,256]{1,0:T(8,128)S(1)}, f32[64,256]{1,0:T(8,128)}, u32[]{:S(2)}) copy-start(f32[64,256]{1,0:T(8,128)} %coupling_ref.3) | copy-start | bytes 196612
  21.7 7.6 %copy-start.3 = (s32[64]{0:T(128)S(1)}, s32[64]{0:T(128)}, u32[]{:S(2)}) copy-start(s32[64]{0:T(128)} %param.23) | copy-start | bytes 772
  21.7 7.6 %copy-start.4 = (s32[64,1]{0,1:T(1,128)S(1)}, s32[64,1]{0,1:T(1,128)}, u32[]{:S(2)}) copy-start(s32[64,1]{0,1:T(1,128)} %param.24) | copy-start | bytes 772
  26.1 6.4 %collective-permute-start.6 = (f32[16,512]{1,0:T(8,128)S(1)}, f32[16,512]{1,0:T(8,128)S(1)}, u32[]{:S(2)}, u32[]{:S(2)}) collective-permute-start(f32[16,512]{1,0:T(8,128)S(1)} %get-tuple-element.53), channel_id=1, source_target_pairs={{0,1},{2,3},{1,0},{3,2},{4,5},{6,7},{5,4},{7,6},{8,9},{10,11},{9,8... | collective-permute-start | bytes 98312 | tf_op jit(solution)/shard_map/ppermute | solution.py:85
  26.7 5.7 %collective-permute-start.7 = (f32[16,512]{1,0:T(8,128)S(1)}, f32[16,512]{1,0:T(8,128)S(1)}, u32[]{:S(2)}, u32[]{:S(2)}) collective-permute-start(f32[16,512]{1,0:T(8,128)S(1)} %get-tuple-element.53), channel_id=1, source_target_pairs={{1,2},{3,0},{2,1},{0,3},{5,6},{7,4},{6,5},{4,7},{9,10},{11,8},{10,... | collective-permute-start | bytes 98312 | tf_op jit(solution)/shard_map/ppermute | solution.py:85
  27.7 4.8 %collective-permute-start.4 = (f32[5,32,128]{2,1,0:T(8,128)S(1)}, f32[5,32,128]{2,1,0:T(8,128)S(1)}, u32[]{:S(2)}, u32[]{:S(2)}) collective-permute-start(f32[5,32,128]{2,1,0:T(8,128)S(1)} %get-tuple-element.51), channel_id=1, source_target_pairs={{0,4},{8,12},{16,20},{24,28},{4,0},{12,8},{20,16},{28,24},{1,5},{9... | collective-permute-start | bytes 245768 | tf_op jit(solution)/shard_map/ppermute | solution.py:85
  27.7 4.8 %collective-permute-start.5 = (f32[5,32,128]{2,1,0:T(8,128)S(1)}, f32[5,32,128]{2,1,0:T(8,128)S(1)}, u32[]{:S(2)}, u32[]{:S(2)}) collective-permute-start(f32[5,32,128]{2,1,0:T(8,128)S(1)} %get-tuple-element.52), channel_id=1, source_target_pairs={{4,8},{12,16},{20,24},{28,0},{8,4},{16,12},{24,20},{0,28},{5,9},{1... | collective-permute-start | bytes 245768 | tf_op jit(solution)/shard_map/ppermute | solution.py:85
  34.9 9.2 %collective-permute-start.10 = (f32[16,512]{1,0:T(8,128)S(1)}, f32[16,512]{1,0:T(8,128)S(1)}, u32[]{:S(2)}, u32[]{:S(2)}) collective-permute-start(f32[16,512]{1,0:T(8,128)S(1)} %get-tuple-element.68), channel_id=1, source_target_pairs={{0,1},{2,3},{1,0},{3,2},{4,5},{6,7},{5,4},{7,6},{8,9},{10,11},{9,8... | collective-permute-start | bytes 98312 | tf_op jit(solution)/shard_map/ppermute | solution.py:85
  35.9 8.2 %collective-permute-start.11 = (f32[16,512]{1,0:T(8,128)S(1)}, f32[16,512]{1,0:T(8,128)S(1)}, u32[]{:S(2)}, u32[]{:S(2)}) collective-permute-start(f32[16,512]{1,0:T(8,128)S(1)} %get-tuple-element.68), channel_id=1, source_target_pairs={{1,2},{3,0},{2,1},{0,3},{5,6},{7,4},{6,5},{4,7},{9,10},{11,8},{10,... | collective-permute-start | bytes 98312 | tf_op jit(solution)/shard_map/ppermute | solution.py:85
  38.3 5.8 %collective-permute-start.8 = (f32[5,32,128]{2,1,0:T(8,128)S(1)}, f32[5,32,128]{2,1,0:T(8,128)S(1)}, u32[]{:S(2)}, u32[]{:S(2)}) collective-permute-start(f32[5,32,128]{2,1,0:T(8,128)S(1)} %get-tuple-element.66), channel_id=1, source_target_pairs={{0,4},{8,12},{16,20},{24,28},{4,0},{12,8},{20,16},{28,24},{1,5},{9... | collective-permute-start | bytes 245768 | tf_op jit(solution)/shard_map/ppermute | solution.py:85
  38.3 5.8 %collective-permute-start.9 = (f32[5,32,128]{2,1,0:T(8,128)S(1)}, f32[5,32,128]{2,1,0:T(8,128)S(1)}, u32[]{:S(2)}, u32[]{:S(2)}) collective-permute-start(f32[5,32,128]{2,1,0:T(8,128)S(1)} %get-tuple-element.67), channel_id=1, source_target_pairs={{4,8},{12,16},{20,24},{28,0},{8,4},{16,12},{24,20},{0,28},{5,9},{1... | collective-permute-start | bytes 245768 | tf_op jit(solution)/shard_map/ppermute | solution.py:85
  41.1 13.1 %all-to-all-start.1 = ((f32[32,2,128]{2,1,0:T(2,128)}), f32[32,2,128]{2,1,0:T(2,128)S(1)}, u32[]{:S(2)}, u32[]{:S(2)}) async-start(f32[32,2,128]{2,1,0:T(2,128)} %bitcast.5), calls=%async_computation.1 | async-start | bytes 65536 | tf_op jit(solution)/shard_map/all_to_all | solution.py:789
  47.5 12.6 %collective-permute-start.14 = (f32[16,512]{1,0:T(8,128)S(1)}, f32[16,512]{1,0:T(8,128)S(1)}, u32[]{:S(2)}, u32[]{:S(2)}) collective-permute-start(f32[16,512]{1,0:T(8,128)S(1)} %get-tuple-element.74), channel_id=1, source_target_pairs={{0,1},{2,3},{1,0},{3,2},{4,5},{6,7},{5,4},{7,6},{8,9},{10,11},{9,8... | collective-permute-start | bytes 98312 | tf_op jit(solution)/shard_map/ppermute | solution.py:85
  49.3 10.8 %collective-permute-start.15 = (f32[16,512]{1,0:T(8,128)S(1)}, f32[16,512]{1,0:T(8,128)S(1)}, u32[]{:S(2)}, u32[]{:S(2)}) collective-permute-start(f32[16,512]{1,0:T(8,128)S(1)} %get-tuple-element.74), channel_id=1, source_target_pairs={{1,2},{3,0},{2,1},{0,3},{5,6},{7,4},{6,5},{4,7},{9,10},{11,8},{10,... | collective-permute-start | bytes 98312 | tf_op jit(solution)/shard_map/ppermute | solution.py:85
  51.7 8.4 %collective-permute-start.12 = (f32[5,32,128]{2,1,0:T(8,128)S(1)}, f32[5,32,128]{2,1,0:T(8,128)S(1)}, u32[]{:S(2)}, u32[]{:S(2)}) collective-permute-start(f32[5,32,128]{2,1,0:T(8,128)S(1)} %get-tuple-element.72), channel_id=1, source_target_pairs={{0,4},{8,12},{16,20},{24,28},{4,0},{12,8},{20,16},{28,24},{1,5},{9... | collective-permute-start | bytes 245768 | tf_op jit(solution)/shard_map/ppermute | solution.py:85
  51.7 8.4 %collective-permute-start.13 = (f32[5,32,128]{2,1,0:T(8,128)S(1)}, f32[5,32,128]{2,1,0:T(8,128)S(1)}, u32[]{:S(2)}, u32[]{:S(2)}) collective-permute-start(f32[5,32,128]{2,1,0:T(8,128)S(1)} %get-tuple-element.73), channel_id=1, source_target_pairs={{4,8},{12,16},{20,24},{28,0},{8,4},{16,12},{24,20},{0,28},{5,9},{1... | collective-permute-start | bytes 245768 | tf_op jit(solution)/shard_map/ppermute | solution.py:85
  54.2 5.9 %copy-start.5 = (f32[3,512,128]{2,1,0:T(8,128)S(1)}, f32[3,512,128]{2,1,0:T(8,128)}, u32[]{:S(2)}) copy-start(f32[3,512,128]{2,1,0:T(8,128)} %get-tuple-element.71.refs_2_) | copy-start | bytes 2359300

commit v3 on v2

--- a/solution.py
+++ b/solution.py
@@ -23,12 +23,15 @@
 
 COSTS = {
     "first": 30_000_000,
+    "table": 60_000_000,
+    "load": 20_000_000,
     "begin": 40_000_000,
     "stress": 25_000_000,
     "surface": 10_000_000,
     "pull": 30_000_000,
     "velocity": 25_000_000,
     "motion_again": 10_000_000,
+    "prepare": 60_000_000,
     "finish": 60_000_000,
 }
 
@@ -197,28 +200,45 @@
         ext[c, x + 2, PAD + layers : PAD + layers + PAD, :] = jnp.zeros((PAD, 128), f32)
 
 
-def edges(layers, arrived, vt_ref, bt_ref, mt_ref, even_ref, odd_ref, col_ref, pack):
+def edges(layers, v_ref, b_ref, m_ref, vt_ref, bt_ref, mt_ref, even_ref, odd_ref, col_ref, pack):
     size_x = vt_ref.shape[1] // layers
 
     def slab(ref, x):
         return ref[x * layers : (x + 1) * layers, :]
 
     for x in range(size_x):
-        arrived(x)
-        pack[x * layers : (x + 1) * layers, :] = packed(
-            [
-                (slab(vt_ref.at[0], x), 0, 3, 1),
-                (slab(vt_ref.at[1], x), 3, 3, 5),
-                (slab(vt_ref.at[2], x), 6, 3, 7),
-                (slab(bt_ref, x), 9, 1, 9),
-                (slab(mt_ref, x), 10, 1, 10),
-            ]
+        cut = pl.ds(x * layers, layers)
+        turned = pl.ds(x, layers, stride=size_x)
+        v = [v_ref[c, turned, :] for c in range(3)]
+        buoy, shear = b_ref[turned, :], m_ref[turned, :]
+        for c in range(3):
+            vt_ref[c, cut, :] = v[c]
+        bt_ref[cut, :] = buoy
+        mt_ref[cut, :] = shear
+        pack[cut, :] = packed(
+            [(v[0], 0, 3, 1), (v[1], 3, 3, 5), (v[2], 6, 3, 7), (buoy, 9, 1, 9), (shear, 10, 1, 10)]
         )
     last = size_x - 1
     up = [slab(vt_ref.at[c], x) for c, x in ((0, last - 1), (0, last), (1, last), (2, last))]
     down = [slab(vt_ref.at[c], x) for c, x in ((0, 0), (1, 0), (1, 1), (2, 0), (2, 1))]
     two_ways(up, down + [slab(bt_ref, 0), slab(mt_ref, 0)], even_ref, odd_ref)
     send_columns(pack, col_ref)
+
+
+def load_kernel(layers, after_ref, s_hbm, l_hbm, st_ref, lt_ref, s_ref, l_ref, sems):
+    del after_ref
+    size_x = l_ref.shape[0] // layers
+    copies = fetch(
+        [l_hbm] + [s_hbm.at[c] for c in range(6)], [l_ref] + [s_ref.at[c] for c in range(6)], sems
+    )
+    for c, copy in enumerate(copies):
+        copy.wait()
+        for x in range(size_x):
+            cut, turned = pl.ds(x * layers, layers), pl.ds(x, layers, stride=size_x)
+            if c == 0:
+                lt_ref[cut, :] = l_ref[turned, :]
+            else:
+                st_ref[c - 1, cut, :] = s_ref[c - 1, turned, :]
 
 
 def materials(layers, b_ref, l_ref, m_ref, above, cols, table_ref, mat_ref, buoy_ref, bs, ms, tb, tm):
@@ -268,7 +288,7 @@
         m_en = jnp.where(in_y & in_x, north(ms[x + 1, inner, :], tm[x + 1, inner, :]), m)
         m_ez = jnp.where(in_z & in_x, ms[x + 1, below, :], m)
         m_nz = jnp.where(in_z & in_y, north(ms[x, below, :], tm[x, below, :]), m)
-        mat_ref[0, cut, :] = time_step * l_ref[x]
+        mat_ref[0, cut, :] = time_step * l_ref[cut, :]
         mat_ref[1, cut, :] = (2.0 * time_step) * m
         mat_ref[2, cut, :] = (0.25 * time_step) * (m + m_e + m_n + m_en)
         mat_ref[3, cut, :] = (0.25 * time_step) * (m + m_e + m_z + m_ez)
@@ -342,8 +362,8 @@
     v_ref,
     b_ref,
     m_ref,
-    s_hbm,
-    l_hbm,
+    s_ref,
+    l_ref,
     stiff_hbm,
     x_even,
     x_odd,
@@ -354,13 +374,9 @@
     even_ref,
     odd_ref,
     col_ref,
+    mat_ref,
     buoy_ref,
     stiff_ref,
-    mat_hbm,
-    buoy_hbm,
-    s_ref,
-    l_ref,
-    mat_ref,
     bs,
     ms,
     tb,
@@ -370,33 +386,23 @@
     pack,
     sems,
 ):
-    size_x = v_ref.shape[1] // layers
-    own = range(size_x)
-    sources = [l_hbm.at[:, x] for x in own] + [s_hbm.at[:, :, x] for x in own]
-    targets = [l_ref.at[x] for x in own] + [s_ref.at[:, x] for x in own]
     half = stiff_ref.shape[0]
-    copies = fetch(
-        sources + [stiff_hbm.at[pl.ds(0, half)]], targets + [stiff_ref.at[...]], sems
-    )
+    half = stiff_ref.shape[0]
+    copies = fetch([stiff_hbm.at[pl.ds(0, half)]], [stiff_ref], sems)
     _, _, south_ok, north_ok = place()
     below, above = below_above("gx", x_even, x_odd)
     receive_columns(y_even, y_odd, (0, 3, 4, 6), south_ok, north_ok, cols)
-    for x in own:
-        copies[x].wait()
     materials(layers, b_ref, l_ref, m_ref, above, cols, table_ref, mat_ref, buoy_ref, bs, ms, tb, tm)
-    leaving = fetch([mat_ref, buoy_ref], [mat_hbm, buoy_hbm], sems.at[pl.ds(2 * size_x + 1, 2)])
 
     def ready(strip):
-        for x in range(strip * STRIP, (strip + 1) * STRIP):
-            copies[size_x + x].wait()
+        pass
 
     def old(c, x, cut):
-        return s_ref[c, x]
+        return s_ref[c, cut, :]
 
     refs = (even_ref, odd_ref, col_ref)
     stresses(layers, v_ref, old, ready, mat_ref, below, above, cols, out_ref, refs, ext, pack)
-    for copy in leaving + copies[2 * size_x :]:
-        copy.wait()
+    copies[0].wait()
 
 
 def stress_kernel(
@@ -441,15 +447,8 @@
     stresses(layers, v_ref, old, ready, mat_ref, below, above, cols, out_ref, refs, ext, pack)
 
 
-def velocity_kernel(
-    layers, last, v_ref, s_ref, buoy_ref, x_even, x_odd, y_even, y_odd, push_ref, *refs
-):
-    if last:
-        out_hbm, out_ref, ext, cols, sems = refs
-    else:
-        out_ref, even_ref, odd_ref, col_ref, kept_hbm, ext, cols, pack, sems = refs
-        keep = pltpu.make_async_copy(s_ref, kept_hbm, sems.at[0])
-        keep.start()
+def moving(layers, v_ref, s_ref, buoy_ref, halo, push_ref, ext, cols):
+    x_even, x_odd, y_even, y_odd = halo
     size_x = v_ref.shape[1] // layers
     west_ok, east_ok, south_ok, north_ok = place()
     below, above = below_above("gx", x_even, x_odd)
@@ -462,8 +461,7 @@
     over = size_x + 2
     extend(ext, ((0, 0, over), (1, 0, over + 1), (2, 1, over), (3, 2, over)), above, east_ok, layers)
 
-    def step(x, carry):
-        cut = pl.ds(pl.multiple_of(x * layers, layers), layers)
+    def fresh(x, cut):
         ghost = cols[cut, :]
         yy, xy, yz = s_ref[1, cut, :], ext[1, x + 2, inner, :], ext[3, x + 2, inner, :]
         gyy, gxy, gyz = roll(ghost, -1), roll(ghost, -5), roll(ghost, -8)
@@ -471,29 +469,45 @@
         ay = across(ext, 1, x, False, layers) + slopes(yy, gyy, True) + down(ext, 3, x, False, layers)
         az = across(ext, 2, x, False, layers) + slopes(yz, gyz, False) + down(ext, 4, x, True, layers)
         layer = lax.broadcasted_iota(jnp.int32, yy.shape, 0)
-        fresh = []
+        result = []
         for c, accel in enumerate((ax, ay, az)):
             pushed = jnp.where(layer == 0, push_ref[c, pl.ds(x, 1), :], 0.0)
-            fresh.append(v_ref[c, cut, :] + buoy_ref[c, cut, :] * accel + pushed)
-        if last:
-            for c in range(3):
-                out_ref[x // TILE, c, :, lax.rem(x, TILE), :] = fresh[c]
-        else:
-            for c in range(3):
-                out_ref[c, cut, :] = fresh[c]
-            pack[cut, :] = packed([(fresh[0], 0, 3, 1), (fresh[1], 3, 3, 5), (fresh[2], 6, 3, 7)])
+            result.append(v_ref[c, cut, :] + buoy_ref[c, cut, :] * accel + pushed)
+        return result
+
+    return fresh
+
+
+def velocity_kernel(
+    layers,
+    v_ref,
+    s_ref,
+    buoy_ref,
+    x_even,
+    x_odd,
+    y_even,
+    y_odd,
+    push_ref,
+    out_ref,
+    even_ref,
+    odd_ref,
+    col_ref,
+    ext,
+    cols,
+    pack,
+):
+    size_x = v_ref.shape[1] // layers
+    halo = (x_even, x_odd, y_even, y_odd)
+    fresh = moving(layers, v_ref, s_ref, buoy_ref, halo, push_ref, ext, cols)
+
+    def step(x, carry):
+        cut = pl.ds(pl.multiple_of(x * layers, layers), layers)
+        v = fresh(x, cut)
+        for c in range(3):
+            out_ref[c, cut, :] = v[c]
+        pack[cut, :] = packed([(v[0], 0, 3, 1), (v[1], 3, 3, 5), (v[2], 6, 3, 7)])
         return carry
 
-    if last:
-        leaving = []
-        for tile in range(size_x // TILE):
-            lax.fori_loop(tile * TILE, (tile + 1) * TILE, step, 0, unroll=4)
-            leaving += fetch(
-                [out_ref.at[tile]], [out_hbm.at[:, :, tile]], sems.at[pl.ds(tile, 1)]
-            )
-        for copy in leaving:
-            copy.wait()
-        return
     lax.fori_loop(0, size_x, step, 0, unroll=4)
     send_columns(pack, col_ref)
 
@@ -503,7 +517,6 @@
     up = [slab(c, size_x - x) for c, x in ((0, 2), (0, 1), (1, 1), (2, 1))]
     down_rows = [slab(c, x) for c, x in ((0, 0), (1, 0), (1, 1), (2, 0), (2, 1))]
     two_ways(up, down_rows, even_ref, odd_ref)
-    keep.wait()
 
 
 def third(value, e):
@@ -571,30 +584,19 @@
     out_ref[...] = jnp.dot(to_slot, row, precision=exact, preferred_element_type=f32)
 
 
-def first_kernel(layers, span, *refs):
-    far, outs, scratch = refs[:9], refs[9:16], refs[16:]
-    small, pack, sems = scratch[:6], scratch[6], scratch[7]
-    vt, bt, mt = outs[:3]
-    size_x = vt.shape[1] // layers
-    cuts = [pl.ds(x * layers, layers) for x in range(size_x)]
-    sources, targets = list(far[3:]), list(small)
-    for x, cut in enumerate(cuts):
-        sources += [far[0].at[:, :, x], far[1].at[:, x], far[2].at[:, x]]
-        targets += [vt.at[:, cut], bt.at[cut], mt.at[cut]]
-    copies = fetch(sources, targets, sems)
-    for copy in copies[:6]:
+def first_kernel(layers, v_hbm, b_hbm, m_hbm, *refs):
+    outs, near, pack, sems = refs[:6], refs[6:9], refs[9], refs[10]
+    for copy in fetch((v_hbm, b_hbm, m_hbm), near, sems):
         copy.wait()
-    table(span, *small, outs[6])
-
-    def arrived(x):
-        for copy in copies[6 + 3 * x : 9 + 3 * x]:
-            copy.wait()
-
-    edges(layers, arrived, *outs[:6], pack)
-    first = mt[pl.ds(0, layers), 0:1]
+    edges(layers, *near, *outs, pack)
+
+
+def table_kernel(span, layers, shear_ref, *refs):
+    table(span, *refs)
+    first = shear_ref[pl.ds(0, layers), 0:1]
     spot = lax.broadcasted_iota(jnp.int32, (layers, 128), 1) - AT_CORNER
     own = spot == lax.broadcasted_iota(jnp.int32, (layers, 128), 0)
-    outs[6][...] += jnp.sum(jnp.where(own, first, 0.0), axis=0, keepdims=True)
+    refs[-1][...] += jnp.sum(jnp.where(own, first, 0.0), axis=0, keepdims=True)
 
 
 def sums_by_third(row, sums):
@@ -736,7 +738,7 @@
     out_ref[...] = rows
 
 
-def finish_kernel(
+def prepare_kernel(
     sent_ref,
     back_ref,
     table_ref,
@@ -745,16 +747,10 @@
     coupling_ref,
     counts_ref,
     owner_ref,
-    stiff_hbm,
     push_ref,
     drift_out,
     rate_out,
-    half,
-    pull,
-    stiff_ref,
-    sems,
 ):
-    copies = fetch_strips(stiff_hbm, 0, stiff_ref, sems)
     table, sent, back = table_ref[...], sent_ref[...], back_ref[...]
     reaction = []
     for c in range(3):
@@ -769,18 +765,89 @@
     mask = counted(counts_ref, coupling.shape)
     rate = base_ref[...] + time_step * coupling * spread_thirds(moved, FIRST, coupling)
     rate = jnp.where(mask, rate, 0.0)
-    drift = jnp.where(mask, drift_ref[...] + time_step * rate, 0.0)
-    half[...] = drift
-    pull[...] = jnp.zeros(pull.shape, f32)
-    size = half.shape[0] // len(copies)
-    for c, copy in enumerate(copies):
-        copy.wait()
-        products(stiff_ref, 0, half, pull, c * size, (c + 1) * size)
-    relative = rate - spread_thirds(moved, SECOND, coupling)
-    rate = rate - time_step * pull[...] - time_step * coupling * relative
-    rate = jnp.where(mask, rate, 0.0)
+    drift_out[...] = jnp.where(mask, drift_ref[...] + time_step * rate, 0.0)
+    rate_out[...] = rate - time_step * coupling * (rate - spread_thirds(moved, SECOND, coupling))
+
+
+def finish_kernel(
+    layers,
+    v_ref,
+    s_ref,
+    buoy_ref,
+    x_even,
+    x_odd,
+    y_even,
+    y_odd,
+    push_ref,
+    half,
+    rate_ref,
+    counts_ref,
+    stiff_hbm,
+    out_hbm,
+    drift_out,
+    rate_out,
+    out_ref,
+    ext,
+    cols,
+    pull,
+    stiff_ref,
+    sems,
+    out_sems,
+):
+    fetch_strips(stiff_hbm, 0, stiff_ref, sems)
+    size_x = v_ref.shape[1] // layers
+    halo = (x_even, x_odd, y_even, y_odd)
+    fresh = moving(layers, v_ref, s_ref, buoy_ref, halo, push_ref, ext, cols)
+    strips = sems.shape[0]
+    share = half.shape[0] // strips
+    batch = size_x // strips
+
+    def advance(strip):
+        for i in range(batch):
+            x = strip * batch + i
+            v = fresh(x, pl.ds(pl.multiple_of(x * layers, layers), layers))
+            for c in range(3):
+                out_ref[x // TILE, c, :, lax.rem(x, TILE), :] = v[c]
+
+    def multiply(strip):
+        cut = pl.ds(pl.multiple_of(strip * share, share), share)
+        pltpu.make_async_copy(stiff_hbm.at[cut], stiff_ref.at[cut], sems.at[strip]).wait()
+        rounded = half[cut, :].astype(jnp.bfloat16)
+        row = lax.broadcasted_iota(jnp.int32, rounded.shape, 0)
+        total = jnp.zeros(rounded.shape, f32)
+        for b in range(share):
+            part = lax.dot_general(
+                rounded,
+                stiff_ref[strip * share + b],
+                (((1,), (1,)), ((), ())),
+                preferred_element_type=f32,
+            )
+            total = jnp.where(row == b, part, total)
+        pull[cut, :] = total
+
+    def leave(tile):
+        return pltpu.make_async_copy(out_ref.at[tile], out_hbm.at[:, :, tile], out_sems.at[tile])
+
+    def step(strip, carry):
+        multiply(strip - 1)
+        advance(strip)
+        return carry
+
+    tiles = size_x // TILE
+    for tile in range(tiles):
+        begin, end = tile * strips // tiles, (tile + 1) * strips // tiles
+        if tile == 0:
+            advance(0)
+            begin = 1
+        lax.fori_loop(begin, end, step, 0)
+        leave(tile).start()
+    multiply(strips - 1)
+    mask = counted(counts_ref, half.shape)
+    rate = jnp.where(mask, rate_ref[...] - time_step * pull[...], 0.0)
     rate_out[...] = rate
-    drift_out[...] = jnp.where(mask, drift + time_step * rate, 0.0)
+    drift_out[...] = jnp.where(mask, half[...] + time_step * rate, 0.0)
+    for tile in range(tiles):
+        leave(tile).wait()
 
 
 def trade(rows):
@@ -825,9 +892,10 @@
     tall = layers + 2 * PAD
     plane = near_by(number, width)
     dma = pltpu.SemaphoreType.DMA
-    far = (soil_velocity, buoyancy, shear_modulus, drift_rate, coupling, contact, counts, owner, corner)
-    outs = call(
-        bind(first_kernel, layers, span),
+    flat = [a.reshape(cells, size_y) for a in (buoyancy, shear_modulus, lame_first)]
+    far = (soil_velocity.reshape(3, cells, size_y), *flat[:2])
+    vt, bt, mt, one, two, col = call(
+        bind(first_kernel, layers),
         "first",
         (
             near_by(3, cells, size_y),
@@ -836,38 +904,45 @@
             near_by(7, layers, size_y),
             near_by(7, layers, size_y),
             near_by(16, cells),
-            near_by(slots, 128),
         ),
         [Far(a) for a in far],
-        [pltpu.VMEM(a.shape, a.dtype) for a in far[3:]] + [field, dma((6 + 3 * size_x,))],
-    )
-    vt, bt, mt, one, two, col, rows = outs
+        [pltpu.VMEM(a.shape, a.dtype) for a in far] + [field, dma((len(far),))],
+    )
+    (rows,) = call(
+        bind(table_kernel, span, layers),
+        "table",
+        (near_by(slots, 128),),
+        (mt, drift_rate, coupling, contact, counts, owner, corner),
+    )
 
     def exchange(one, two, col):
         return swap(one, "gx", 0), swap(two, "gx", 1), swap(col, "gy", 0), swap(col, "gy", 1)
 
     halo = exchange(one, two, col)
     rows = trade(rows)
+    st, lt = call(
+        bind(load_kernel, layers),
+        "load",
+        (near_by(6, cells, size_y), near_by(cells, size_y)),
+        (rows, Far(soil_stress.reshape(6, cells, size_y)), Far(flat[2])),
+        [vm(6, cells, size_y), field, dma((7,))],
+    )
     half = number // 2
     payload = (near_by(5, layers, size_y), near_by(5, layers, size_y), near_by(16, cells))
     ext = vm(3, size_x + 4, tall, size_y)
     stack = vm(size_x + 1, tall, size_y)
-    st, one, two, col, buoys, stiff, mat_kept, buoy_kept = call(
+    st, one, two, col, means, buoys, stiff = call(
         bind(begin_kernel, layers),
         "begin",
         (
             near_by(6, cells, size_y),
             *payload,
+            near_by(5, cells, size_y),
             near_by(3, cells, size_y),
             near_by(half, width, width, dtype=stiffness.dtype),
-            pltpu.HBM((5, cells, size_y), f32),
-            pltpu.HBM((3, cells, size_y), f32),
         ),
-        (vt, bt, mt, Far(soil_stress), Far(lame_first), Far(stiffness), *halo, rows),
+        (vt, bt, mt, st, lt, Far(stiffness), *halo, rows),
         [
-            vm(6, size_x, layers, size_y),
-            vm(size_x, layers, size_y),
-            vm(5, cells, size_y),
             stack,
             stack,
             stack,
@@ -875,28 +950,9 @@
             ext,
             field,
             field,
-            dma((2 * size_x + 3,)),
+            dma((1,)),
         ],
-        far_outs=(6, 7),
-    )
-
-    def velocity_step(last, v, s, buoys, halo, push):
-        scratch = [vm(5, size_x + 4, tall, size_y), field]
-        tiles = size_x // TILE
-        if last:
-            outs = [pltpu.HBM((3, layers, tiles, TILE, size_y), f32)]
-            scratch = [vm(tiles, 3, layers, TILE, size_y)] + scratch + [dma((tiles,))]
-        else:
-            outs = [near_by(3, cells, size_y), *payload, pltpu.HBM((6, cells, size_y), f32)]
-            scratch += [field, dma((1,))]
-        return call(
-            bind(velocity_kernel, layers, last),
-            "velocity",
-            tuple(outs),
-            (v, s, buoys, *halo, push),
-            scratch,
-            far_outs=(0,) if last else (4,),
-        )
+    )
 
     halo = exchange(one, two, col)
     maps, moved, push = call(
@@ -918,7 +974,14 @@
         ],
     )
     push, following = lax.optimization_barrier((push, following))
-    vt, one, two, col, kept = velocity_step(False, vt, st, buoys, halo, push)
+    bulk = vm(5, size_x + 4, tall, size_y)
+    vt, one, two, col = call(
+        bind(velocity_kernel, layers),
+        "velocity",
+        (near_by(3, cells, size_y), *payload),
+        (vt, st, buoys, *halo, push),
+        [bulk, field, field],
+    )
     halo = exchange(one, two, col)
     (sent,) = call(
         bind(motion_again_kernel, layers),
@@ -933,7 +996,7 @@
         bind(stress_kernel, layers),
         "stress",
         (near_by(6, cells, size_y), *payload),
-        (vt, Far(kept), Far(mat_kept), *halo),
+        (vt, Far(st), Far(means), *halo),
         [
             vm(6, cells, size_y),
             vm(5, cells, size_y),
@@ -946,18 +1009,42 @@
     halo = exchange(one, two, col)
     sent, st = lax.optimization_barrier((sent, st))
     push, drift, rate = call(
-        finish_kernel,
+        prepare_kernel,
+        "prepare",
+        (near_by(3, size_x, size_y), plane, plane),
+        (sent, back, rows, base, drift, coupling, counts, owner),
+    )
+    tiles = size_x // TILE
+    v, drift, rate = call(
+        bind(finish_kernel, layers),
         "finish",
-        (near_by(3, size_x, size_y), shape(number, width), shape(number, width)),
-        (sent, back, rows, base, drift, coupling, counts, owner, Far(stiffness)),
+        (
+            pltpu.HBM((3, layers, tiles, TILE, size_y), f32),
+            shape(number, width),
+            shape(number, width),
+        ),
+        (
+            vt,
+            st,
+            buoys,
+            *halo,
+            push,
+            drift,
+            rate,
+            counts,
+            Far(stiffness),
+        ),
         [
-            vm(number, width),
+            vm(tiles, 3, layers, TILE, size_y),
+            bulk,
+            field,
             vm(number, width),
             pltpu.VMEM(stiffness.shape, stiffness.dtype),
-            dma((2 * chunks,)),
+            dma((chunks,)),
+            dma((tiles,)),
         ],
-    )
-    (v,) = velocity_step(True, vt, st, buoy_kept, halo, push)
+        far_outs=(0,),
+    )
     return v.reshape(soil_velocity.shape), drift, rate
 
 

time: 63.2 us -> 61.2 us (0.968)
  Pallas kernels: 27.3 us -> 25.9 us
  starting transfers between devices: 32.4 us -> 31.7 us
    pallas_call x9 -> x11, Pallas kernels: 27.3 us -> 25.9 us  [call(): pl.pallas_call(kernel, name=name, out_shape=outs, in_specs=specs, out_spe...]
    ppermute x16, starting transfers between devices: 22.1 us -> 21.3 us  [swap(): return lax.ppermute(block, axis, pairs + [(b, a) for a, b in pairs])]
  transfers between devices with their start and end apart: 18 -> 18, of which waited for: 2 -> 3; matrix products, arithmetic and copies ran while one was open for 0% -> 0% of each run, Pallas kernels for 22% -> 19%
where the time goes in v3:
time: 61.2 us; the launch traced here: 60.9 us
  starting transfers between devices  31.7 us (52%)
  Pallas kernels  25.9 us (42%)
  waiting for transfers between devices  2.08 us (3%)
  between operations  1.1 us (2%)
    pallas_call x11, Pallas kernels, call(): pl.pallas_call(kernel, name=name, out_shape=outs, in_specs=specs, out_spe...  25.9 us
    ppermute x16, starting transfers between devices, swap(): return lax.ppermute(block, axis, pairs + [(b, a) for a, b in pairs])  21.3 us
    all_to_all x2, starting transfers between devices, trade(): lax.all_to_all(blocks, ('gx', 'gy'), split_axis=0, concat_axis=0, tiled=T...  10.5 us
    ppermute x16, waiting for transfers between devices, swap(): return lax.ppermute(block, axis, pairs + [(b, a) for a, b in pairs])  1.42 us
  transfers between devices with their start and end apart: 18, of which 3 were waited for; matrix products, arithmetic and copies ran while one was open for 0% of the time, Pallas kernels for 19%

profile of v3, /device:TPU:0, one launch (start us, length us, event | category | flops | bytes accessed | tf_op | source)
XLA Modules:
  0.0 60.9 jit_solution(1053369996026755510)
XLA Ops:
  0.6 0.0 copy-start
  0.6 0.0 copy-start.2
  0.7 0.0 copy-start.3
  0.7 0.0 copy-start.4
  0.7 0.0 copy-start.5
  0.7 0.0 copy-start.6
  0.7 2.1 %first.1 = (f32[3,512,128]{2,1,0:T(8,128)S(1)}, f32[512,128]{1,0:T(8,128)S(1)}, f32[512,128]{1,0:T(8,128)S(1)}, f32[7,32,128]{2,1,0:T(8,128)S(1)}, f32[7,32,128]{2,1,0:T(8,128)S(1)}, /*index=5*/f32[16,512]{1,0:T(8,128)S(1)}) custom-call(f32[3,512,128]{2,1,0:T(8,128)} %bitcast.27, f32[512,128]{1,0:T(8,128)} %bitcast.28, f32[512,128]{1,0:T(8,128)} %bitcast.29), custom_call_target="tpu_custom_call" | custom-call | flops 30000001024 | bytes 30000000 | tf_op jit(solution)/shard_map/first/pallas_call | solution.py:52
  2.8 0.0 copy-done
  2.8 0.0 copy-done.2
  2.8 0.0 copy-done.3
  2.8 0.0 copy-done.4
  2.8 0.0 copy-done.5
  2.8 0.0 copy-done.6
  2.8 1.0 %table.1 = f32[64,128]{1,0:T(8,128)} custom-call(f32[512,128]{1,0:T(8,128)S(1)} %get-tuple-element.46.refs_0_.refs_2_, f32[64,256]{1,0:T(8,128)S(1)} %copy-done, f32[64,256]{1,0:T(8,128)S(1)} %copy-done.2, f32[64,64]{1,0:T(8,128)S(1)} %copy-done.3, s32[1,64]{1,0:T(1,128)S(1)} %bitcast.22, s32[1,64]{1,0:T(1,128)S(1)} %bitcast.19, s32[1,64]{1,0:T(1,128)S(1)} %bitcast.18), custom_call_target="tpu_custom_call" | custom-call | flops 60000002048 | bytes 60000000 | tf_op jit(solution)/shard_map/table/pallas_call | solution.py:52
  3.8 7.3 %all-to-all-start = ((f32[32,2,128]{2,1,0:T(2,128)}), f32[32,2,128]{2,1,0:T(2,128)S(1)}, u32[]{:S(2)}, u32[]{:S(2)}) async-start(f32[32,2,128]{2,1,0:T(2,128)} %bitcast.6), calls=%async_computation | async-start | bytes 65536 | tf_op jit(solution)/shard_map/all_to_all | solution.py:856
  11.1 1.8 %collective-permute-start.2 = (f32[16,512]{1,0:T(8,128)S(1)}, f32[16,512]{1,0:T(8,128)S(1)}, u32[]{:S(2)}, u32[]{:S(2)}) collective-permute-start(f32[16,512]{1,0:T(8,128)S(1)} %get-tuple-element.51), channel_id=1, source_target_pairs={{0,1},{2,3},{1,0},{3,2},{4,5},{6,7},{5,4},{7,6},{8,9},{10,11},{9,8... | collective-permute-start | bytes 98312 | tf_op jit(solution)/shard_map/ppermute | solution.py:88
  13.0 2.4 %collective-permute-start.3 = (f32[16,512]{1,0:T(8,128)S(1)}, f32[16,512]{1,0:T(8,128)S(1)}, u32[]{:S(2)}, u32[]{:S(2)}) collective-permute-start(f32[16,512]{1,0:T(8,128)S(1)} %get-tuple-element.51), channel_id=1, source_target_pairs={{1,2},{3,0},{2,1},{0,3},{5,6},{7,4},{6,5},{4,7},{9,10},{11,8},{10,... | collective-permute-start | bytes 98312 | tf_op jit(solution)/shard_map/ppermute | solution.py:88
  15.3 0.0 collective-permute-start
  15.3 2.5 %collective-permute-start.1 = (f32[7,32,128]{2,1,0:T(8,128)S(1)}, f32[7,32,128]{2,1,0:T(8,128)S(1)}, u32[]{:S(2)}, u32[]{:S(2)}) collective-permute-start(f32[7,32,128]{2,1,0:T(8,128)S(1)} %get-tuple-element.50), channel_id=1, source_target_pairs={{4,8},{12,16},{20,24},{28,0},{8,4},{16,12},{24,20},{0,28},{5,9},{1... | collective-permute-start | bytes 344072 | tf_op jit(solution)/shard_map/ppermute | solution.py:88
  17.8 0.7 %all-to-all-done = f32[32,2,128]{2,1,0:T(2,128)S(1)} async-done(((f32[32,2,128]{2,1,0:T(2,128)}), f32[32,2,128]{2,1,0:T(2,128)S(1)}, u32[]{:S(2)}, u32[]{:S(2)}) %all-to-all-start) | async-done | bytes 32800 | tf_op jit(solution)/shard_map/all_to_all | solution.py:856
  18.5 1.6 %load.1 = (f32[6,512,128]{2,1,0:T(8,128)S(1)}, f32[512,128]{1,0:T(8,128)S(1)}) custom-call(f32[64,128]{1,0:T(8,128)S(1)} %bitcast.13, f32[6,512,128]{2,1,0:T(8,128)} %bitcast.26, f32[512,128]{1,0:T(8,128)} %bitcast.30), custom_call_target="tpu_custom_call" | custom-call | flops 20000000000 | bytes 20000000 | tf_op jit(solution)/shard_map/load/pallas_call | solution.py:52
  20.1 0.8 %surface.1 = (f32[16,64,128]{2,1,0:T(8,128)S(1)}, f32[64,128]{1,0:T(8,128)S(1)}, f32[3,16,128]{2,1,0:T(8,128)S(1)}) custom-call(f32[64,128]{1,0:T(8,128)S(1)} %bitcast.14, f32[3,512,128]{2,1,0:T(8,128)S(1)} %get-tuple-element.44.refs_0_.refs_1_), custom_call_target="tpu_custom_call" | custom-call | flops 10000000000 | bytes 10000000 | tf_op jit(solution)/shard_map/surface/pallas_call | solution.py:52
  21.0 0.0 collective-permute-done.2.refs_8_
  21.0 0.0 collective-permute-done.3.refs_9_
  21.0 0.0 collective-permute-done.refs_6_
  21.0 0.0 collective-permute-done.1.refs_7_
  21.0 3.8 %begin.1 = (f32[6,512,128]{2,1,0:T(8,128)S(1)}, f32[5,32,128]{2,1,0:T(8,128)S(1)}, f32[5,32,128]{2,1,0:T(8,128)S(1)}, f32[16,512]{1,0:T(8,128)S(1)}, f32[5,512,1...) custom-call(f32[3,512,128]{2,1,0:T(8,128)S(1)} %get-tuple-element.44.refs_0_.refs_1_, ...), custom_call_target="tpu_custom_call" | custom-call | flops 40000000000 | bytes 40000000 | tf_op jit(solution)/shard_map/begin/pallas_call | solution.py:52
  24.9 0.0 copy-start.8
  24.9 0.0 copy-start.7
  24.9 0.0 copy-start.9
  24.9 0.6 %collective-permute-start.6 = (f32[16,512]{1,0:T(8,128)S(1)}, f32[16,512]{1,0:T(8,128)S(1)}, u32[]{:S(2)}, u32[]{:S(2)}) collective-permute-start(f32[16,512]{1,0:T(8,128)S(1)} %get-tuple-element.56), channel_id=1, source_target_pairs={{0,1},{2,3},{1,0},{3,2},{4,5},{6,7},{5,4},{7,6},{8,9},{10,11},{9,8... | collective-permute-start | bytes 98312 | tf_op jit(solution)/shard_map/ppermute | solution.py:88
  25.5 1.4 %collective-permute-start.7 = (f32[16,512]{1,0:T(8,128)S(1)}, f32[16,512]{1,0:T(8,128)S(1)}, u32[]{:S(2)}, u32[]{:S(2)}) collective-permute-start(f32[16,512]{1,0:T(8,128)S(1)} %get-tuple-element.56), channel_id=1, source_target_pairs={{1,2},{3,0},{2,1},{0,3},{5,6},{7,4},{6,5},{4,7},{9,10},{11,8},{10,... | collective-permute-start | bytes 98312 | tf_op jit(solution)/shard_map/ppermute | solution.py:88
  26.9 0.0 collective-permute-start.4
  26.9 1.2 %collective-permute-start.5 = (f32[5,32,128]{2,1,0:T(8,128)S(1)}, f32[5,32,128]{2,1,0:T(8,128)S(1)}, u32[]{:S(2)}, u32[]{:S(2)}) collective-permute-start(f32[5,32,128]{2,1,0:T(8,128)S(1)} %get-tuple-element.55), channel_id=1, source_target_pairs={{4,8},{12,16},{20,24},{28,0},{8,4},{16,12},{24,20},{0,28},{5,9},{1... | collective-permute-start | bytes 245768 | tf_op jit(solution)/shard_map/ppermute | solution.py:88
  28.2 0.0 copy-done.1
  28.2 3.1 %pull.1 = (f32[64,256]{1,0:T(8,128)S(1)}, f32[64,256]{1,0:T(8,128)S(1)}, f32[64,128]{1,0:T(8,128)S(1)}) custom-call(bf16[32,256,256]{2,1,0:T(8,128)(2,1)S(1)} %get-tuple-element.58.stiff_ref, bf16[64,256,256]{2,1,0:T(8,128)(2,1)} %refs_11_.1, f32[64,256]{1,0:T(8,128)S(1)} %copy-done.1, f32[64,256]{1,0:T(8,128)S(1)} %copy-done, f32[64,256]{1,0:T(8,128)S(1)} %copy-done.2, ...), custom_call_target="tpu_custom_call" | custom-call | flops 30000001024 | bytes 30000000 | tf_op jit(solution)/shard_map/pull/pallas_call | solution.py:52
  31.2 0.0 collective-permute-done.6.refs_5_
  31.3 0.0 collective-permute-done.7.refs_6_
  31.3 0.0 collective-permute-done.4.refs_3_
  31.3 0.7 %collective-permute-done.5.refs_4_ = f32[5,32,128]{2,1,0:T(8,128)S(1)} collective-permute-done((f32[5,32,128]{2,1,0:T(8,128)S(1)}, f32[5,32,128]{2,1,0:T(8,128)S(1)}, u32[]{:S(2)}, u32[]{:S(2)}) %collective-permute-start.5) | collective-permute-done | bytes 81952 | tf_op jit(solution)/shard_map/ppermute | solution.py:88
  31.9 0.0 copy-done.7
  31.9 2.3 %velocity.1 = (f32[3,512,128]{2,1,0:T(8,128)S(1)}, f32[5,32,128]{2,1,0:T(8,128)S(1)}, f32[5,32,128]{2,1,0:T(8,128)S(1)}, f32[16,512]{1,0:T(8,128)S(1)}) custom-call(f32[3,512,128]{2,1,0:T(8,128)S(1)} %get-tuple-element.44.refs_0_.refs_1_, f32[6,512,128]{2,1,0:T(8,128)S(1)} %get-tuple-element.52.refs_1_, f32[3,512,128]{2,1,0:T(8,128)S(1)} %get-tuple-element.53.refs_2_, ...), custom_call_target="tpu_custom_call" | custom-call | flops 24999999488 | bytes 25000000 | tf_op jit(solution)/shard_map/velocity/pallas_call | solution.py:52
  34.3 0.4 collective-permute-start.10
  34.7 2.4 %collective-permute-start.11 = (f32[16,512]{1,0:T(8,128)S(1)}, f32[16,512]{1,0:T(8,128)S(1)}, u32[]{:S(2)}, u32[]{:S(2)}) collective-permute-start(f32[16,512]{1,0:T(8,128)S(1)} %get-tuple-element.70), channel_id=1, source_target_pairs={{1,2},{3,0},{2,1},{0,3},{5,6},{7,4},{6,5},{4,7},{9,10},{11,8},{10,... | collective-permute-start | bytes 98312 | tf_op jit(solution)/shard_map/ppermute | solution.py:88
  37.1 0.0 collective-permute-start.8
  37.1 1.9 %collective-permute-start.9 = (f32[5,32,128]{2,1,0:T(8,128)S(1)}, f32[5,32,128]{2,1,0:T(8,128)S(1)}, u32[]{:S(2)}, u32[]{:S(2)}) collective-permute-start(f32[5,32,128]{2,1,0:T(8,128)S(1)} %get-tuple-element.69), channel_id=1, source_target_pairs={{4,8},{12,16},{20,24},{28,0},{8,4},{16,12},{24,20},{0,28},{5,9},{1... | collective-permute-start | bytes 245768 | tf_op jit(solution)/shard_map/ppermute | solution.py:88
  39.0 0.8 %motion_again.1.sent_ref = f32[64,128]{1,0:T(8,128)} custom-call(f32[3,512,128]{2,1,0:T(8,128)S(1)} %get-tuple-element.65.refs_0_, f32[16,64,128]{2,1,0:T(8,128)S(1)} %get-tuple-element.62.refs_1_, f32[64,128]{1,0:T(8,128)S(1)} %get-tuple-element.63.refs_2_, f32[64,128]{1,0:T(8,128)S(1)} %get-tuple-element.64.refs_3_), custom_call_target="tpu_custom_call" | custom-call | flops 10000000000 | bytes 10000000 | tf_op jit(solution)/shard_map/motion_again/pallas_call | solution.py:52
  39.8 3.2 %all-to-all-start.1 = ((f32[32,2,128]{2,1,0:T(2,128)}), f32[32,2,128]{2,1,0:T(2,128)S(1)}, u32[]{:S(2)}, u32[]{:S(2)}) async-start(f32[32,2,128]{2,1,0:T(2,128)} %bitcast.10), calls=%async_computation.1 | async-start | bytes 65536 | tf_op jit(solution)/shard_map/all_to_all | solution.py:856
  43.0 0.0 collective-permute-done.10.refs_5_
  43.0 0.0 collective-permute-done.11.refs_6_
  43.1 0.0 collective-permute-done.8.refs_3_
  43.1 0.0 collective-permute-done.9.refs_4_
  43.1 3.4 %stress.1 = (f32[6,512,128]{2,1,0:T(8,128)S(1)}, f32[5,32,128]{2,1,0:T(8,128)S(1)}, f32[5,32,128]{2,1,0:T(8,128)S(1)}, f32[16,512]{1,0:T(8,128)S(1)}) custom-call(f32[3,512,128]{2,1,0:T(8,128)S(1)} %get-tuple-element.65.refs_0_, f32[6,512,128]{2,1,0:T(8,128)} %copy-done.7, f32[5,512,128]{2,1,0:T(8,128)} %copy-done.8, ...), custom_call_target="tpu_custom_call" | custom-call | flops 24999999488 | bytes 25000000 | tf_op jit(solution)/shard_map/stress/pallas_call | solution.py:52
  46.4 1.7 %collective-permute-start.14 = (f32[16,512]{1,0:T(8,128)S(1)}, f32[16,512]{1,0:T(8,128)S(1)}, u32[]{:S(2)}, u32[]{:S(2)}) collective-permute-start(f32[16,512]{1,0:T(8,128)S(1)} %get-tuple-element.75), channel_id=1, source_target_pairs={{0,1},{2,3},{1,0},{3,2},{4,5},{6,7},{5,4},{7,6},{8,9},{10,11},{9,8... | collective-permute-start | bytes 98312 | tf_op jit(solution)/shard_map/ppermute | solution.py:88
  48.1 2.4 %collective-permute-start.15 = (f32[16,512]{1,0:T(8,128)S(1)}, f32[16,512]{1,0:T(8,128)S(1)}, u32[]{:S(2)}, u32[]{:S(2)}) collective-permute-start(f32[16,512]{1,0:T(8,128)S(1)} %get-tuple-element.75), channel_id=1, source_target_pairs={{1,2},{3,0},{2,1},{0,3},{5,6},{7,4},{6,5},{4,7},{9,10},{11,8},{10,... | collective-permute-start | bytes 98312 | tf_op jit(solution)/shard_map/ppermute | solution.py:88
  50.5 0.0 collective-permute-start.12
  50.5 2.5 %collective-permute-start.13 = (f32[5,32,128]{2,1,0:T(8,128)S(1)}, f32[5,32,128]{2,1,0:T(8,128)S(1)}, u32[]{:S(2)}, u32[]{:S(2)}) collective-permute-start(f32[5,32,128]{2,1,0:T(8,128)S(1)} %get-tuple-element.74), channel_id=1, source_target_pairs={{4,8},{12,16},{20,24},{28,0},{8,4},{16,12},{24,20},{0,28},{5,9},{1... | collective-permute-start | bytes 245768 | tf_op jit(solution)/shard_map/ppermute | solution.py:88
  53.0 0.0 all-to-all-done.1
  53.0 1.7 %prepare.1 = (f32[3,16,128]{2,1,0:T(8,128)S(1)}, f32[64,256]{1,0:T(8,128)S(1)}, f32[64,256]{1,0:T(8,128)S(1)}) custom-call(f32[64,128]{1,0:T(8,128)} %motion_again.1.sent_ref, f32[64,128]{1,0:T(8,128)S(1)} %bitcast.17, f32[64,128]{1,0:T(8,128)S(1)} %bitcast.16, f32[64,256]{1,0:T(8,128)S(1)} %get-tuple-element.77.base_ref, ...), custom_call_target="tpu_custom_call" | custom-call | flops 60000002048 | bytes 60000000 | tf_op jit(solution)/shard_map/prepare/pallas_call | solution.py:52
  54.7 0.0 collective-permute-done.14.refs_5_
  54.7 0.0 collective-permute-done.15.refs_6_
  54.8 0.0 collective-permute-done.12.refs_3_
  54.8 0.7 %collective-permute-done.13.refs_4_ = f32[5,32,128]{2,1,0:T(8,128)S(1)} collective-permute-done((f32[5,32,128]{2,1,0:T(8,128)S(1)}, f32[5,32,128]{2,1,0:T(8,128)S(1)}, u32[]{:S(2)}, u32[]{:S(2)}) %collective-permute-start.13) | collective-permute-done | bytes 81952 | tf_op jit(solution)/shard_map/ppermute | solution.py:88
  55.5 5.2 %finish.1 = (f32[3,32,2,8,128]{4,3,2,1,0:T(8,128)}, f32[64,256]{1,0:T(8,128)}, f32[64,256]{1,0:T(8,128)}) custom-call(f32[3,512,128]{2,1,0:T(8,128)S(1)} %get-tuple-element.65.refs_0_, f32[6,512,128]{2,1,0:T(8,128)S(1)} %get-tuple-element.72.refs_1_, f32[3,512,128]{2,1,0:T(8,128)S(1)} %copy-done.10, f32[5,32,128]{2,1,0:T(8,128)S(1)} %collective-permute-done.12.refs_3_, ...), custom_call_target="tpu_custom_call" | custom-call | flops 60000002048 | bytes 60000000 | tf_op jit(solution)/shard_map/finish/pallas_call | solution.py:52
  (5 shorter events, 0.0 us)
Async XLA Ops:
  0.6 2.1 %copy-start = (f32[64,256]{1,0:T(8,128)S(1)}, f32[64,256]{1,0:T(8,128)}, u32[]{:S(2)}) copy-start(f32[64,256]{1,0:T(8,128)} %rate_ref.1) | copy-start | bytes 196612
  0.6 2.1 %copy-start.2 = (f32[64,256]{1,0:T(8,128)S(1)}, f32[64,256]{1,0:T(8,128)}, u32[]{:S(2)}) copy-start(f32[64,256]{1,0:T(8,128)} %coupling_ref.3) | copy-start | bytes 196612
  0.7 2.1 %copy-start.3 = (f32[64,64]{1,0:T(8,128)S(1)}, f32[64,64]{1,0:T(8,128)}, u32[]{:S(2)}) copy-start(f32[64,64]{1,0:T(8,128)} %refs_3_.1) | copy-start | bytes 49156
  0.7 2.1 %copy-start.4 = (s32[64]{0:T(128)S(1)}, s32[64]{0:T(128)}, u32[]{:S(2)}) copy-start(s32[64]{0:T(128)} %param.25) | copy-start | bytes 772
  0.7 2.1 %copy-start.5 = (s32[64,1]{0,1:T(1,128)S(1)}, s32[64,1]{0,1:T(1,128)}, u32[]{:S(2)}) copy-start(s32[64,1]{0,1:T(1,128)} %param.24) | copy-start | bytes 772
  0.7 2.1 %copy-start.6 = (s32[64]{0:T(128)S(1)}, s32[64]{0:T(128)}, u32[]{:S(2)}) copy-start(s32[64]{0:T(128)} %param.23) | copy-start | bytes 772
  3.8 14.7 %all-to-all-start = ((f32[32,2,128]{2,1,0:T(2,128)}), f32[32,2,128]{2,1,0:T(2,128)S(1)}, u32[]{:S(2)}, u32[]{:S(2)}) async-start(f32[32,2,128]{2,1,0:T(2,128)} %bitcast.6), calls=%async_computation | async-start | bytes 65536 | tf_op jit(solution)/shard_map/all_to_all | solution.py:856
  11.1 9.8 %collective-permute-start.2 = (f32[16,512]{1,0:T(8,128)S(1)}, f32[16,512]{1,0:T(8,128)S(1)}, u32[]{:S(2)}, u32[]{:S(2)}) collective-permute-start(f32[16,512]{1,0:T(8,128)S(1)} %get-tuple-element.51), channel_id=1, source_target_pairs={{0,1},{2,3},{1,0},{3,2},{4,5},{6,7},{5,4},{7,6},{8,9},{10,11},{9,8... | collective-permute-start | bytes 98312 | tf_op jit(solution)/shard_map/ppermute | solution.py:88
  13.0 8.0 %collective-permute-start.3 = (f32[16,512]{1,0:T(8,128)S(1)}, f32[16,512]{1,0:T(8,128)S(1)}, u32[]{:S(2)}, u32[]{:S(2)}) collective-permute-start(f32[16,512]{1,0:T(8,128)S(1)} %get-tuple-element.51), channel_id=1, source_target_pairs={{1,2},{3,0},{2,1},{0,3},{5,6},{7,4},{6,5},{4,7},{9,10},{11,8},{10,... | collective-permute-start | bytes 98312 | tf_op jit(solution)/shard_map/ppermute | solution.py:88
  15.3 5.7 %collective-permute-start = (f32[7,32,128]{2,1,0:T(8,128)S(1)}, f32[7,32,128]{2,1,0:T(8,128)S(1)}, u32[]{:S(2)}, u32[]{:S(2)}) collective-permute-start(f32[7,32,128]{2,1,0:T(8,128)S(1)} %get-tuple-element.49), channel_id=1, source_target_pairs={{0,4},{8,12},{16,20},{24,28},{4,0},{12,8},{20,16},{28,24},{1,5},{9... | collective-permute-start | bytes 344072 | tf_op jit(solution)/shard_map/ppermute | solution.py:88
  15.3 5.7 %collective-permute-start.1 = (f32[7,32,128]{2,1,0:T(8,128)S(1)}, f32[7,32,128]{2,1,0:T(8,128)S(1)}, u32[]{:S(2)}, u32[]{:S(2)}) collective-permute-start(f32[7,32,128]{2,1,0:T(8,128)S(1)} %get-tuple-element.50), channel_id=1, source_target_pairs={{4,8},{12,16},{20,24},{28,0},{8,4},{16,12},{24,20},{0,28},{5,9},{1... | collective-permute-start | bytes 344072 | tf_op jit(solution)/shard_map/ppermute | solution.py:88
  21.0 7.1 %copy-start.1 = (f32[64,256]{1,0:T(8,128)S(1)}, f32[64,256]{1,0:T(8,128)}, u32[]{:S(2)}) copy-start(f32[64,256]{1,0:T(8,128)} %raw_ref.1) | copy-start | bytes 196612
  24.9 6.4 %copy-start.8 = (f32[5,512,128]{2,1,0:T(8,128)}, f32[5,512,128]{2,1,0:T(8,128)S(1)}, u32[]{:S(2)}) copy-start(f32[5,512,128]{2,1,0:T(8,128)S(1)} %get-tuple-element.67.refs_2_) | copy-start | bytes 3932164
  24.9 7.1 %copy-start.7 = (f32[6,512,128]{2,1,0:T(8,128)}, f32[6,512,128]{2,1,0:T(8,128)S(1)}, u32[]{:S(2)}) copy-start(f32[6,512,128]{2,1,0:T(8,128)S(1)} %get-tuple-element.52.refs_1_) | copy-start | bytes 4718596
  24.9 7.1 %copy-start.9 = (f32[3,512,128]{2,1,0:T(8,128)}, f32[3,512,128]{2,1,0:T(8,128)S(1)}, u32[]{:S(2)}) copy-start(f32[3,512,128]{2,1,0:T(8,128)S(1)} %get-tuple-element.53.refs_2_) | copy-start | bytes 2359300
  24.9 6.3 %collective-permute-start.6 = (f32[16,512]{1,0:T(8,128)S(1)}, f32[16,512]{1,0:T(8,128)S(1)}, u32[]{:S(2)}, u32[]{:S(2)}) collective-permute-start(f32[16,512]{1,0:T(8,128)S(1)} %get-tuple-element.56), channel_id=1, source_target_pairs={{0,1},{2,3},{1,0},{3,2},{4,5},{6,7},{5,4},{7,6},{8,9},{10,11},{9,8... | collective-permute-start | bytes 98312 | tf_op jit(solution)/shard_map/ppermute | solution.py:88
  25.5 5.7 %collective-permute-start.7 = (f32[16,512]{1,0:T(8,128)S(1)}, f32[16,512]{1,0:T(8,128)S(1)}, u32[]{:S(2)}, u32[]{:S(2)}) collective-permute-start(f32[16,512]{1,0:T(8,128)S(1)} %get-tuple-element.56), channel_id=1, source_target_pairs={{1,2},{3,0},{2,1},{0,3},{5,6},{7,4},{6,5},{4,7},{9,10},{11,8},{10,... | collective-permute-start | bytes 98312 | tf_op jit(solution)/shard_map/ppermute | solution.py:88
  26.9 4.3 %collective-permute-start.4 = (f32[5,32,128]{2,1,0:T(8,128)S(1)}, f32[5,32,128]{2,1,0:T(8,128)S(1)}, u32[]{:S(2)}, u32[]{:S(2)}) collective-permute-start(f32[5,32,128]{2,1,0:T(8,128)S(1)} %get-tuple-element.54), channel_id=1, source_target_pairs={{0,4},{8,12},{16,20},{24,28},{4,0},{12,8},{20,16},{28,24},{1,5},{9... | collective-permute-start | bytes 245768 | tf_op jit(solution)/shard_map/ppermute | solution.py:88
  26.9 5.0 %collective-permute-start.5 = (f32[5,32,128]{2,1,0:T(8,128)S(1)}, f32[5,32,128]{2,1,0:T(8,128)S(1)}, u32[]{:S(2)}, u32[]{:S(2)}) collective-permute-start(f32[5,32,128]{2,1,0:T(8,128)S(1)} %get-tuple-element.55), channel_id=1, source_target_pairs={{4,8},{12,16},{20,24},{28,0},{8,4},{16,12},{24,20},{0,28},{5,9},{1... | collective-permute-start | bytes 245768 | tf_op jit(solution)/shard_map/ppermute | solution.py:88
  34.3 8.8 %collective-permute-start.10 = (f32[16,512]{1,0:T(8,128)S(1)}, f32[16,512]{1,0:T(8,128)S(1)}, u32[]{:S(2)}, u32[]{:S(2)}) collective-permute-start(f32[16,512]{1,0:T(8,128)S(1)} %get-tuple-element.70), channel_id=1, source_target_pairs={{0,1},{2,3},{1,0},{3,2},{4,5},{6,7},{5,4},{7,6},{8,9},{10,11},{9,8... | collective-permute-start | bytes 98312 | tf_op jit(solution)/shard_map/ppermute | solution.py:88
  34.7 8.3 %collective-permute-start.11 = (f32[16,512]{1,0:T(8,128)S(1)}, f32[16,512]{1,0:T(8,128)S(1)}, u32[]{:S(2)}, u32[]{:S(2)}) collective-permute-start(f32[16,512]{1,0:T(8,128)S(1)} %get-tuple-element.70), channel_id=1, source_target_pairs={{1,2},{3,0},{2,1},{0,3},{5,6},{7,4},{6,5},{4,7},{9,10},{11,8},{10,... | collective-permute-start | bytes 98312 | tf_op jit(solution)/shard_map/ppermute | solution.py:88
  37.1 6.0 %collective-permute-start.8 = (f32[5,32,128]{2,1,0:T(8,128)S(1)}, f32[5,32,128]{2,1,0:T(8,128)S(1)}, u32[]{:S(2)}, u32[]{:S(2)}) collective-permute-start(f32[5,32,128]{2,1,0:T(8,128)S(1)} %get-tuple-element.68), channel_id=1, source_target_pairs={{0,4},{8,12},{16,20},{24,28},{4,0},{12,8},{20,16},{28,24},{1,5},{9... | collective-permute-start | bytes 245768 | tf_op jit(solution)/shard_map/ppermute | solution.py:88
  37.1 6.0 %collective-permute-start.9 = (f32[5,32,128]{2,1,0:T(8,128)S(1)}, f32[5,32,128]{2,1,0:T(8,128)S(1)}, u32[]{:S(2)}, u32[]{:S(2)}) collective-permute-start(f32[5,32,128]{2,1,0:T(8,128)S(1)} %get-tuple-element.69), channel_id=1, source_target_pairs={{4,8},{12,16},{20,24},{28,0},{8,4},{16,12},{24,20},{0,28},{5,9},{1... | collective-permute-start | bytes 245768 | tf_op jit(solution)/shard_map/ppermute | solution.py:88
  39.8 13.1 %all-to-all-start.1 = ((f32[32,2,128]{2,1,0:T(2,128)}), f32[32,2,128]{2,1,0:T(2,128)S(1)}, u32[]{:S(2)}, u32[]{:S(2)}) async-start(f32[32,2,128]{2,1,0:T(2,128)} %bitcast.10), calls=%async_computation.1 | async-start | bytes 65536 | tf_op jit(solution)/shard_map/all_to_all | solution.py:856
  46.4 8.3 %collective-permute-start.14 = (f32[16,512]{1,0:T(8,128)S(1)}, f32[16,512]{1,0:T(8,128)S(1)}, u32[]{:S(2)}, u32[]{:S(2)}) collective-permute-start(f32[16,512]{1,0:T(8,128)S(1)} %get-tuple-element.75), channel_id=1, source_target_pairs={{0,1},{2,3},{1,0},{3,2},{4,5},{6,7},{5,4},{7,6},{8,9},{10,11},{9,8... | collective-permute-start | bytes 98312 | tf_op jit(solution)/shard_map/ppermute | solution.py:88
  48.1 6.6 %collective-permute-start.15 = (f32[16,512]{1,0:T(8,128)S(1)}, f32[16,512]{1,0:T(8,128)S(1)}, u32[]{:S(2)}, u32[]{:S(2)}) collective-permute-start(f32[16,512]{1,0:T(8,128)S(1)} %get-tuple-element.75), channel_id=1, source_target_pairs={{1,2},{3,0},{2,1},{0,3},{5,6},{7,4},{6,5},{4,7},{9,10},{11,8},{10,... | collective-permute-start | bytes 98312 | tf_op jit(solution)/shard_map/ppermute | solution.py:88
  50.5 4.3 %collective-permute-start.12 = (f32[5,32,128]{2,1,0:T(8,128)S(1)}, f32[5,32,128]{2,1,0:T(8,128)S(1)}, u32[]{:S(2)}, u32[]{:S(2)}) collective-permute-start(f32[5,32,128]{2,1,0:T(8,128)S(1)} %get-tuple-element.73), channel_id=1, source_target_pairs={{0,4},{8,12},{16,20},{24,28},{4,0},{12,8},{20,16},{28,24},{1,5},{9... | collective-permute-start | bytes 245768 | tf_op jit(solution)/shard_map/ppermute | solution.py:88
  50.5 5.0 %collective-permute-start.13 = (f32[5,32,128]{2,1,0:T(8,128)S(1)}, f32[5,32,128]{2,1,0:T(8,128)S(1)}, u32[]{:S(2)}, u32[]{:S(2)}) collective-permute-start(f32[5,32,128]{2,1,0:T(8,128)S(1)} %get-tuple-element.74), channel_id=1, source_target_pairs={{4,8},{12,16},{20,24},{28,0},{8,4},{16,12},{24,20},{0,28},{5,9},{1... | collective-permute-start | bytes 245768 | tf_op jit(solution)/shard_map/ppermute | solution.py:88
  53.0 2.5 %copy-start.10 = (f32[3,512,128]{2,1,0:T(8,128)S(1)}, f32[3,512,128]{2,1,0:T(8,128)}, u32[]{:S(2)}) copy-start(f32[3,512,128]{2,1,0:T(8,128)} %copy-done.9) | copy-start | bytes 2359300

commit v4 on v3

--- a/solution.py
+++ b/solution.py
@@ -157,16 +157,38 @@
         out_ref[cut, :] = whole.T
 
 
-def slopes(f, ghost, forward):
-    lane = lanes_of(f)
-    last = f.shape[-1] - 1
-    up1 = roll(jnp.where(lane == 0, ghost, f), -1)
-    down1 = roll(jnp.where(lane == last, ghost, f), 1)
-    if forward:
-        up2 = roll(jnp.where(lane <= 1, ghost, f), -2)
-        return near * (up1 - f) - far * (up2 - down1)
-    down2 = roll(jnp.where(lane >= last - 1, ghost, f), 2)
-    return near * (f - down1) - far * (up1 - down2)
+def bands(forward, amount):
+    row = lax.broadcasted_iota(jnp.int32, (256, 128), 0)
+    lane = row - 128
+    beyond = jnp.where(lane < amount, lane - amount, 128 + lane - amount)
+    shift = jnp.where(row < 128, row, beyond) - lax.broadcasted_iota(jnp.int32, (256, 128), 1)
+    first, last = (amount - 1, amount + 1) if forward else (amount - 2, amount)
+    valid = (row < 128) | ((lane >= first) & (lane <= last))
+    value = jnp.zeros((256, 128), f32)
+    at = 0 if forward else -1
+    for step, entry in ((at + 1, 27.0), (at, -27.0), (at + 2, -1.0), (at - 1, 1.0)):
+        value = jnp.where(shift == step, entry, value)
+    return jnp.where(valid, value, 0.0).astype(jnp.bfloat16)
+
+
+def parted(value):
+    large = value.astype(jnp.bfloat16)
+    return large, (value - large.astype(f32)).astype(jnp.bfloat16)
+
+
+def slopes(fields, cols, out_ref):
+    matrices = [bands(forward, amount) for _, forward, amount in fields]
+    size = 256
+    for begin in range(0, cols.shape[0], size):
+        cut = slice(begin, begin + size)
+        ghost = parted(cols[cut, :])
+        for i, (read, _, _) in enumerate(fields):
+            total = None
+            for own, other in zip(parted(read(cut)), ghost):
+                both = jnp.concatenate([own, other], axis=1)
+                part = jnp.dot(both, matrices[i], preferred_element_type=f32)
+                total = part if total is None else total + part
+            out_ref[i, cut, :] = total * (1.0 / 24.0)
 
 
 def across(ext, c, x, forward, layers):
@@ -306,25 +328,28 @@
         ext[c, x, PAD : PAD + layers, :] = jnp.where(ok, at(row), 0.0)
 
 
-def stresses(layers, v_ref, old, ready, mat_ref, below, above, cols, out_ref, refs, ext, pack):
+def stresses(layers, v_ref, old, ready, mat_ref, below, above, cols, out_ref, refs, ext, pack, slope):
     even_ref, odd_ref, col_ref = refs
     size_x = v_ref.shape[1] // layers
     west_ok, east_ok, _, _ = place()
     for c in range(3):
         fill(ext, c, v_ref, c, size_x, layers)
-    inner = slice(PAD, PAD + layers)
     extend(ext, ((0, 0, 0), (1, 0, 1), (2, 1, 1), (3, 2, 1)), below, west_ok, layers)
     over = size_x + 2
     rows = ((0, 0, over), (1, 1, over), (2, 1, over + 1), (3, 2, over), (4, 2, over + 1))
     extend(ext, rows, above, east_ok, layers)
 
+    fields = (
+        (lambda cut: v_ref[1, cut, :], False, 5),
+        (lambda cut: v_ref[0, cut, :], True, 1),
+        (lambda cut: v_ref[2, cut, :], True, 7),
+    )
+    slopes(fields, cols, slope)
+
     def step(x, carry):
         cut = pl.ds(pl.multiple_of(x * layers, layers), layers)
-        ghost = cols[cut, :]
-        vx, vy, vz = [ext[c, x + 2, inner, :] for c in range(3)]
-        gx, gy, gz = roll(ghost, -1), roll(ghost, -5), roll(ghost, -7)
         dx = across(ext, 0, x, False, layers)
-        dy = slopes(vy, gy, False)
+        dy = slope[0, cut, :]
         dz = down(ext, 2, x, False, layers)
         both = mat_ref[0, cut, :] * (dx + dy + dz)
         twice = mat_ref[1, cut, :]
@@ -332,13 +357,13 @@
         yy = old(1, x, cut) + (both + twice * dy)
         zz = old(2, x, cut) + (both + twice * dz)
         xy = old(3, x, cut) + mat_ref[2, cut, :] * (
-            slopes(vx, gx, True) + across(ext, 1, x, True, layers)
+            slope[1, cut, :] + across(ext, 1, x, True, layers)
         )
         xz = old(4, x, cut) + mat_ref[3, cut, :] * (
             down(ext, 0, x, True, layers) + across(ext, 2, x, True, layers)
         )
         yz = old(5, x, cut) + mat_ref[4, cut, :] * (
-            down(ext, 1, x, True, layers) + slopes(vz, gz, True)
+            down(ext, 1, x, True, layers) + slope[2, cut, :]
         )
         for c, value in enumerate((xx, yy, zz, xy, xz, yz)):
             out_ref[c, cut, :] = value
@@ -384,6 +409,7 @@
     ext,
     cols,
     pack,
+    slope,
     sems,
 ):
     half = stiff_ref.shape[0]
@@ -401,7 +427,7 @@
         return s_ref[c, cut, :]
 
     refs = (even_ref, odd_ref, col_ref)
-    stresses(layers, v_ref, old, ready, mat_ref, below, above, cols, out_ref, refs, ext, pack)
+    stresses(layers, v_ref, old, ready, mat_ref, below, above, cols, out_ref, refs, ext, pack, slope)
     copies[0].wait()
 
 
@@ -423,6 +449,7 @@
     ext,
     cols,
     pack,
+    slope,
     sems,
 ):
     strips = v_ref.shape[1] // layers // STRIP
@@ -444,10 +471,10 @@
         return s_ref[c, cut, :]
 
     refs = (even_ref, odd_ref, col_ref)
-    stresses(layers, v_ref, old, ready, mat_ref, below, above, cols, out_ref, refs, ext, pack)
-
-
-def moving(layers, v_ref, s_ref, buoy_ref, halo, push_ref, ext, cols):
+    stresses(layers, v_ref, old, ready, mat_ref, below, above, cols, out_ref, refs, ext, pack, slope)
+
+
+def moving(layers, v_ref, s_ref, buoy_ref, halo, push_ref, ext, cols, slope):
     x_even, x_odd, y_even, y_odd = halo
     size_x = v_ref.shape[1] // layers
     west_ok, east_ok, south_ok, north_ok = place()
@@ -455,20 +482,23 @@
     receive_columns(y_even, y_odd, (0, 3, 4, 6, 7), south_ok, north_ok, cols)
     for c, src in enumerate((0, 3, 4, 5, 2)):
         fill(ext, c, s_ref, src, size_x, layers)
-    inner = slice(PAD, PAD + layers)
     rows = ((0, 0, 1), (1, 1, 0), (2, 1, 1), (3, 2, 0), (4, 2, 1))
     extend(ext, rows, below, west_ok, layers)
     over = size_x + 2
     extend(ext, ((0, 0, over), (1, 0, over + 1), (2, 1, over), (3, 2, over)), above, east_ok, layers)
 
+    fields = (
+        (lambda cut: s_ref[3, cut, :], False, 5),
+        (lambda cut: s_ref[1, cut, :], True, 1),
+        (lambda cut: s_ref[5, cut, :], False, 8),
+    )
+    slopes(fields, cols, slope)
+
     def fresh(x, cut):
-        ghost = cols[cut, :]
-        yy, xy, yz = s_ref[1, cut, :], ext[1, x + 2, inner, :], ext[3, x + 2, inner, :]
-        gyy, gxy, gyz = roll(ghost, -1), roll(ghost, -5), roll(ghost, -8)
-        ax = across(ext, 0, x, True, layers) + slopes(xy, gxy, False) + down(ext, 2, x, False, layers)
-        ay = across(ext, 1, x, False, layers) + slopes(yy, gyy, True) + down(ext, 3, x, False, layers)
-        az = across(ext, 2, x, False, layers) + slopes(yz, gyz, False) + down(ext, 4, x, True, layers)
-        layer = lax.broadcasted_iota(jnp.int32, yy.shape, 0)
+        ax = across(ext, 0, x, True, layers) + slope[0, cut, :] + down(ext, 2, x, False, layers)
+        ay = across(ext, 1, x, False, layers) + slope[1, cut, :] + down(ext, 3, x, False, layers)
+        az = across(ext, 2, x, False, layers) + slope[2, cut, :] + down(ext, 4, x, True, layers)
+        layer = lax.broadcasted_iota(jnp.int32, ax.shape, 0)
         result = []
         for c, accel in enumerate((ax, ay, az)):
             pushed = jnp.where(layer == 0, push_ref[c, pl.ds(x, 1), :], 0.0)
@@ -495,10 +525,11 @@
     ext,
     cols,
     pack,
+    slope,
 ):
     size_x = v_ref.shape[1] // layers
     halo = (x_even, x_odd, y_even, y_odd)
-    fresh = moving(layers, v_ref, s_ref, buoy_ref, halo, push_ref, ext, cols)
+    fresh = moving(layers, v_ref, s_ref, buoy_ref, halo, push_ref, ext, cols, slope)
 
     def step(x, carry):
         cut = pl.ds(pl.multiple_of(x * layers, layers), layers)
@@ -789,6 +820,7 @@
     out_ref,
     ext,
     cols,
+    slope,
     pull,
     stiff_ref,
     sems,
@@ -797,7 +829,7 @@
     fetch_strips(stiff_hbm, 0, stiff_ref, sems)
     size_x = v_ref.shape[1] // layers
     halo = (x_even, x_odd, y_even, y_odd)
-    fresh = moving(layers, v_ref, s_ref, buoy_ref, halo, push_ref, ext, cols)
+    fresh = moving(layers, v_ref, s_ref, buoy_ref, halo, push_ref, ext, cols, slope)
     strips = sems.shape[0]
     share = half.shape[0] // strips
     batch = size_x // strips
@@ -950,6 +982,7 @@
             ext,
             field,
             field,
+            vm(3, cells, size_y),
             dma((1,)),
         ],
     )
@@ -980,7 +1013,7 @@
         "velocity",
         (near_by(3, cells, size_y), *payload),
         (vt, st, buoys, *halo, push),
-        [bulk, field, field],
+        [bulk, field, field, vm(3, cells, size_y)],
     )
     halo = exchange(one, two, col)
     (sent,) = call(
@@ -1003,6 +1036,7 @@
             ext,
             field,
             field,
+            vm(3, cells, size_y),
             dma((2 * strips,)),
         ],
     )
@@ -1038,6 +1072,7 @@
             vm(tiles, 3, layers, TILE, size_y),
             bulk,
             field,
+            vm(3, cells, size_y),
             vm(number, width),
             pltpu.VMEM(stiffness.shape, stiffness.dtype),
             dma((chunks,)),

time: 61.2 us -> 58.1 us (0.949)
  Pallas kernels: 25.9 us -> 23 us
    pallas_call x11, Pallas kernels: 25.9 us -> 23 us  [call(): pl.pallas_call(kernel, name=name, out_shape=outs, in_specs=specs, out_spe...]
  transfers between devices with their start and end apart: 18 -> 18, of which waited for: 3 -> 3; matrix products, arithmetic and copies ran while one was open for 0% -> 0% of each run, Pallas kernels for 19% -> 18%
where the time goes in v4:
time: 58.1 us; the launch traced here: 57.8 us
  starting transfers between devices  31.8 us (55%)
  Pallas kernels  23 us (40%)
  waiting for transfers between devices  2.03 us (3%)
  between operations  0.94 us (2%)
    pallas_call x11, Pallas kernels, call(): pl.pallas_call(kernel, name=name, out_shape=outs, in_specs=specs, out_spe...  23 us
    ppermute x16, starting transfers between devices, swap(): return lax.ppermute(block, axis, pairs + [(b, a) for a, b in pairs])  21.5 us
    all_to_all x2, starting transfers between devices, trade(): lax.all_to_all(blocks, ('gx', 'gy'), split_axis=0, concat_axis=0, tiled=T...  10.3 us
    ppermute x16, waiting for transfers between devices, swap(): return lax.ppermute(block, axis, pairs + [(b, a) for a, b in pairs])  1.37 us
  transfers between devices with their start and end apart: 18, of which 3 were waited for; matrix products, arithmetic and copies ran while one was open for 0% of the time, Pallas kernels for 18%

profile of v4, /device:TPU:0, one launch (start us, length us, event | category | flops | bytes accessed | tf_op | source)
XLA Modules:
  0.0 57.8 jit_solution(9890894977908415551)
XLA Ops:
  0.6 0.0 copy-start
  0.6 0.0 copy-start.2
  0.7 0.0 copy-start.3
  0.7 0.0 copy-start.4
  0.7 0.0 copy-start.5
  0.7 0.0 copy-start.6
  0.7 2.1 %first.1 = (f32[3,512,128]{2,1,0:T(8,128)S(1)}, f32[512,128]{1,0:T(8,128)S(1)}, f32[512,128]{1,0:T(8,128)S(1)}, f32[7,32,128]{2,1,0:T(8,128)S(1)}, f32[7,32,128]{2,1,0:T(8,128)S(1)}, /*index=5*/f32[16,512]{1,0:T(8,128)S(1)}) custom-call(f32[3,512,128]{2,1,0:T(8,128)} %bitcast.27, f32[512,128]{1,0:T(8,128)} %bitcast.28, f32[512,128]{1,0:T(8,128)} %bitcast.29), custom_call_target="tpu_custom_call" | custom-call | flops 30000001024 | bytes 30000000 | tf_op jit(solution)/shard_map/first/pallas_call | solution.py:52
  2.8 0.0 copy-done
  2.8 0.0 copy-done.2
  2.8 0.0 copy-done.3
  2.8 0.0 copy-done.4
  2.8 0.0 copy-done.5
  2.8 0.0 copy-done.6
  2.8 1.0 %table.1 = f32[64,128]{1,0:T(8,128)} custom-call(f32[512,128]{1,0:T(8,128)S(1)} %get-tuple-element.46.refs_0_.refs_2_, f32[64,256]{1,0:T(8,128)S(1)} %copy-done, f32[64,256]{1,0:T(8,128)S(1)} %copy-done.2, f32[64,64]{1,0:T(8,128)S(1)} %copy-done.3, s32[1,64]{1,0:T(1,128)S(1)} %bitcast.22, s32[1,64]{1,0:T(1,128)S(1)} %bitcast.19, s32[1,64]{1,0:T(1,128)S(1)} %bitcast.18), custom_call_target="tpu_custom_call" | custom-call | flops 60000002048 | bytes 60000000 | tf_op jit(solution)/shard_map/table/pallas_call | solution.py:52
  3.8 7.3 %all-to-all-start = ((f32[32,2,128]{2,1,0:T(2,128)}), f32[32,2,128]{2,1,0:T(2,128)S(1)}, u32[]{:S(2)}, u32[]{:S(2)}) async-start(f32[32,2,128]{2,1,0:T(2,128)} %bitcast.6), calls=%async_computation | async-start | bytes 65536 | tf_op jit(solution)/shard_map/all_to_all | solution.py:888
  11.1 1.8 %collective-permute-start.2 = (f32[16,512]{1,0:T(8,128)S(1)}, f32[16,512]{1,0:T(8,128)S(1)}, u32[]{:S(2)}, u32[]{:S(2)}) collective-permute-start(f32[16,512]{1,0:T(8,128)S(1)} %get-tuple-element.51), channel_id=1, source_target_pairs={{0,1},{2,3},{1,0},{3,2},{4,5},{6,7},{5,4},{7,6},{8,9},{10,11},{9,8... | collective-permute-start | bytes 98312 | tf_op jit(solution)/shard_map/ppermute | solution.py:88
  13.0 2.4 %collective-permute-start.3 = (f32[16,512]{1,0:T(8,128)S(1)}, f32[16,512]{1,0:T(8,128)S(1)}, u32[]{:S(2)}, u32[]{:S(2)}) collective-permute-start(f32[16,512]{1,0:T(8,128)S(1)} %get-tuple-element.51), channel_id=1, source_target_pairs={{1,2},{3,0},{2,1},{0,3},{5,6},{7,4},{6,5},{4,7},{9,10},{11,8},{10,... | collective-permute-start | bytes 98312 | tf_op jit(solution)/shard_map/ppermute | solution.py:88
  15.3 0.0 collective-permute-start
  15.3 2.5 %collective-permute-start.1 = (f32[7,32,128]{2,1,0:T(8,128)S(1)}, f32[7,32,128]{2,1,0:T(8,128)S(1)}, u32[]{:S(2)}, u32[]{:S(2)}) collective-permute-start(f32[7,32,128]{2,1,0:T(8,128)S(1)} %get-tuple-element.50), channel_id=1, source_target_pairs={{4,8},{12,16},{20,24},{28,0},{8,4},{16,12},{24,20},{0,28},{5,9},{1... | collective-permute-start | bytes 344072 | tf_op jit(solution)/shard_map/ppermute | solution.py:88
  17.8 0.7 %all-to-all-done = f32[32,2,128]{2,1,0:T(2,128)S(1)} async-done(((f32[32,2,128]{2,1,0:T(2,128)}), f32[32,2,128]{2,1,0:T(2,128)S(1)}, u32[]{:S(2)}, u32[]{:S(2)}) %all-to-all-start) | async-done | bytes 32800 | tf_op jit(solution)/shard_map/all_to_all | solution.py:888
  18.5 1.6 %load.1 = (f32[6,512,128]{2,1,0:T(8,128)S(1)}, f32[512,128]{1,0:T(8,128)S(1)}) custom-call(f32[64,128]{1,0:T(8,128)S(1)} %bitcast.13, f32[6,512,128]{2,1,0:T(8,128)} %bitcast.26, f32[512,128]{1,0:T(8,128)} %bitcast.30), custom_call_target="tpu_custom_call" | custom-call | flops 20000000000 | bytes 20000000 | tf_op jit(solution)/shard_map/load/pallas_call | solution.py:52
  20.1 0.8 %surface.1 = (f32[16,64,128]{2,1,0:T(8,128)S(1)}, f32[64,128]{1,0:T(8,128)S(1)}, f32[3,16,128]{2,1,0:T(8,128)S(1)}) custom-call(f32[64,128]{1,0:T(8,128)S(1)} %bitcast.14, f32[3,512,128]{2,1,0:T(8,128)S(1)} %get-tuple-element.44.refs_0_.refs_1_), custom_call_target="tpu_custom_call" | custom-call | flops 10000000000 | bytes 10000000 | tf_op jit(solution)/shard_map/surface/pallas_call | solution.py:52
  21.0 0.0 collective-permute-done.2.refs_8_
  21.0 0.0 collective-permute-done.3.refs_9_
  21.0 0.0 collective-permute-done.refs_6_
  21.0 0.0 collective-permute-done.1.refs_7_
  21.0 2.2 %begin.1 = (f32[6,512,128]{2,1,0:T(8,128)S(1)}, f32[5,32,128]{2,1,0:T(8,128)S(1)}, f32[5,32,128]{2,1,0:T(8,128)S(1)}, f32[16,512]{1,0:T(8,128)S(1)}, f32[5,512,1...) custom-call(f32[3,512,128]{2,1,0:T(8,128)S(1)} %get-tuple-element.44.refs_0_.refs_1_, ...), custom_call_target="tpu_custom_call" | custom-call | flops 40000000000 | bytes 40000000 | tf_op jit(solution)/shard_map/begin/pallas_call | solution.py:52
  23.3 0.0 copy-start.8
  23.3 0.0 copy-start.7
  23.3 0.0 copy-start.9
  23.3 0.6 %collective-permute-start.6 = (f32[16,512]{1,0:T(8,128)S(1)}, f32[16,512]{1,0:T(8,128)S(1)}, u32[]{:S(2)}, u32[]{:S(2)}) collective-permute-start(f32[16,512]{1,0:T(8,128)S(1)} %get-tuple-element.56), channel_id=1, source_target_pairs={{0,1},{2,3},{1,0},{3,2},{4,5},{6,7},{5,4},{7,6},{8,9},{10,11},{9,8... | collective-permute-start | bytes 98312 | tf_op jit(solution)/shard_map/ppermute | solution.py:88
  24.0 1.4 %collective-permute-start.7 = (f32[16,512]{1,0:T(8,128)S(1)}, f32[16,512]{1,0:T(8,128)S(1)}, u32[]{:S(2)}, u32[]{:S(2)}) collective-permute-start(f32[16,512]{1,0:T(8,128)S(1)} %get-tuple-element.56), channel_id=1, source_target_pairs={{1,2},{3,0},{2,1},{0,3},{5,6},{7,4},{6,5},{4,7},{9,10},{11,8},{10,... | collective-permute-start | bytes 98312 | tf_op jit(solution)/shard_map/ppermute | solution.py:88
  25.3 0.0 collective-permute-start.4
  25.3 1.2 %collective-permute-start.5 = (f32[5,32,128]{2,1,0:T(8,128)S(1)}, f32[5,32,128]{2,1,0:T(8,128)S(1)}, u32[]{:S(2)}, u32[]{:S(2)}) collective-permute-start(f32[5,32,128]{2,1,0:T(8,128)S(1)} %get-tuple-element.55), channel_id=1, source_target_pairs={{4,8},{12,16},{20,24},{28,0},{8,4},{16,12},{24,20},{0,28},{5,9},{1... | collective-permute-start | bytes 245768 | tf_op jit(solution)/shard_map/ppermute | solution.py:88
  26.6 3.1 %pull.1 = (f32[64,256]{1,0:T(8,128)S(1)}, f32[64,256]{1,0:T(8,128)S(1)}, f32[64,128]{1,0:T(8,128)S(1)}) custom-call(bf16[32,256,256]{2,1,0:T(8,128)(2,1)S(1)} %get-tuple-element.58.stiff_ref, bf16[64,256,256]{2,1,0:T(8,128)(2,1)} %refs_11_.1, f32[64,256]{1,0:T(8,128)S(1)} %copy-done.1, f32[64,256]{1,0:T(8,128)S(1)} %copy-done, f32[64,256]{1,0:T(8,128)S(1)} %copy-done.2, ...), custom_call_target="tpu_custom_call" | custom-call | flops 30000001024 | bytes 30000000 | tf_op jit(solution)/shard_map/pull/pallas_call | solution.py:52
  29.6 0.0 copy-done.8
  29.6 0.0 collective-permute-done.6.refs_5_
  29.7 0.0 collective-permute-done.7.refs_6_
  29.7 0.0 collective-permute-done.4.refs_3_
  29.7 0.6 %collective-permute-done.5.refs_4_ = f32[5,32,128]{2,1,0:T(8,128)S(1)} collective-permute-done((f32[5,32,128]{2,1,0:T(8,128)S(1)}, f32[5,32,128]{2,1,0:T(8,128)S(1)}, u32[]{:S(2)}, u32[]{:S(2)}) %collective-permute-start.5) | collective-permute-done | bytes 81952 | tf_op jit(solution)/shard_map/ppermute | solution.py:88
  30.3 1.5 %velocity.1 = (f32[3,512,128]{2,1,0:T(8,128)S(1)}, f32[5,32,128]{2,1,0:T(8,128)S(1)}, f32[5,32,128]{2,1,0:T(8,128)S(1)}, f32[16,512]{1,0:T(8,128)S(1)}) custom-call(f32[3,512,128]{2,1,0:T(8,128)S(1)} %get-tuple-element.44.refs_0_.refs_1_, f32[6,512,128]{2,1,0:T(8,128)S(1)} %get-tuple-element.52.refs_1_, f32[3,512,128]{2,1,0:T(8,128)S(1)} %get-tuple-element.53.refs_2_, ...), custom_call_target="tpu_custom_call" | custom-call | flops 24999999488 | bytes 25000000 | tf_op jit(solution)/shard_map/velocity/pallas_call | solution.py:52
  31.8 0.5 collective-permute-start.10
  32.3 2.4 %collective-permute-start.11 = (f32[16,512]{1,0:T(8,128)S(1)}, f32[16,512]{1,0:T(8,128)S(1)}, u32[]{:S(2)}, u32[]{:S(2)}) collective-permute-start(f32[16,512]{1,0:T(8,128)S(1)} %get-tuple-element.70), channel_id=1, source_target_pairs={{1,2},{3,0},{2,1},{0,3},{5,6},{7,4},{6,5},{4,7},{9,10},{11,8},{10,... | collective-permute-start | bytes 98312 | tf_op jit(solution)/shard_map/ppermute | solution.py:88
  34.7 0.0 collective-permute-start.8
  34.7 1.9 %collective-permute-start.9 = (f32[5,32,128]{2,1,0:T(8,128)S(1)}, f32[5,32,128]{2,1,0:T(8,128)S(1)}, u32[]{:S(2)}, u32[]{:S(2)}) collective-permute-start(f32[5,32,128]{2,1,0:T(8,128)S(1)} %get-tuple-element.69), channel_id=1, source_target_pairs={{4,8},{12,16},{20,24},{28,0},{8,4},{16,12},{24,20},{0,28},{5,9},{1... | collective-permute-start | bytes 245768 | tf_op jit(solution)/shard_map/ppermute | solution.py:88
  36.6 0.8 %motion_again.1.sent_ref = f32[64,128]{1,0:T(8,128)} custom-call(f32[3,512,128]{2,1,0:T(8,128)S(1)} %get-tuple-element.65.refs_0_, f32[16,64,128]{2,1,0:T(8,128)S(1)} %get-tuple-element.62.refs_1_, f32[64,128]{1,0:T(8,128)S(1)} %get-tuple-element.63.refs_2_, f32[64,128]{1,0:T(8,128)S(1)} %get-tuple-element.64.refs_3_), custom_call_target="tpu_custom_call" | custom-call | flops 10000000000 | bytes 10000000 | tf_op jit(solution)/shard_map/motion_again/pallas_call | solution.py:52
  37.5 3.0 %all-to-all-start.1 = ((f32[32,2,128]{2,1,0:T(2,128)}), f32[32,2,128]{2,1,0:T(2,128)S(1)}, u32[]{:S(2)}, u32[]{:S(2)}) async-start(f32[32,2,128]{2,1,0:T(2,128)} %bitcast.10), calls=%async_computation.1 | async-start | bytes 65536 | tf_op jit(solution)/shard_map/all_to_all | solution.py:888
  40.5 0.0 collective-permute-done.10.refs_5_
  40.5 0.0 collective-permute-done.11.refs_6_
  40.5 0.0 collective-permute-done.8.refs_3_
  40.5 0.0 collective-permute-done.9.refs_4_
  40.5 2.5 %stress.1 = (f32[6,512,128]{2,1,0:T(8,128)S(1)}, f32[5,32,128]{2,1,0:T(8,128)S(1)}, f32[5,32,128]{2,1,0:T(8,128)S(1)}, f32[16,512]{1,0:T(8,128)S(1)}) custom-call(f32[3,512,128]{2,1,0:T(8,128)S(1)} %get-tuple-element.65.refs_0_, f32[6,512,128]{2,1,0:T(8,128)} %copy-done.7, f32[5,512,128]{2,1,0:T(8,128)} %copy-done.8, ...), custom_call_target="tpu_custom_call" | custom-call | flops 24999999488 | bytes 25000000 | tf_op jit(solution)/shard_map/stress/pallas_call | solution.py:52
  43.1 1.8 %collective-permute-start.14 = (f32[16,512]{1,0:T(8,128)S(1)}, f32[16,512]{1,0:T(8,128)S(1)}, u32[]{:S(2)}, u32[]{:S(2)}) collective-permute-start(f32[16,512]{1,0:T(8,128)S(1)} %get-tuple-element.75), channel_id=1, source_target_pairs={{0,1},{2,3},{1,0},{3,2},{4,5},{6,7},{5,4},{7,6},{8,9},{10,11},{9,8... | collective-permute-start | bytes 98312 | tf_op jit(solution)/shard_map/ppermute | solution.py:88
  44.9 2.4 %collective-permute-start.15 = (f32[16,512]{1,0:T(8,128)S(1)}, f32[16,512]{1,0:T(8,128)S(1)}, u32[]{:S(2)}, u32[]{:S(2)}) collective-permute-start(f32[16,512]{1,0:T(8,128)S(1)} %get-tuple-element.75), channel_id=1, source_target_pairs={{1,2},{3,0},{2,1},{0,3},{5,6},{7,4},{6,5},{4,7},{9,10},{11,8},{10,... | collective-permute-start | bytes 98312 | tf_op jit(solution)/shard_map/ppermute | solution.py:88
  47.3 0.0 collective-permute-start.12
  47.3 2.5 %collective-permute-start.13 = (f32[5,32,128]{2,1,0:T(8,128)S(1)}, f32[5,32,128]{2,1,0:T(8,128)S(1)}, u32[]{:S(2)}, u32[]{:S(2)}) collective-permute-start(f32[5,32,128]{2,1,0:T(8,128)S(1)} %get-tuple-element.74), channel_id=1, source_target_pairs={{4,8},{12,16},{20,24},{28,0},{8,4},{16,12},{24,20},{0,28},{5,9},{1... | collective-permute-start | bytes 245768 | tf_op jit(solution)/shard_map/ppermute | solution.py:88
  49.8 0.0 all-to-all-done.1
  49.8 1.7 %prepare.1 = (f32[3,16,128]{2,1,0:T(8,128)S(1)}, f32[64,256]{1,0:T(8,128)S(1)}, f32[64,256]{1,0:T(8,128)S(1)}) custom-call(f32[64,128]{1,0:T(8,128)} %motion_again.1.sent_ref, f32[64,128]{1,0:T(8,128)S(1)} %bitcast.17, f32[64,128]{1,0:T(8,128)S(1)} %bitcast.16, f32[64,256]{1,0:T(8,128)S(1)} %get-tuple-element.77.base_ref, ...), custom_call_target="tpu_custom_call" | custom-call | flops 60000002048 | bytes 60000000 | tf_op jit(solution)/shard_map/prepare/pallas_call | solution.py:52
  51.5 0.0 collective-permute-done.14.refs_5_
  51.5 0.0 collective-permute-done.15.refs_6_
  51.5 0.0 collective-permute-done.12.refs_3_
  51.5 0.7 %collective-permute-done.13.refs_4_ = f32[5,32,128]{2,1,0:T(8,128)S(1)} collective-permute-done((f32[5,32,128]{2,1,0:T(8,128)S(1)}, f32[5,32,128]{2,1,0:T(8,128)S(1)}, u32[]{:S(2)}, u32[]{:S(2)}) %collective-permute-start.13) | collective-permute-done | bytes 81952 | tf_op jit(solution)/shard_map/ppermute | solution.py:88
  52.2 0.0 copy-done.10
  52.2 5.6 %finish.1 = (f32[3,32,2,8,128]{4,3,2,1,0:T(8,128)}, f32[64,256]{1,0:T(8,128)}, f32[64,256]{1,0:T(8,128)}) custom-call(f32[3,512,128]{2,1,0:T(8,128)S(1)} %get-tuple-element.65.refs_0_, f32[6,512,128]{2,1,0:T(8,128)S(1)} %get-tuple-element.72.refs_1_, f32[3,512,128]{2,1,0:T(8,128)S(1)} %copy-done.10, f32[5,32,128]{2,1,0:T(8,128)S(1)} %collective-permute-done.12.refs_3_, ...), custom_call_target="tpu_custom_call" | custom-call | flops 60000002048 | bytes 60000000 | tf_op jit(solution)/shard_map/finish/pallas_call | solution.py:52
  (5 shorter events, 0.0 us)
Async XLA Ops:
  0.6 2.1 %copy-start = (f32[64,256]{1,0:T(8,128)S(1)}, f32[64,256]{1,0:T(8,128)}, u32[]{:S(2)}) copy-start(f32[64,256]{1,0:T(8,128)} %rate_ref.1) | copy-start | bytes 196612
  0.6 2.1 %copy-start.2 = (f32[64,256]{1,0:T(8,128)S(1)}, f32[64,256]{1,0:T(8,128)}, u32[]{:S(2)}) copy-start(f32[64,256]{1,0:T(8,128)} %coupling_ref.3) | copy-start | bytes 196612
  0.7 2.1 %copy-start.3 = (f32[64,64]{1,0:T(8,128)S(1)}, f32[64,64]{1,0:T(8,128)}, u32[]{:S(2)}) copy-start(f32[64,64]{1,0:T(8,128)} %refs_3_.1) | copy-start | bytes 49156
  0.7 2.1 %copy-start.4 = (s32[64]{0:T(128)S(1)}, s32[64]{0:T(128)}, u32[]{:S(2)}) copy-start(s32[64]{0:T(128)} %param.25) | copy-start | bytes 772
  0.7 2.1 %copy-start.5 = (s32[64,1]{0,1:T(1,128)S(1)}, s32[64,1]{0,1:T(1,128)}, u32[]{:S(2)}) copy-start(s32[64,1]{0,1:T(1,128)} %param.24) | copy-start | bytes 772
  0.7 2.1 %copy-start.6 = (s32[64]{0:T(128)S(1)}, s32[64]{0:T(128)}, u32[]{:S(2)}) copy-start(s32[64]{0:T(128)} %param.23) | copy-start | bytes 772
  3.8 14.7 %all-to-all-start = ((f32[32,2,128]{2,1,0:T(2,128)}), f32[32,2,128]{2,1,0:T(2,128)S(1)}, u32[]{:S(2)}, u32[]{:S(2)}) async-start(f32[32,2,128]{2,1,0:T(2,128)} %bitcast.6), calls=%async_computation | async-start | bytes 65536 | tf_op jit(solution)/shard_map/all_to_all | solution.py:888
  11.1 9.8 %collective-permute-start.2 = (f32[16,512]{1,0:T(8,128)S(1)}, f32[16,512]{1,0:T(8,128)S(1)}, u32[]{:S(2)}, u32[]{:S(2)}) collective-permute-start(f32[16,512]{1,0:T(8,128)S(1)} %get-tuple-element.51), channel_id=1, source_target_pairs={{0,1},{2,3},{1,0},{3,2},{4,5},{6,7},{5,4},{7,6},{8,9},{10,11},{9,8... | collective-permute-start | bytes 98312 | tf_op jit(solution)/shard_map/ppermute | solution.py:88
  13.0 8.0 %collective-permute-start.3 = (f32[16,512]{1,0:T(8,128)S(1)}, f32[16,512]{1,0:T(8,128)S(1)}, u32[]{:S(2)}, u32[]{:S(2)}) collective-permute-start(f32[16,512]{1,0:T(8,128)S(1)} %get-tuple-element.51), channel_id=1, source_target_pairs={{1,2},{3,0},{2,1},{0,3},{5,6},{7,4},{6,5},{4,7},{9,10},{11,8},{10,... | collective-permute-start | bytes 98312 | tf_op jit(solution)/shard_map/ppermute | solution.py:88
  15.3 5.7 %collective-permute-start = (f32[7,32,128]{2,1,0:T(8,128)S(1)}, f32[7,32,128]{2,1,0:T(8,128)S(1)}, u32[]{:S(2)}, u32[]{:S(2)}) collective-permute-start(f32[7,32,128]{2,1,0:T(8,128)S(1)} %get-tuple-element.49), channel_id=1, source_target_pairs={{0,4},{8,12},{16,20},{24,28},{4,0},{12,8},{20,16},{28,24},{1,5},{9... | collective-permute-start | bytes 344072 | tf_op jit(solution)/shard_map/ppermute | solution.py:88
  15.3 5.7 %collective-permute-start.1 = (f32[7,32,128]{2,1,0:T(8,128)S(1)}, f32[7,32,128]{2,1,0:T(8,128)S(1)}, u32[]{:S(2)}, u32[]{:S(2)}) collective-permute-start(f32[7,32,128]{2,1,0:T(8,128)S(1)} %get-tuple-element.50), channel_id=1, source_target_pairs={{4,8},{12,16},{20,24},{28,0},{8,4},{16,12},{24,20},{0,28},{5,9},{1... | collective-permute-start | bytes 344072 | tf_op jit(solution)/shard_map/ppermute | solution.py:88
  21.0 5.5 %copy-start.1 = (f32[64,256]{1,0:T(8,128)S(1)}, f32[64,256]{1,0:T(8,128)}, u32[]{:S(2)}) copy-start(f32[64,256]{1,0:T(8,128)} %raw_ref.1) | copy-start | bytes 196612
  23.3 6.4 %copy-start.8 = (f32[5,512,128]{2,1,0:T(8,128)}, f32[5,512,128]{2,1,0:T(8,128)S(1)}, u32[]{:S(2)}) copy-start(f32[5,512,128]{2,1,0:T(8,128)S(1)} %get-tuple-element.67.refs_2_) | copy-start | bytes 3932164
  23.3 7.0 %copy-start.7 = (f32[6,512,128]{2,1,0:T(8,128)}, f32[6,512,128]{2,1,0:T(8,128)S(1)}, u32[]{:S(2)}) copy-start(f32[6,512,128]{2,1,0:T(8,128)S(1)} %get-tuple-element.52.refs_1_) | copy-start | bytes 4718596
  23.3 7.0 %copy-start.9 = (f32[3,512,128]{2,1,0:T(8,128)}, f32[3,512,128]{2,1,0:T(8,128)S(1)}, u32[]{:S(2)}) copy-start(f32[3,512,128]{2,1,0:T(8,128)S(1)} %get-tuple-element.53.refs_2_) | copy-start | bytes 2359300
  23.3 6.3 %collective-permute-start.6 = (f32[16,512]{1,0:T(8,128)S(1)}, f32[16,512]{1,0:T(8,128)S(1)}, u32[]{:S(2)}, u32[]{:S(2)}) collective-permute-start(f32[16,512]{1,0:T(8,128)S(1)} %get-tuple-element.56), channel_id=1, source_target_pairs={{0,1},{2,3},{1,0},{3,2},{4,5},{6,7},{5,4},{7,6},{8,9},{10,11},{9,8... | collective-permute-start | bytes 98312 | tf_op jit(solution)/shard_map/ppermute | solution.py:88
  24.0 5.7 %collective-permute-start.7 = (f32[16,512]{1,0:T(8,128)S(1)}, f32[16,512]{1,0:T(8,128)S(1)}, u32[]{:S(2)}, u32[]{:S(2)}) collective-permute-start(f32[16,512]{1,0:T(8,128)S(1)} %get-tuple-element.56), channel_id=1, source_target_pairs={{1,2},{3,0},{2,1},{0,3},{5,6},{7,4},{6,5},{4,7},{9,10},{11,8},{10,... | collective-permute-start | bytes 98312 | tf_op jit(solution)/shard_map/ppermute | solution.py:88
  25.3 4.4 %collective-permute-start.4 = (f32[5,32,128]{2,1,0:T(8,128)S(1)}, f32[5,32,128]{2,1,0:T(8,128)S(1)}, u32[]{:S(2)}, u32[]{:S(2)}) collective-permute-start(f32[5,32,128]{2,1,0:T(8,128)S(1)} %get-tuple-element.54), channel_id=1, source_target_pairs={{0,4},{8,12},{16,20},{24,28},{4,0},{12,8},{20,16},{28,24},{1,5},{9... | collective-permute-start | bytes 245768 | tf_op jit(solution)/shard_map/ppermute | solution.py:88
  25.3 5.0 %collective-permute-start.5 = (f32[5,32,128]{2,1,0:T(8,128)S(1)}, f32[5,32,128]{2,1,0:T(8,128)S(1)}, u32[]{:S(2)}, u32[]{:S(2)}) collective-permute-start(f32[5,32,128]{2,1,0:T(8,128)S(1)} %get-tuple-element.55), channel_id=1, source_target_pairs={{4,8},{12,16},{20,24},{28,0},{8,4},{16,12},{24,20},{0,28},{5,9},{1... | collective-permute-start | bytes 245768 | tf_op jit(solution)/shard_map/ppermute | solution.py:88
  31.8 8.6 %collective-permute-start.10 = (f32[16,512]{1,0:T(8,128)S(1)}, f32[16,512]{1,0:T(8,128)S(1)}, u32[]{:S(2)}, u32[]{:S(2)}) collective-permute-start(f32[16,512]{1,0:T(8,128)S(1)} %get-tuple-element.70), channel_id=1, source_target_pairs={{0,1},{2,3},{1,0},{3,2},{4,5},{6,7},{5,4},{7,6},{8,9},{10,11},{9,8... | collective-permute-start | bytes 98312 | tf_op jit(solution)/shard_map/ppermute | solution.py:88
  32.3 8.2 %collective-permute-start.11 = (f32[16,512]{1,0:T(8,128)S(1)}, f32[16,512]{1,0:T(8,128)S(1)}, u32[]{:S(2)}, u32[]{:S(2)}) collective-permute-start(f32[16,512]{1,0:T(8,128)S(1)} %get-tuple-element.70), channel_id=1, source_target_pairs={{1,2},{3,0},{2,1},{0,3},{5,6},{7,4},{6,5},{4,7},{9,10},{11,8},{10,... | collective-permute-start | bytes 98312 | tf_op jit(solution)/shard_map/ppermute | solution.py:88
  34.7 5.8 %collective-permute-start.8 = (f32[5,32,128]{2,1,0:T(8,128)S(1)}, f32[5,32,128]{2,1,0:T(8,128)S(1)}, u32[]{:S(2)}, u32[]{:S(2)}) collective-permute-start(f32[5,32,128]{2,1,0:T(8,128)S(1)} %get-tuple-element.68), channel_id=1, source_target_pairs={{0,4},{8,12},{16,20},{24,28},{4,0},{12,8},{20,16},{28,24},{1,5},{9... | collective-permute-start | bytes 245768 | tf_op jit(solution)/shard_map/ppermute | solution.py:88
  34.7 5.8 %collective-permute-start.9 = (f32[5,32,128]{2,1,0:T(8,128)S(1)}, f32[5,32,128]{2,1,0:T(8,128)S(1)}, u32[]{:S(2)}, u32[]{:S(2)}) collective-permute-start(f32[5,32,128]{2,1,0:T(8,128)S(1)} %get-tuple-element.69), channel_id=1, source_target_pairs={{4,8},{12,16},{20,24},{28,0},{8,4},{16,12},{24,20},{0,28},{5,9},{1... | collective-permute-start | bytes 245768 | tf_op jit(solution)/shard_map/ppermute | solution.py:88
  37.5 12.3 %all-to-all-start.1 = ((f32[32,2,128]{2,1,0:T(2,128)}), f32[32,2,128]{2,1,0:T(2,128)S(1)}, u32[]{:S(2)}, u32[]{:S(2)}) async-start(f32[32,2,128]{2,1,0:T(2,128)} %bitcast.10), calls=%async_computation.1 | async-start | bytes 65536 | tf_op jit(solution)/shard_map/all_to_all | solution.py:888
  43.1 8.5 %collective-permute-start.14 = (f32[16,512]{1,0:T(8,128)S(1)}, f32[16,512]{1,0:T(8,128)S(1)}, u32[]{:S(2)}, u32[]{:S(2)}) collective-permute-start(f32[16,512]{1,0:T(8,128)S(1)} %get-tuple-element.75), channel_id=1, source_target_pairs={{0,1},{2,3},{1,0},{3,2},{4,5},{6,7},{5,4},{7,6},{8,9},{10,11},{9,8... | collective-permute-start | bytes 98312 | tf_op jit(solution)/shard_map/ppermute | solution.py:88
  44.9 6.6 %collective-permute-start.15 = (f32[16,512]{1,0:T(8,128)S(1)}, f32[16,512]{1,0:T(8,128)S(1)}, u32[]{:S(2)}, u32[]{:S(2)}) collective-permute-start(f32[16,512]{1,0:T(8,128)S(1)} %get-tuple-element.75), channel_id=1, source_target_pairs={{1,2},{3,0},{2,1},{0,3},{5,6},{7,4},{6,5},{4,7},{9,10},{11,8},{10,... | collective-permute-start | bytes 98312 | tf_op jit(solution)/shard_map/ppermute | solution.py:88
  47.3 4.3 %collective-permute-start.12 = (f32[5,32,128]{2,1,0:T(8,128)S(1)}, f32[5,32,128]{2,1,0:T(8,128)S(1)}, u32[]{:S(2)}, u32[]{:S(2)}) collective-permute-start(f32[5,32,128]{2,1,0:T(8,128)S(1)} %get-tuple-element.73), channel_id=1, source_target_pairs={{0,4},{8,12},{16,20},{24,28},{4,0},{12,8},{20,16},{28,24},{1,5},{9... | collective-permute-start | bytes 245768 | tf_op jit(solution)/shard_map/ppermute | solution.py:88
  47.3 5.0 %collective-permute-start.13 = (f32[5,32,128]{2,1,0:T(8,128)S(1)}, f32[5,32,128]{2,1,0:T(8,128)S(1)}, u32[]{:S(2)}, u32[]{:S(2)}) collective-permute-start(f32[5,32,128]{2,1,0:T(8,128)S(1)} %get-tuple-element.74), channel_id=1, source_target_pairs={{4,8},{12,16},{20,24},{28,0},{8,4},{16,12},{24,20},{0,28},{5,9},{1... | collective-permute-start | bytes 245768 | tf_op jit(solution)/shard_map/ppermute | solution.py:88
  49.8 2.5 %copy-start.10 = (f32[3,512,128]{2,1,0:T(8,128)S(1)}, f32[3,512,128]{2,1,0:T(8,128)}, u32[]{:S(2)}) copy-start(f32[3,512,128]{2,1,0:T(8,128)} %copy-done.9) | copy-start | bytes 2359300

commit v5 on v4

--- a/solution.py
+++ b/solution.py
@@ -23,7 +23,6 @@
 
 COSTS = {
     "first": 30_000_000,
-    "table": 60_000_000,
     "load": 20_000_000,
     "begin": 40_000_000,
     "stress": 25_000_000,
@@ -539,7 +538,7 @@
         pack[cut, :] = packed([(v[0], 0, 3, 1), (v[1], 3, 3, 5), (v[2], 6, 3, 7)])
         return carry
 
-    lax.fori_loop(0, size_x, step, 0, unroll=4)
+    lax.fori_loop(0, size_x, step, 0, unroll=8)
     send_columns(pack, col_ref)
 
     def slab(c, x):
@@ -615,19 +614,21 @@
     out_ref[...] = jnp.dot(to_slot, row, precision=exact, preferred_element_type=f32)
 
 
-def first_kernel(layers, v_hbm, b_hbm, m_hbm, *refs):
-    outs, near, pack, sems = refs[:6], refs[6:9], refs[9], refs[10]
-    for copy in fetch((v_hbm, b_hbm, m_hbm), near, sems):
+def first_kernel(layers, span, *refs):
+    far, outs, near, pack, sems = refs[:9], refs[9:16], refs[16:25], refs[25], refs[26]
+    rows_ref, shear_ref = outs[6], outs[2]
+    order = list(range(3, 9)) + list(range(3))
+    copies = fetch([far[i] for i in order], [near[i] for i in order], sems)
+    for copy in copies[:6]:
         copy.wait()
-    edges(layers, *near, *outs, pack)
-
-
-def table_kernel(span, layers, shear_ref, *refs):
-    table(span, *refs)
+    table(span, *near[3:], rows_ref)
+    for copy in copies[6:]:
+        copy.wait()
+    edges(layers, *near[:3], *outs[:6], pack)
     first = shear_ref[pl.ds(0, layers), 0:1]
     spot = lax.broadcasted_iota(jnp.int32, (layers, 128), 1) - AT_CORNER
     own = spot == lax.broadcasted_iota(jnp.int32, (layers, 128), 0)
-    refs[-1][...] += jnp.sum(jnp.where(own, first, 0.0), axis=0, keepdims=True)
+    rows_ref[...] += jnp.sum(jnp.where(own, first, 0.0), axis=0, keepdims=True)
 
 
 def sums_by_third(row, sums):
@@ -778,10 +779,14 @@
     coupling_ref,
     counts_ref,
     owner_ref,
+    stiff_hbm,
     push_ref,
     drift_out,
     rate_out,
+    stiff_ref,
+    sems,
 ):
+    copies = fetch_strips(stiff_hbm, 0, stiff_ref, sems)
     table, sent, back = table_ref[...], sent_ref[...], back_ref[...]
     reaction = []
     for c in range(3):
@@ -798,6 +803,8 @@
     rate = jnp.where(mask, rate, 0.0)
     drift_out[...] = jnp.where(mask, drift_ref[...] + time_step * rate, 0.0)
     rate_out[...] = rate - time_step * coupling * (rate - spread_thirds(moved, SECOND, coupling))
+    for copy in copies:
+        copy.wait()
 
 
 def finish_kernel(
@@ -813,6 +820,7 @@
     half,
     rate_ref,
     counts_ref,
+    early_ref,
     stiff_hbm,
     out_hbm,
     drift_out,
@@ -822,16 +830,18 @@
     cols,
     slope,
     pull,
-    stiff_ref,
+    late_ref,
     sems,
     out_sems,
 ):
-    fetch_strips(stiff_hbm, 0, stiff_ref, sems)
+    early = early_ref.shape[0]
+    fetch_strips(stiff_hbm, early, late_ref, sems)
     size_x = v_ref.shape[1] // layers
     halo = (x_even, x_odd, y_even, y_odd)
     fresh = moving(layers, v_ref, s_ref, buoy_ref, halo, push_ref, ext, cols, slope)
-    strips = sems.shape[0]
-    share = half.shape[0] // strips
+    share = late_ref.shape[0] // sems.shape[0]
+    strips = half.shape[0] // share
+    sooner = early // share
     batch = size_x // strips
 
     def advance(strip):
@@ -841,16 +851,15 @@
             for c in range(3):
                 out_ref[x // TILE, c, :, lax.rem(x, TILE), :] = v[c]
 
-    def multiply(strip):
+    def multiply(stiff_ref, at, strip):
         cut = pl.ds(pl.multiple_of(strip * share, share), share)
-        pltpu.make_async_copy(stiff_hbm.at[cut], stiff_ref.at[cut], sems.at[strip]).wait()
         rounded = half[cut, :].astype(jnp.bfloat16)
         row = lax.broadcasted_iota(jnp.int32, rounded.shape, 0)
         total = jnp.zeros(rounded.shape, f32)
         for b in range(share):
             part = lax.dot_general(
                 rounded,
-                stiff_ref[strip * share + b],
+                stiff_ref[strip * share + b - at],
                 (((1,), (1,)), ((), ())),
                 preferred_element_type=f32,
             )
@@ -861,19 +870,28 @@
         return pltpu.make_async_copy(out_ref.at[tile], out_hbm.at[:, :, tile], out_sems.at[tile])
 
     def step(strip, carry):
-        multiply(strip - 1)
+        multiply(early_ref, 0, strip)
+        advance(strip)
+        return carry
+
+    def late_step(strip, carry):
+        begin = pl.multiple_of(strip * share - early, share)
+        pltpu.make_async_copy(
+            stiff_hbm.at[pl.ds(strip * share, share)],
+            late_ref.at[pl.ds(begin, share)],
+            sems.at[strip - sooner],
+        ).wait()
+        multiply(late_ref, early, strip)
         advance(strip)
         return carry
 
     tiles = size_x // TILE
     for tile in range(tiles):
         begin, end = tile * strips // tiles, (tile + 1) * strips // tiles
-        if tile == 0:
-            advance(0)
-            begin = 1
-        lax.fori_loop(begin, end, step, 0)
+        middle = min(max(begin, sooner), end)
+        lax.fori_loop(begin, middle, step, 0)
+        lax.fori_loop(middle, end, late_step, 0)
         leave(tile).start()
-    multiply(strips - 1)
     mask = counted(counts_ref, half.shape)
     rate = jnp.where(mask, rate_ref[...] - time_step * pull[...], 0.0)
     rate_out[...] = rate
@@ -926,8 +944,9 @@
     dma = pltpu.SemaphoreType.DMA
     flat = [a.reshape(cells, size_y) for a in (buoyancy, shear_modulus, lame_first)]
     far = (soil_velocity.reshape(3, cells, size_y), *flat[:2])
-    vt, bt, mt, one, two, col = call(
-        bind(first_kernel, layers),
+    far += (drift_rate, coupling, contact, counts, owner, corner)
+    vt, bt, mt, one, two, col, rows = call(
+        bind(first_kernel, layers, span),
         "first",
         (
             near_by(3, cells, size_y),
@@ -936,15 +955,10 @@
             near_by(7, layers, size_y),
             near_by(7, layers, size_y),
             near_by(16, cells),
+            near_by(slots, 128),
         ),
         [Far(a) for a in far],
         [pltpu.VMEM(a.shape, a.dtype) for a in far] + [field, dma((len(far),))],
-    )
-    (rows,) = call(
-        bind(table_kernel, span, layers),
-        "table",
-        (near_by(slots, 128),),
-        (mt, drift_rate, coupling, contact, counts, owner, corner),
     )
 
     def exchange(one, two, col):
@@ -1042,11 +1056,18 @@
     )
     halo = exchange(one, two, col)
     sent, st = lax.optimization_barrier((sent, st))
-    push, drift, rate = call(
+    early = number // 4
+    push, drift, rate, stiff = call(
         prepare_kernel,
         "prepare",
-        (near_by(3, size_x, size_y), plane, plane),
-        (sent, back, rows, base, drift, coupling, counts, owner),
+        (
+            near_by(3, size_x, size_y),
+            plane,
+            plane,
+            near_by(early, width, width, dtype=stiffness.dtype),
+        ),
+        (sent, back, rows, base, drift, coupling, counts, owner, Far(stiffness)),
+        [dma((1,))],
     )
     tiles = size_x // TILE
     v, drift, rate = call(
@@ -1066,6 +1087,7 @@
             drift,
             rate,
             counts,
+            stiff,
             Far(stiffness),
         ),
         [
@@ -1074,8 +1096,8 @@
             field,
             vm(3, cells, size_y),
             vm(number, width),
-            pltpu.VMEM(stiffness.shape, stiffness.dtype),
-            dma((chunks,)),
+            pltpu.VMEM((number - early, width, width), stiffness.dtype),
+            dma((3,)),
             dma((tiles,)),
         ],
         far_outs=(0,),

time: 58.1 us -> 57.3 us (0.986)
  waiting for transfers between devices: 2.03 us -> 1.33 us
    ppermute x16, waiting for transfers between devices: 1.37 us -> 0.67 us  [swap(): return lax.ppermute(block, axis, pairs + [(b, a) for a, b in pairs])]
    pallas_call x11 -> x10, Pallas kernels: 23 us -> 22.9 us  [call(): pl.pallas_call(kernel, name=name, out_shape=outs, in_specs=specs, out_spe...]
  transfers between devices with their start and end apart: 18 -> 18, of which waited for: 3 -> 2; matrix products, arithmetic and copies ran while one was open for 0% -> 0% of each run, Pallas kernels for 18% -> 20%
where the time goes in v5:
time: 57.3 us; the launch traced here: 56.9 us
  starting transfers between devices  31.8 us (55%)
  Pallas kernels  22.9 us (40%)
  waiting for transfers between devices  1.33 us (2%)
  between operations  0.91 us (2%)
    pallas_call x10, Pallas kernels, call(): pl.pallas_call(kernel, name=name, out_shape=outs, in_specs=specs, out_spe...  22.9 us
    ppermute x16, starting transfers between devices, swap(): return lax.ppermute(block, axis, pairs + [(b, a) for a, b in pairs])  21.5 us
    all_to_all x2, starting transfers between devices, trade(): lax.all_to_all(blocks, ('gx', 'gy'), split_axis=0, concat_axis=0, tiled=T...  10.3 us
  transfers between devices with their start and end apart: 18, of which 2 were waited for; matrix products, arithmetic and copies ran while one was open for 0% of the time, Pallas kernels for 20%

profile of v5, /device:TPU:0, one launch (start us, length us, event | category | flops | bytes accessed | tf_op | source)
XLA Modules:
  0.0 56.9 jit_solution(9111162011478381063)
XLA Ops:
  0.6 2.8 %first.1 = (f32[3,512,128]{2,1,0:T(8,128)S(1)}, f32[512,128]{1,0:T(8,128)S(1)}, f32[512,128]{1,0:T(8,128)S(1)}, f32[7,32,128]{2,1,0:T(8,128)S(1)}, f32[7,32,128]...) custom-call(f32[3,512,128]{2,1,0:T(8,128)} %bitcast.26, f32[512,128]{1,0:T(8,128)} %bitcast.27, ...), custom_call_target="tpu_custom_call" | custom-call | flops 30000001024 | bytes 30000000 | tf_op jit(solution)/shard_map/first/pallas_call | solution.py:51
  3.4 7.3 %all-to-all-start = ((f32[32,2,128]{2,1,0:T(2,128)}), f32[32,2,128]{2,1,0:T(2,128)S(1)}, u32[]{:S(2)}, u32[]{:S(2)}) async-start(f32[32,2,128]{2,1,0:T(2,128)} %bitcast.6), calls=%async_computation | async-start | bytes 65536 | tf_op jit(solution)/shard_map/all_to_all | solution.py:906
  10.7 1.8 %collective-permute-start.2 = (f32[16,512]{1,0:T(8,128)S(1)}, f32[16,512]{1,0:T(8,128)S(1)}, u32[]{:S(2)}, u32[]{:S(2)}) collective-permute-start(f32[16,512]{1,0:T(8,128)S(1)} %get-tuple-element.54), channel_id=1, source_target_pairs={{0,1},{2,3},{1,0},{3,2},{4,5},{6,7},{5,4},{7,6},{8,9},{10,11},{9,8... | collective-permute-start | bytes 98312 | tf_op jit(solution)/shard_map/ppermute | solution.py:87
  12.6 2.4 %collective-permute-start.3 = (f32[16,512]{1,0:T(8,128)S(1)}, f32[16,512]{1,0:T(8,128)S(1)}, u32[]{:S(2)}, u32[]{:S(2)}) collective-permute-start(f32[16,512]{1,0:T(8,128)S(1)} %get-tuple-element.54), channel_id=1, source_target_pairs={{1,2},{3,0},{2,1},{0,3},{5,6},{7,4},{6,5},{4,7},{9,10},{11,8},{10,... | collective-permute-start | bytes 98312 | tf_op jit(solution)/shard_map/ppermute | solution.py:87
  14.9 0.0 collective-permute-start
  14.9 2.5 %collective-permute-start.1 = (f32[7,32,128]{2,1,0:T(8,128)S(1)}, f32[7,32,128]{2,1,0:T(8,128)S(1)}, u32[]{:S(2)}, u32[]{:S(2)}) collective-permute-start(f32[7,32,128]{2,1,0:T(8,128)S(1)} %get-tuple-element.53), channel_id=1, source_target_pairs={{4,8},{12,16},{20,24},{28,0},{8,4},{16,12},{24,20},{0,28},{5,9},{1... | collective-permute-start | bytes 344072 | tf_op jit(solution)/shard_map/ppermute | solution.py:87
  17.4 0.7 %all-to-all-done = f32[32,2,128]{2,1,0:T(2,128)S(1)} async-done(((f32[32,2,128]{2,1,0:T(2,128)}), f32[32,2,128]{2,1,0:T(2,128)S(1)}, u32[]{:S(2)}, u32[]{:S(2)}) %all-to-all-start) | async-done | bytes 32800 | tf_op jit(solution)/shard_map/all_to_all | solution.py:906
  18.1 1.6 %load.1 = (f32[6,512,128]{2,1,0:T(8,128)S(1)}, f32[512,128]{1,0:T(8,128)S(1)}) custom-call(f32[64,128]{1,0:T(8,128)S(1)} %bitcast.13, f32[6,512,128]{2,1,0:T(8,128)} %bitcast.25, f32[512,128]{1,0:T(8,128)} %bitcast.29), custom_call_target="tpu_custom_call" | custom-call | flops 20000000000 | bytes 20000000 | tf_op jit(solution)/shard_map/load/pallas_call | solution.py:51
  19.7 0.8 %surface.1 = (f32[16,64,128]{2,1,0:T(8,128)S(1)}, f32[64,128]{1,0:T(8,128)S(1)}, f32[3,16,128]{2,1,0:T(8,128)S(1)}) custom-call(f32[64,128]{1,0:T(8,128)S(1)} %bitcast.14, f32[3,512,128]{2,1,0:T(8,128)S(1)} %get-tuple-element.46.refs_0_.refs_1_), custom_call_target="tpu_custom_call" | custom-call | flops 10000000000 | bytes 10000000 | tf_op jit(solution)/shard_map/surface/pallas_call | solution.py:51
  20.6 0.0 collective-permute-done.2.refs_8_
  20.6 0.0 collective-permute-done.3.refs_9_
  20.6 0.0 collective-permute-done.refs_6_
  20.6 0.0 collective-permute-done.1.refs_7_
  20.6 0.0 copy-start
  20.6 0.0 copy-start.1
  20.6 0.0 copy-start.2
  20.6 0.0 copy-start.3
  20.7 0.0 copy-start.4
  20.7 2.3 %begin.1 = (f32[6,512,128]{2,1,0:T(8,128)S(1)}, f32[5,32,128]{2,1,0:T(8,128)S(1)}, f32[5,32,128]{2,1,0:T(8,128)S(1)}, f32[16,512]{1,0:T(8,128)S(1)}, f32[5,512,1...) custom-call(f32[3,512,128]{2,1,0:T(8,128)S(1)} %get-tuple-element.46.refs_0_.refs_1_, ...), custom_call_target="tpu_custom_call" | custom-call | flops 40000000000 | bytes 40000000 | tf_op jit(solution)/shard_map/begin/pallas_call | solution.py:51
  22.9 0.0 copy-start.6
  23.0 0.0 copy-start.5
  23.0 0.0 copy-start.7
  23.0 0.7 %collective-permute-start.6 = (f32[16,512]{1,0:T(8,128)S(1)}, f32[16,512]{1,0:T(8,128)S(1)}, u32[]{:S(2)}, u32[]{:S(2)}) collective-permute-start(f32[16,512]{1,0:T(8,128)S(1)} %get-tuple-element.59), channel_id=1, source_target_pairs={{0,1},{2,3},{1,0},{3,2},{4,5},{6,7},{5,4},{7,6},{8,9},{10,11},{9,8... | collective-permute-start | bytes 98312 | tf_op jit(solution)/shard_map/ppermute | solution.py:87
  23.6 1.4 %collective-permute-start.7 = (f32[16,512]{1,0:T(8,128)S(1)}, f32[16,512]{1,0:T(8,128)S(1)}, u32[]{:S(2)}, u32[]{:S(2)}) collective-permute-start(f32[16,512]{1,0:T(8,128)S(1)} %get-tuple-element.59), channel_id=1, source_target_pairs={{1,2},{3,0},{2,1},{0,3},{5,6},{7,4},{6,5},{4,7},{9,10},{11,8},{10,... | collective-permute-start | bytes 98312 | tf_op jit(solution)/shard_map/ppermute | solution.py:87
  25.0 0.0 collective-permute-start.4
  25.0 1.2 %collective-permute-start.5 = (f32[5,32,128]{2,1,0:T(8,128)S(1)}, f32[5,32,128]{2,1,0:T(8,128)S(1)}, u32[]{:S(2)}, u32[]{:S(2)}) collective-permute-start(f32[5,32,128]{2,1,0:T(8,128)S(1)} %get-tuple-element.58), channel_id=1, source_target_pairs={{4,8},{12,16},{20,24},{28,0},{8,4},{16,12},{24,20},{0,28},{5,9},{1... | collective-permute-start | bytes 245768 | tf_op jit(solution)/shard_map/ppermute | solution.py:87
  26.2 0.0 copy-done
  26.2 0.0 copy-done.1
  26.2 0.0 copy-done.2
  26.3 0.0 copy-done.3
  26.3 0.0 copy-done.4
  26.3 3.1 %pull.1 = (f32[64,256]{1,0:T(8,128)S(1)}, f32[64,256]{1,0:T(8,128)S(1)}, f32[64,128]{1,0:T(8,128)S(1)}) custom-call(bf16[32,256,256]{2,1,0:T(8,128)(2,1)S(1)} %get-tuple-element.61.stiff_ref, bf16[64,256,256]{2,1,0:T(8,128)(2,1)} %refs_12_.1, f32[64,256]{1,0:T(8,128)S(1)} %copy-done.1, f32[64,256]{1,0:T(8,128)S(1)} %copy-done, f32[64,256]{1,0:T(8,128)S(1)} %copy-done.2, ...), custom_call_target="tpu_custom_call" | custom-call | flops 30000001024 | bytes 30000000 | tf_op jit(solution)/shard_map/pull/pallas_call | solution.py:51
  29.3 0.0 copy-done.6
  29.4 0.0 collective-permute-done.6.refs_5_
  29.4 0.0 collective-permute-done.7.refs_6_
  29.4 0.0 collective-permute-done.4.refs_3_
  29.4 0.6 %collective-permute-done.5.refs_4_ = f32[5,32,128]{2,1,0:T(8,128)S(1)} collective-permute-done((f32[5,32,128]{2,1,0:T(8,128)S(1)}, f32[5,32,128]{2,1,0:T(8,128)S(1)}, u32[]{:S(2)}, u32[]{:S(2)}) %collective-permute-start.5) | collective-permute-done | bytes 81952 | tf_op jit(solution)/shard_map/ppermute | solution.py:87
  30.0 0.0 copy-done.5
  30.0 0.0 copy-done.7
  30.0 1.4 %velocity.1 = (f32[3,512,128]{2,1,0:T(8,128)S(1)}, f32[5,32,128]{2,1,0:T(8,128)S(1)}, f32[5,32,128]{2,1,0:T(8,128)S(1)}, f32[16,512]{1,0:T(8,128)S(1)}) custom-call(f32[3,512,128]{2,1,0:T(8,128)S(1)} %get-tuple-element.46.refs_0_.refs_1_, f32[6,512,128]{2,1,0:T(8,128)S(1)} %get-tuple-element.55.refs_1_, f32[3,512,128]{2,1,0:T(8,128)S(1)} %get-tuple-element.56.refs_2_, ...), custom_call_target="tpu_custom_call" | custom-call | flops 24999999488 | bytes 25000000 | tf_op jit(solution)/shard_map/velocity/pallas_call | solution.py:51
  31.4 0.5 collective-permute-start.10
  31.9 2.4 %collective-permute-start.11 = (f32[16,512]{1,0:T(8,128)S(1)}, f32[16,512]{1,0:T(8,128)S(1)}, u32[]{:S(2)}, u32[]{:S(2)}) collective-permute-start(f32[16,512]{1,0:T(8,128)S(1)} %get-tuple-element.73), channel_id=1, source_target_pairs={{1,2},{3,0},{2,1},{0,3},{5,6},{7,4},{6,5},{4,7},{9,10},{11,8},{10,... | collective-permute-start | bytes 98312 | tf_op jit(solution)/shard_map/ppermute | solution.py:87
  34.3 0.0 collective-permute-start.8
  34.3 1.9 %collective-permute-start.9 = (f32[5,32,128]{2,1,0:T(8,128)S(1)}, f32[5,32,128]{2,1,0:T(8,128)S(1)}, u32[]{:S(2)}, u32[]{:S(2)}) collective-permute-start(f32[5,32,128]{2,1,0:T(8,128)S(1)} %get-tuple-element.72), channel_id=1, source_target_pairs={{4,8},{12,16},{20,24},{28,0},{8,4},{16,12},{24,20},{0,28},{5,9},{1... | collective-permute-start | bytes 245768 | tf_op jit(solution)/shard_map/ppermute | solution.py:87
  36.2 0.8 %motion_again.1.sent_ref = f32[64,128]{1,0:T(8,128)} custom-call(f32[3,512,128]{2,1,0:T(8,128)S(1)} %get-tuple-element.68.refs_0_, f32[16,64,128]{2,1,0:T(8,128)S(1)} %get-tuple-element.65.refs_1_, f32[64,128]{1,0:T(8,128)S(1)} %get-tuple-element.66.refs_2_, f32[64,128]{1,0:T(8,128)S(1)} %get-tuple-element.67.refs_3_), custom_call_target="tpu_custom_call" | custom-call | flops 10000000000 | bytes 10000000 | tf_op jit(solution)/shard_map/motion_again/pallas_call | solution.py:51
  37.0 3.0 %all-to-all-start.1 = ((f32[32,2,128]{2,1,0:T(2,128)}), f32[32,2,128]{2,1,0:T(2,128)S(1)}, u32[]{:S(2)}, u32[]{:S(2)}) async-start(f32[32,2,128]{2,1,0:T(2,128)} %bitcast.10), calls=%async_computation.1 | async-start | bytes 65536 | tf_op jit(solution)/shard_map/all_to_all | solution.py:906
  40.0 0.0 collective-permute-done.10.refs_5_
  40.0 0.0 collective-permute-done.11.refs_6_
  40.1 0.0 collective-permute-done.8.refs_3_
  40.1 0.0 collective-permute-done.9.refs_4_
  40.1 2.5 %stress.1 = (f32[6,512,128]{2,1,0:T(8,128)S(1)}, f32[5,32,128]{2,1,0:T(8,128)S(1)}, f32[5,32,128]{2,1,0:T(8,128)S(1)}, f32[16,512]{1,0:T(8,128)S(1)}) custom-call(f32[3,512,128]{2,1,0:T(8,128)S(1)} %get-tuple-element.68.refs_0_, f32[6,512,128]{2,1,0:T(8,128)} %copy-done.5, f32[5,512,128]{2,1,0:T(8,128)} %copy-done.6, ...), custom_call_target="tpu_custom_call" | custom-call | flops 24999999488 | bytes 25000000 | tf_op jit(solution)/shard_map/stress/pallas_call | solution.py:51
  42.6 1.8 %collective-permute-start.14 = (f32[16,512]{1,0:T(8,128)S(1)}, f32[16,512]{1,0:T(8,128)S(1)}, u32[]{:S(2)}, u32[]{:S(2)}) collective-permute-start(f32[16,512]{1,0:T(8,128)S(1)} %get-tuple-element.78), channel_id=1, source_target_pairs={{0,1},{2,3},{1,0},{3,2},{4,5},{6,7},{5,4},{7,6},{8,9},{10,11},{9,8... | collective-permute-start | bytes 98312 | tf_op jit(solution)/shard_map/ppermute | solution.py:87
  44.5 2.4 %collective-permute-start.15 = (f32[16,512]{1,0:T(8,128)S(1)}, f32[16,512]{1,0:T(8,128)S(1)}, u32[]{:S(2)}, u32[]{:S(2)}) collective-permute-start(f32[16,512]{1,0:T(8,128)S(1)} %get-tuple-element.78), channel_id=1, source_target_pairs={{1,2},{3,0},{2,1},{0,3},{5,6},{7,4},{6,5},{4,7},{9,10},{11,8},{10,... | collective-permute-start | bytes 98312 | tf_op jit(solution)/shard_map/ppermute | solution.py:87
  46.8 0.0 collective-permute-start.12
  46.8 2.5 %collective-permute-start.13 = (f32[5,32,128]{2,1,0:T(8,128)S(1)}, f32[5,32,128]{2,1,0:T(8,128)S(1)}, u32[]{:S(2)}, u32[]{:S(2)}) collective-permute-start(f32[5,32,128]{2,1,0:T(8,128)S(1)} %get-tuple-element.77), channel_id=1, source_target_pairs={{4,8},{12,16},{20,24},{28,0},{8,4},{16,12},{24,20},{0,28},{5,9},{1... | collective-permute-start | bytes 245768 | tf_op jit(solution)/shard_map/ppermute | solution.py:87
  49.3 0.0 all-to-all-done.1
  49.3 0.0 copy-start.8
  49.3 2.4 %prepare.1 = (f32[3,16,128]{2,1,0:T(8,128)S(1)}, f32[64,256]{1,0:T(8,128)S(1)}, f32[64,256]{1,0:T(8,128)S(1)}, bf16[16,256,256]{2,1,0:T(8,128)(2,1)S(1)}) custom-call(f32[64,128]{1,0:T(8,128)} %motion_again.1.sent_ref, f32[64,128]{1,0:T(8,128)S(1)} %bitcast.17, f32[64,128]{1,0:T(8,128)S(1)} %bitcast.16, f32[64,256]{1,0:T(8,128)S(1)} %get-tuple-element.80.base_ref, ...), custom_call_target="tpu_custom_call" | custom-call | flops 60000002048 | bytes 60000000 | tf_op jit(solution)/shard_map/prepare/pallas_call | solution.py:51
  51.8 0.0 collective-permute-done.14.refs_5_
  51.8 0.0 collective-permute-done.15.refs_6_
  51.8 0.0 collective-permute-done.12.refs_3_
  51.8 0.0 collective-permute-done.13.refs_4_
  51.8 0.0 copy-done.8
  51.8 5.1 %finish.1 = (f32[3,32,2,8,128]{4,3,2,1,0:T(8,128)}, f32[64,256]{1,0:T(8,128)}, f32[64,256]{1,0:T(8,128)}) custom-call(f32[3,512,128]{2,1,0:T(8,128)S(1)} %get-tuple-element.68.refs_0_, f32[6,512,128]{2,1,0:T(8,128)S(1)} %get-tuple-element.75.refs_1_, f32[3,512,128]{2,1,0:T(8,128)S(1)} %copy-done.8, f32[5,32,128]{2,1,0:T(8,128)S(1)} %collective-permute-done.12.refs_3_, ...), custom_call_target="tpu_custom_call" | custom-call | flops 60000002048 | bytes 60000000 | tf_op jit(solution)/shard_map/finish/pallas_call | solution.py:51
Async XLA Ops:
  3.4 14.7 %all-to-all-start = ((f32[32,2,128]{2,1,0:T(2,128)}), f32[32,2,128]{2,1,0:T(2,128)S(1)}, u32[]{:S(2)}, u32[]{:S(2)}) async-start(f32[32,2,128]{2,1,0:T(2,128)} %bitcast.6), calls=%async_computation | async-start | bytes 65536 | tf_op jit(solution)/shard_map/all_to_all | solution.py:906
  10.7 9.8 %collective-permute-start.2 = (f32[16,512]{1,0:T(8,128)S(1)}, f32[16,512]{1,0:T(8,128)S(1)}, u32[]{:S(2)}, u32[]{:S(2)}) collective-permute-start(f32[16,512]{1,0:T(8,128)S(1)} %get-tuple-element.54), channel_id=1, source_target_pairs={{0,1},{2,3},{1,0},{3,2},{4,5},{6,7},{5,4},{7,6},{8,9},{10,11},{9,8... | collective-permute-start | bytes 98312 | tf_op jit(solution)/shard_map/ppermute | solution.py:87
  12.6 8.0 %collective-permute-start.3 = (f32[16,512]{1,0:T(8,128)S(1)}, f32[16,512]{1,0:T(8,128)S(1)}, u32[]{:S(2)}, u32[]{:S(2)}) collective-permute-start(f32[16,512]{1,0:T(8,128)S(1)} %get-tuple-element.54), channel_id=1, source_target_pairs={{1,2},{3,0},{2,1},{0,3},{5,6},{7,4},{6,5},{4,7},{9,10},{11,8},{10,... | collective-permute-start | bytes 98312 | tf_op jit(solution)/shard_map/ppermute | solution.py:87
  14.9 5.7 %collective-permute-start = (f32[7,32,128]{2,1,0:T(8,128)S(1)}, f32[7,32,128]{2,1,0:T(8,128)S(1)}, u32[]{:S(2)}, u32[]{:S(2)}) collective-permute-start(f32[7,32,128]{2,1,0:T(8,128)S(1)} %get-tuple-element.52), channel_id=1, source_target_pairs={{0,4},{8,12},{16,20},{24,28},{4,0},{12,8},{20,16},{28,24},{1,5},{9... | collective-permute-start | bytes 344072 | tf_op jit(solution)/shard_map/ppermute | solution.py:87
  14.9 5.7 %collective-permute-start.1 = (f32[7,32,128]{2,1,0:T(8,128)S(1)}, f32[7,32,128]{2,1,0:T(8,128)S(1)}, u32[]{:S(2)}, u32[]{:S(2)}) collective-permute-start(f32[7,32,128]{2,1,0:T(8,128)S(1)} %get-tuple-element.53), channel_id=1, source_target_pairs={{4,8},{12,16},{20,24},{28,0},{8,4},{16,12},{24,20},{0,28},{5,9},{1... | collective-permute-start | bytes 344072 | tf_op jit(solution)/shard_map/ppermute | solution.py:87
  20.6 5.6 %copy-start = (f32[64,256]{1,0:T(8,128)S(1)}, f32[64,256]{1,0:T(8,128)}, u32[]{:S(2)}) copy-start(f32[64,256]{1,0:T(8,128)} %rate_ref.1) | copy-start | bytes 196612
  20.6 5.6 %copy-start.1 = (f32[64,256]{1,0:T(8,128)S(1)}, f32[64,256]{1,0:T(8,128)}, u32[]{:S(2)}) copy-start(f32[64,256]{1,0:T(8,128)} %raw_ref.1) | copy-start | bytes 196612
  20.6 5.6 %copy-start.2 = (f32[64,256]{1,0:T(8,128)S(1)}, f32[64,256]{1,0:T(8,128)}, u32[]{:S(2)}) copy-start(f32[64,256]{1,0:T(8,128)} %coupling_ref.3) | copy-start | bytes 196612
  20.6 5.6 %copy-start.3 = (s32[64,1]{0,1:T(1,128)S(1)}, s32[64,1]{0,1:T(1,128)}, u32[]{:S(2)}) copy-start(s32[64,1]{0,1:T(1,128)} %param.24) | copy-start | bytes 772
  20.7 5.6 %copy-start.4 = (s32[64]{0:T(128)S(1)}, s32[64]{0:T(128)}, u32[]{:S(2)}) copy-start(s32[64]{0:T(128)} %param.23) | copy-start | bytes 772
  22.9 6.4 %copy-start.6 = (f32[5,512,128]{2,1,0:T(8,128)}, f32[5,512,128]{2,1,0:T(8,128)S(1)}, u32[]{:S(2)}) copy-start(f32[5,512,128]{2,1,0:T(8,128)S(1)} %get-tuple-element.70.refs_2_) | copy-start | bytes 3932164
  23.0 7.0 %copy-start.5 = (f32[6,512,128]{2,1,0:T(8,128)}, f32[6,512,128]{2,1,0:T(8,128)S(1)}, u32[]{:S(2)}) copy-start(f32[6,512,128]{2,1,0:T(8,128)S(1)} %get-tuple-element.55.refs_1_) | copy-start | bytes 4718596
  23.0 7.0 %copy-start.7 = (f32[3,512,128]{2,1,0:T(8,128)}, f32[3,512,128]{2,1,0:T(8,128)S(1)}, u32[]{:S(2)}) copy-start(f32[3,512,128]{2,1,0:T(8,128)S(1)} %get-tuple-element.56.refs_2_) | copy-start | bytes 2359300
  23.0 6.4 %collective-permute-start.6 = (f32[16,512]{1,0:T(8,128)S(1)}, f32[16,512]{1,0:T(8,128)S(1)}, u32[]{:S(2)}, u32[]{:S(2)}) collective-permute-start(f32[16,512]{1,0:T(8,128)S(1)} %get-tuple-element.59), channel_id=1, source_target_pairs={{0,1},{2,3},{1,0},{3,2},{4,5},{6,7},{5,4},{7,6},{8,9},{10,11},{9,8... | collective-permute-start | bytes 98312 | tf_op jit(solution)/shard_map/ppermute | solution.py:87
  23.6 5.7 %collective-permute-start.7 = (f32[16,512]{1,0:T(8,128)S(1)}, f32[16,512]{1,0:T(8,128)S(1)}, u32[]{:S(2)}, u32[]{:S(2)}) collective-permute-start(f32[16,512]{1,0:T(8,128)S(1)} %get-tuple-element.59), channel_id=1, source_target_pairs={{1,2},{3,0},{2,1},{0,3},{5,6},{7,4},{6,5},{4,7},{9,10},{11,8},{10,... | collective-permute-start | bytes 98312 | tf_op jit(solution)/shard_map/ppermute | solution.py:87
  25.0 4.4 %collective-permute-start.4 = (f32[5,32,128]{2,1,0:T(8,128)S(1)}, f32[5,32,128]{2,1,0:T(8,128)S(1)}, u32[]{:S(2)}, u32[]{:S(2)}) collective-permute-start(f32[5,32,128]{2,1,0:T(8,128)S(1)} %get-tuple-element.57), channel_id=1, source_target_pairs={{0,4},{8,12},{16,20},{24,28},{4,0},{12,8},{20,16},{28,24},{1,5},{9... | collective-permute-start | bytes 245768 | tf_op jit(solution)/shard_map/ppermute | solution.py:87
  25.0 5.0 %collective-permute-start.5 = (f32[5,32,128]{2,1,0:T(8,128)S(1)}, f32[5,32,128]{2,1,0:T(8,128)S(1)}, u32[]{:S(2)}, u32[]{:S(2)}) collective-permute-start(f32[5,32,128]{2,1,0:T(8,128)S(1)} %get-tuple-element.58), channel_id=1, source_target_pairs={{4,8},{12,16},{20,24},{28,0},{8,4},{16,12},{24,20},{0,28},{5,9},{1... | collective-permute-start | bytes 245768 | tf_op jit(solution)/shard_map/ppermute | solution.py:87
  31.4 8.6 %collective-permute-start.10 = (f32[16,512]{1,0:T(8,128)S(1)}, f32[16,512]{1,0:T(8,128)S(1)}, u32[]{:S(2)}, u32[]{:S(2)}) collective-permute-start(f32[16,512]{1,0:T(8,128)S(1)} %get-tuple-element.73), channel_id=1, source_target_pairs={{0,1},{2,3},{1,0},{3,2},{4,5},{6,7},{5,4},{7,6},{8,9},{10,11},{9,8... | collective-permute-start | bytes 98312 | tf_op jit(solution)/shard_map/ppermute | solution.py:87
  31.9 8.2 %collective-permute-start.11 = (f32[16,512]{1,0:T(8,128)S(1)}, f32[16,512]{1,0:T(8,128)S(1)}, u32[]{:S(2)}, u32[]{:S(2)}) collective-permute-start(f32[16,512]{1,0:T(8,128)S(1)} %get-tuple-element.73), channel_id=1, source_target_pairs={{1,2},{3,0},{2,1},{0,3},{5,6},{7,4},{6,5},{4,7},{9,10},{11,8},{10,... | collective-permute-start | bytes 98312 | tf_op jit(solution)/shard_map/ppermute | solution.py:87
  34.3 5.8 %collective-permute-start.8 = (f32[5,32,128]{2,1,0:T(8,128)S(1)}, f32[5,32,128]{2,1,0:T(8,128)S(1)}, u32[]{:S(2)}, u32[]{:S(2)}) collective-permute-start(f32[5,32,128]{2,1,0:T(8,128)S(1)} %get-tuple-element.71), channel_id=1, source_target_pairs={{0,4},{8,12},{16,20},{24,28},{4,0},{12,8},{20,16},{28,24},{1,5},{9... | collective-permute-start | bytes 245768 | tf_op jit(solution)/shard_map/ppermute | solution.py:87
  34.3 5.8 %collective-permute-start.9 = (f32[5,32,128]{2,1,0:T(8,128)S(1)}, f32[5,32,128]{2,1,0:T(8,128)S(1)}, u32[]{:S(2)}, u32[]{:S(2)}) collective-permute-start(f32[5,32,128]{2,1,0:T(8,128)S(1)} %get-tuple-element.72), channel_id=1, source_target_pairs={{4,8},{12,16},{20,24},{28,0},{8,4},{16,12},{24,20},{0,28},{5,9},{1... | collective-permute-start | bytes 245768 | tf_op jit(solution)/shard_map/ppermute | solution.py:87
  37.0 12.3 %all-to-all-start.1 = ((f32[32,2,128]{2,1,0:T(2,128)}), f32[32,2,128]{2,1,0:T(2,128)S(1)}, u32[]{:S(2)}, u32[]{:S(2)}) async-start(f32[32,2,128]{2,1,0:T(2,128)} %bitcast.10), calls=%async_computation.1 | async-start | bytes 65536 | tf_op jit(solution)/shard_map/all_to_all | solution.py:906
  42.6 9.2 %collective-permute-start.14 = (f32[16,512]{1,0:T(8,128)S(1)}, f32[16,512]{1,0:T(8,128)S(1)}, u32[]{:S(2)}, u32[]{:S(2)}) collective-permute-start(f32[16,512]{1,0:T(8,128)S(1)} %get-tuple-element.78), channel_id=1, source_target_pairs={{0,1},{2,3},{1,0},{3,2},{4,5},{6,7},{5,4},{7,6},{8,9},{10,11},{9,8... | collective-permute-start | bytes 98312 | tf_op jit(solution)/shard_map/ppermute | solution.py:87
  44.5 7.3 %collective-permute-start.15 = (f32[16,512]{1,0:T(8,128)S(1)}, f32[16,512]{1,0:T(8,128)S(1)}, u32[]{:S(2)}, u32[]{:S(2)}) collective-permute-start(f32[16,512]{1,0:T(8,128)S(1)} %get-tuple-element.78), channel_id=1, source_target_pairs={{1,2},{3,0},{2,1},{0,3},{5,6},{7,4},{6,5},{4,7},{9,10},{11,8},{10,... | collective-permute-start | bytes 98312 | tf_op jit(solution)/shard_map/ppermute | solution.py:87
  46.8 5.0 %collective-permute-start.12 = (f32[5,32,128]{2,1,0:T(8,128)S(1)}, f32[5,32,128]{2,1,0:T(8,128)S(1)}, u32[]{:S(2)}, u32[]{:S(2)}) collective-permute-start(f32[5,32,128]{2,1,0:T(8,128)S(1)} %get-tuple-element.76), channel_id=1, source_target_pairs={{0,4},{8,12},{16,20},{24,28},{4,0},{12,8},{20,16},{28,24},{1,5},{9... | collective-permute-start | bytes 245768 | tf_op jit(solution)/shard_map/ppermute | solution.py:87
  46.8 5.0 %collective-permute-start.13 = (f32[5,32,128]{2,1,0:T(8,128)S(1)}, f32[5,32,128]{2,1,0:T(8,128)S(1)}, u32[]{:S(2)}, u32[]{:S(2)}) collective-permute-start(f32[5,32,128]{2,1,0:T(8,128)S(1)} %get-tuple-element.77), channel_id=1, source_target_pairs={{4,8},{12,16},{20,24},{28,0},{8,4},{16,12},{24,20},{0,28},{5,9},{1... | collective-permute-start | bytes 245768 | tf_op jit(solution)/shard_map/ppermute | solution.py:87
  49.3 2.5 %copy-start.8 = (f32[3,512,128]{2,1,0:T(8,128)S(1)}, f32[3,512,128]{2,1,0:T(8,128)}, u32[]{:S(2)}) copy-start(f32[3,512,128]{2,1,0:T(8,128)} %copy-done.7) | copy-start | bytes 2359300

commit v6 on v5

--- a/solution.py
+++ b/solution.py
@@ -177,7 +177,7 @@
 
 def slopes(fields, cols, out_ref):
     matrices = [bands(forward, amount) for _, forward, amount in fields]
-    size = 256
+    size = 512
     for begin in range(0, cols.shape[0], size):
         cut = slice(begin, begin + size)
         ghost = parted(cols[cut, :])

time: 57.3 us -> 57.2 us (level)
  no operation moved by 1% of the time
where the time goes in v6:
time: 57.2 us; the launch traced here: 56.9 us
  starting transfers between devices  31.8 us (56%)
  Pallas kernels  22.8 us (40%)
  waiting for transfers between devices  1.33 us (2%)
  between operations  0.91 us (2%)
    pallas_call x10, Pallas kernels, call(): pl.pallas_call(kernel, name=name, out_shape=outs, in_specs=specs, out_spe...  22.8 us
    ppermute x16, starting transfers between devices, swap(): return lax.ppermute(block, axis, pairs + [(b, a) for a, b in pairs])  21.5 us
    all_to_all x2, starting transfers between devices, trade(): lax.all_to_all(blocks, ('gx', 'gy'), split_axis=0, concat_axis=0, tiled=T...  10.3 us
  transfers between devices with their start and end apart: 18, of which 2 were waited for; matrix products, arithmetic and copies ran while one was open for 0% of the time, Pallas kernels for 20%

profile of v6, /device:TPU:0, one launch (start us, length us, event | category | flops | bytes accessed | tf_op | source)
XLA Modules:
  0.0 56.9 jit_solution(3668864214415960982)
XLA Ops:
  0.6 2.8 %first.1 = (f32[3,512,128]{2,1,0:T(8,128)S(1)}, f32[512,128]{1,0:T(8,128)S(1)}, f32[512,128]{1,0:T(8,128)S(1)}, f32[7,32,128]{2,1,0:T(8,128)S(1)}, f32[7,32,128]...) custom-call(f32[3,512,128]{2,1,0:T(8,128)} %bitcast.26, f32[512,128]{1,0:T(8,128)} %bitcast.27, ...), custom_call_target="tpu_custom_call" | custom-call | flops 30000001024 | bytes 30000000 | tf_op jit(solution)/shard_map/first/pallas_call | solution.py:51
  3.4 7.3 %all-to-all-start = ((f32[32,2,128]{2,1,0:T(2,128)}), f32[32,2,128]{2,1,0:T(2,128)S(1)}, u32[]{:S(2)}, u32[]{:S(2)}) async-start(f32[32,2,128]{2,1,0:T(2,128)} %bitcast.6), calls=%async_computation | async-start | bytes 65536 | tf_op jit(solution)/shard_map/all_to_all | solution.py:906
  10.7 1.8 %collective-permute-start.2 = (f32[16,512]{1,0:T(8,128)S(1)}, f32[16,512]{1,0:T(8,128)S(1)}, u32[]{:S(2)}, u32[]{:S(2)}) collective-permute-start(f32[16,512]{1,0:T(8,128)S(1)} %get-tuple-element.54), channel_id=1, source_target_pairs={{0,1},{2,3},{1,0},{3,2},{4,5},{6,7},{5,4},{7,6},{8,9},{10,11},{9,8... | collective-permute-start | bytes 98312 | tf_op jit(solution)/shard_map/ppermute | solution.py:87
  12.6 2.4 %collective-permute-start.3 = (f32[16,512]{1,0:T(8,128)S(1)}, f32[16,512]{1,0:T(8,128)S(1)}, u32[]{:S(2)}, u32[]{:S(2)}) collective-permute-start(f32[16,512]{1,0:T(8,128)S(1)} %get-tuple-element.54), channel_id=1, source_target_pairs={{1,2},{3,0},{2,1},{0,3},{5,6},{7,4},{6,5},{4,7},{9,10},{11,8},{10,... | collective-permute-start | bytes 98312 | tf_op jit(solution)/shard_map/ppermute | solution.py:87
  14.9 0.0 collective-permute-start
  14.9 2.5 %collective-permute-start.1 = (f32[7,32,128]{2,1,0:T(8,128)S(1)}, f32[7,32,128]{2,1,0:T(8,128)S(1)}, u32[]{:S(2)}, u32[]{:S(2)}) collective-permute-start(f32[7,32,128]{2,1,0:T(8,128)S(1)} %get-tuple-element.53), channel_id=1, source_target_pairs={{4,8},{12,16},{20,24},{28,0},{8,4},{16,12},{24,20},{0,28},{5,9},{1... | collective-permute-start | bytes 344072 | tf_op jit(solution)/shard_map/ppermute | solution.py:87
  17.4 0.7 %all-to-all-done = f32[32,2,128]{2,1,0:T(2,128)S(1)} async-done(((f32[32,2,128]{2,1,0:T(2,128)}), f32[32,2,128]{2,1,0:T(2,128)S(1)}, u32[]{:S(2)}, u32[]{:S(2)}) %all-to-all-start) | async-done | bytes 32800 | tf_op jit(solution)/shard_map/all_to_all | solution.py:906
  18.1 1.6 %load.1 = (f32[6,512,128]{2,1,0:T(8,128)S(1)}, f32[512,128]{1,0:T(8,128)S(1)}) custom-call(f32[64,128]{1,0:T(8,128)S(1)} %bitcast.13, f32[6,512,128]{2,1,0:T(8,128)} %bitcast.25, f32[512,128]{1,0:T(8,128)} %bitcast.29), custom_call_target="tpu_custom_call" | custom-call | flops 20000000000 | bytes 20000000 | tf_op jit(solution)/shard_map/load/pallas_call | solution.py:51
  19.7 0.8 %surface.1 = (f32[16,64,128]{2,1,0:T(8,128)S(1)}, f32[64,128]{1,0:T(8,128)S(1)}, f32[3,16,128]{2,1,0:T(8,128)S(1)}) custom-call(f32[64,128]{1,0:T(8,128)S(1)} %bitcast.14, f32[3,512,128]{2,1,0:T(8,128)S(1)} %get-tuple-element.46.refs_0_.refs_1_), custom_call_target="tpu_custom_call" | custom-call | flops 10000000000 | bytes 10000000 | tf_op jit(solution)/shard_map/surface/pallas_call | solution.py:51
  20.6 0.0 collective-permute-done.2.refs_8_
  20.6 0.0 collective-permute-done.3.refs_9_
  20.6 0.0 collective-permute-done.refs_6_
  20.6 0.0 collective-permute-done.1.refs_7_
  20.6 0.0 copy-start
  20.6 0.0 copy-start.1
  20.6 0.0 copy-start.2
  20.6 0.0 copy-start.3
  20.7 0.0 copy-start.4
  20.7 2.3 %begin.1 = (f32[6,512,128]{2,1,0:T(8,128)S(1)}, f32[5,32,128]{2,1,0:T(8,128)S(1)}, f32[5,32,128]{2,1,0:T(8,128)S(1)}, f32[16,512]{1,0:T(8,128)S(1)}, f32[5,512,1...) custom-call(f32[3,512,128]{2,1,0:T(8,128)S(1)} %get-tuple-element.46.refs_0_.refs_1_, ...), custom_call_target="tpu_custom_call" | custom-call | flops 40000000000 | bytes 40000000 | tf_op jit(solution)/shard_map/begin/pallas_call | solution.py:51
  22.9 0.0 copy-start.6
  23.0 0.0 copy-start.5
  23.0 0.0 copy-start.7
  23.0 0.7 %collective-permute-start.6 = (f32[16,512]{1,0:T(8,128)S(1)}, f32[16,512]{1,0:T(8,128)S(1)}, u32[]{:S(2)}, u32[]{:S(2)}) collective-permute-start(f32[16,512]{1,0:T(8,128)S(1)} %get-tuple-element.59), channel_id=1, source_target_pairs={{0,1},{2,3},{1,0},{3,2},{4,5},{6,7},{5,4},{7,6},{8,9},{10,11},{9,8... | collective-permute-start | bytes 98312 | tf_op jit(solution)/shard_map/ppermute | solution.py:87
  23.6 1.4 %collective-permute-start.7 = (f32[16,512]{1,0:T(8,128)S(1)}, f32[16,512]{1,0:T(8,128)S(1)}, u32[]{:S(2)}, u32[]{:S(2)}) collective-permute-start(f32[16,512]{1,0:T(8,128)S(1)} %get-tuple-element.59), channel_id=1, source_target_pairs={{1,2},{3,0},{2,1},{0,3},{5,6},{7,4},{6,5},{4,7},{9,10},{11,8},{10,... | collective-permute-start | bytes 98312 | tf_op jit(solution)/shard_map/ppermute | solution.py:87
  25.0 0.0 collective-permute-start.4
  25.0 1.2 %collective-permute-start.5 = (f32[5,32,128]{2,1,0:T(8,128)S(1)}, f32[5,32,128]{2,1,0:T(8,128)S(1)}, u32[]{:S(2)}, u32[]{:S(2)}) collective-permute-start(f32[5,32,128]{2,1,0:T(8,128)S(1)} %get-tuple-element.58), channel_id=1, source_target_pairs={{4,8},{12,16},{20,24},{28,0},{8,4},{16,12},{24,20},{0,28},{5,9},{1... | collective-permute-start | bytes 245768 | tf_op jit(solution)/shard_map/ppermute | solution.py:87
  26.2 0.0 copy-done
  26.2 0.0 copy-done.1
  26.2 0.0 copy-done.2
  26.3 0.0 copy-done.3
  26.3 0.0 copy-done.4
  26.3 3.1 %pull.1 = (f32[64,256]{1,0:T(8,128)S(1)}, f32[64,256]{1,0:T(8,128)S(1)}, f32[64,128]{1,0:T(8,128)S(1)}) custom-call(bf16[32,256,256]{2,1,0:T(8,128)(2,1)S(1)} %get-tuple-element.61.stiff_ref, bf16[64,256,256]{2,1,0:T(8,128)(2,1)} %refs_12_.1, f32[64,256]{1,0:T(8,128)S(1)} %copy-done.1, f32[64,256]{1,0:T(8,128)S(1)} %copy-done, f32[64,256]{1,0:T(8,128)S(1)} %copy-done.2, ...), custom_call_target="tpu_custom_call" | custom-call | flops 30000001024 | bytes 30000000 | tf_op jit(solution)/shard_map/pull/pallas_call | solution.py:51
  29.3 0.0 copy-done.6
  29.4 0.0 collective-permute-done.6.refs_5_
  29.4 0.0 collective-permute-done.7.refs_6_
  29.4 0.0 collective-permute-done.4.refs_3_
  29.4 0.6 %collective-permute-done.5.refs_4_ = f32[5,32,128]{2,1,0:T(8,128)S(1)} collective-permute-done((f32[5,32,128]{2,1,0:T(8,128)S(1)}, f32[5,32,128]{2,1,0:T(8,128)S(1)}, u32[]{:S(2)}, u32[]{:S(2)}) %collective-permute-start.5) | collective-permute-done | bytes 81952 | tf_op jit(solution)/shard_map/ppermute | solution.py:87
  30.0 0.0 copy-done.5
  30.0 0.0 copy-done.7
  30.0 1.4 %velocity.1 = (f32[3,512,128]{2,1,0:T(8,128)S(1)}, f32[5,32,128]{2,1,0:T(8,128)S(1)}, f32[5,32,128]{2,1,0:T(8,128)S(1)}, f32[16,512]{1,0:T(8,128)S(1)}) custom-call(f32[3,512,128]{2,1,0:T(8,128)S(1)} %get-tuple-element.46.refs_0_.refs_1_, f32[6,512,128]{2,1,0:T(8,128)S(1)} %get-tuple-element.55.refs_1_, f32[3,512,128]{2,1,0:T(8,128)S(1)} %get-tuple-element.56.refs_2_, ...), custom_call_target="tpu_custom_call" | custom-call | flops 24999999488 | bytes 25000000 | tf_op jit(solution)/shard_map/velocity/pallas_call | solution.py:51
  31.4 0.5 collective-permute-start.10
  31.9 2.4 %collective-permute-start.11 = (f32[16,512]{1,0:T(8,128)S(1)}, f32[16,512]{1,0:T(8,128)S(1)}, u32[]{:S(2)}, u32[]{:S(2)}) collective-permute-start(f32[16,512]{1,0:T(8,128)S(1)} %get-tuple-element.73), channel_id=1, source_target_pairs={{1,2},{3,0},{2,1},{0,3},{5,6},{7,4},{6,5},{4,7},{9,10},{11,8},{10,... | collective-permute-start | bytes 98312 | tf_op jit(solution)/shard_map/ppermute | solution.py:87
  34.3 0.0 collective-permute-start.8
  34.3 1.9 %collective-permute-start.9 = (f32[5,32,128]{2,1,0:T(8,128)S(1)}, f32[5,32,128]{2,1,0:T(8,128)S(1)}, u32[]{:S(2)}, u32[]{:S(2)}) collective-permute-start(f32[5,32,128]{2,1,0:T(8,128)S(1)} %get-tuple-element.72), channel_id=1, source_target_pairs={{4,8},{12,16},{20,24},{28,0},{8,4},{16,12},{24,20},{0,28},{5,9},{1... | collective-permute-start | bytes 245768 | tf_op jit(solution)/shard_map/ppermute | solution.py:87
  36.2 0.8 %motion_again.1.sent_ref = f32[64,128]{1,0:T(8,128)} custom-call(f32[3,512,128]{2,1,0:T(8,128)S(1)} %get-tuple-element.68.refs_0_, f32[16,64,128]{2,1,0:T(8,128)S(1)} %get-tuple-element.65.refs_1_, f32[64,128]{1,0:T(8,128)S(1)} %get-tuple-element.66.refs_2_, f32[64,128]{1,0:T(8,128)S(1)} %get-tuple-element.67.refs_3_), custom_call_target="tpu_custom_call" | custom-call | flops 10000000000 | bytes 10000000 | tf_op jit(solution)/shard_map/motion_again/pallas_call | solution.py:51
  37.1 3.0 %all-to-all-start.1 = ((f32[32,2,128]{2,1,0:T(2,128)}), f32[32,2,128]{2,1,0:T(2,128)S(1)}, u32[]{:S(2)}, u32[]{:S(2)}) async-start(f32[32,2,128]{2,1,0:T(2,128)} %bitcast.10), calls=%async_computation.1 | async-start | bytes 65536 | tf_op jit(solution)/shard_map/all_to_all | solution.py:906
  40.0 0.0 collective-permute-done.10.refs_5_
  40.0 0.0 collective-permute-done.11.refs_6_
  40.1 0.0 collective-permute-done.8.refs_3_
  40.1 0.0 collective-permute-done.9.refs_4_
  40.1 2.5 %stress.1 = (f32[6,512,128]{2,1,0:T(8,128)S(1)}, f32[5,32,128]{2,1,0:T(8,128)S(1)}, f32[5,32,128]{2,1,0:T(8,128)S(1)}, f32[16,512]{1,0:T(8,128)S(1)}) custom-call(f32[3,512,128]{2,1,0:T(8,128)S(1)} %get-tuple-element.68.refs_0_, f32[6,512,128]{2,1,0:T(8,128)} %copy-done.5, f32[5,512,128]{2,1,0:T(8,128)} %copy-done.6, ...), custom_call_target="tpu_custom_call" | custom-call | flops 24999999488 | bytes 25000000 | tf_op jit(solution)/shard_map/stress/pallas_call | solution.py:51
  42.5 1.8 %collective-permute-start.14 = (f32[16,512]{1,0:T(8,128)S(1)}, f32[16,512]{1,0:T(8,128)S(1)}, u32[]{:S(2)}, u32[]{:S(2)}) collective-permute-start(f32[16,512]{1,0:T(8,128)S(1)} %get-tuple-element.78), channel_id=1, source_target_pairs={{0,1},{2,3},{1,0},{3,2},{4,5},{6,7},{5,4},{7,6},{8,9},{10,11},{9,8... | collective-permute-start | bytes 98312 | tf_op jit(solution)/shard_map/ppermute | solution.py:87
  44.4 2.4 %collective-permute-start.15 = (f32[16,512]{1,0:T(8,128)S(1)}, f32[16,512]{1,0:T(8,128)S(1)}, u32[]{:S(2)}, u32[]{:S(2)}) collective-permute-start(f32[16,512]{1,0:T(8,128)S(1)} %get-tuple-element.78), channel_id=1, source_target_pairs={{1,2},{3,0},{2,1},{0,3},{5,6},{7,4},{6,5},{4,7},{9,10},{11,8},{10,... | collective-permute-start | bytes 98312 | tf_op jit(solution)/shard_map/ppermute | solution.py:87
  46.8 0.0 collective-permute-start.12
  46.8 2.5 %collective-permute-start.13 = (f32[5,32,128]{2,1,0:T(8,128)S(1)}, f32[5,32,128]{2,1,0:T(8,128)S(1)}, u32[]{:S(2)}, u32[]{:S(2)}) collective-permute-start(f32[5,32,128]{2,1,0:T(8,128)S(1)} %get-tuple-element.77), channel_id=1, source_target_pairs={{4,8},{12,16},{20,24},{28,0},{8,4},{16,12},{24,20},{0,28},{5,9},{1... | collective-permute-start | bytes 245768 | tf_op jit(solution)/shard_map/ppermute | solution.py:87
  49.3 0.0 all-to-all-done.1
  49.3 0.0 copy-start.8
  49.3 2.4 %prepare.1 = (f32[3,16,128]{2,1,0:T(8,128)S(1)}, f32[64,256]{1,0:T(8,128)S(1)}, f32[64,256]{1,0:T(8,128)S(1)}, bf16[16,256,256]{2,1,0:T(8,128)(2,1)S(1)}) custom-call(f32[64,128]{1,0:T(8,128)} %motion_again.1.sent_ref, f32[64,128]{1,0:T(8,128)S(1)} %bitcast.17, f32[64,128]{1,0:T(8,128)S(1)} %bitcast.16, f32[64,256]{1,0:T(8,128)S(1)} %get-tuple-element.80.base_ref, ...), custom_call_target="tpu_custom_call" | custom-call | flops 60000002048 | bytes 60000000 | tf_op jit(solution)/shard_map/prepare/pallas_call | solution.py:51
  51.7 0.0 collective-permute-done.14.refs_5_
  51.7 0.0 collective-permute-done.15.refs_6_
  51.7 0.0 collective-permute-done.12.refs_3_
  51.7 0.0 collective-permute-done.13.refs_4_
  51.7 0.0 copy-done.8
  51.8 5.1 %finish.1 = (f32[3,32,2,8,128]{4,3,2,1,0:T(8,128)}, f32[64,256]{1,0:T(8,128)}, f32[64,256]{1,0:T(8,128)}) custom-call(f32[3,512,128]{2,1,0:T(8,128)S(1)} %get-tuple-element.68.refs_0_, f32[6,512,128]{2,1,0:T(8,128)S(1)} %get-tuple-element.75.refs_1_, f32[3,512,128]{2,1,0:T(8,128)S(1)} %copy-done.8, f32[5,32,128]{2,1,0:T(8,128)S(1)} %collective-permute-done.12.refs_3_, ...), custom_call_target="tpu_custom_call" | custom-call | flops 60000002048 | bytes 60000000 | tf_op jit(solution)/shard_map/finish/pallas_call | solution.py:51
Async XLA Ops:
  3.4 14.7 %all-to-all-start = ((f32[32,2,128]{2,1,0:T(2,128)}), f32[32,2,128]{2,1,0:T(2,128)S(1)}, u32[]{:S(2)}, u32[]{:S(2)}) async-start(f32[32,2,128]{2,1,0:T(2,128)} %bitcast.6), calls=%async_computation | async-start | bytes 65536 | tf_op jit(solution)/shard_map/all_to_all | solution.py:906
  10.7 9.8 %collective-permute-start.2 = (f32[16,512]{1,0:T(8,128)S(1)}, f32[16,512]{1,0:T(8,128)S(1)}, u32[]{:S(2)}, u32[]{:S(2)}) collective-permute-start(f32[16,512]{1,0:T(8,128)S(1)} %get-tuple-element.54), channel_id=1, source_target_pairs={{0,1},{2,3},{1,0},{3,2},{4,5},{6,7},{5,4},{7,6},{8,9},{10,11},{9,8... | collective-permute-start | bytes 98312 | tf_op jit(solution)/shard_map/ppermute | solution.py:87
  12.6 8.0 %collective-permute-start.3 = (f32[16,512]{1,0:T(8,128)S(1)}, f32[16,512]{1,0:T(8,128)S(1)}, u32[]{:S(2)}, u32[]{:S(2)}) collective-permute-start(f32[16,512]{1,0:T(8,128)S(1)} %get-tuple-element.54), channel_id=1, source_target_pairs={{1,2},{3,0},{2,1},{0,3},{5,6},{7,4},{6,5},{4,7},{9,10},{11,8},{10,... | collective-permute-start | bytes 98312 | tf_op jit(solution)/shard_map/ppermute | solution.py:87
  14.9 5.7 %collective-permute-start = (f32[7,32,128]{2,1,0:T(8,128)S(1)}, f32[7,32,128]{2,1,0:T(8,128)S(1)}, u32[]{:S(2)}, u32[]{:S(2)}) collective-permute-start(f32[7,32,128]{2,1,0:T(8,128)S(1)} %get-tuple-element.52), channel_id=1, source_target_pairs={{0,4},{8,12},{16,20},{24,28},{4,0},{12,8},{20,16},{28,24},{1,5},{9... | collective-permute-start | bytes 344072 | tf_op jit(solution)/shard_map/ppermute | solution.py:87
  14.9 5.7 %collective-permute-start.1 = (f32[7,32,128]{2,1,0:T(8,128)S(1)}, f32[7,32,128]{2,1,0:T(8,128)S(1)}, u32[]{:S(2)}, u32[]{:S(2)}) collective-permute-start(f32[7,32,128]{2,1,0:T(8,128)S(1)} %get-tuple-element.53), channel_id=1, source_target_pairs={{4,8},{12,16},{20,24},{28,0},{8,4},{16,12},{24,20},{0,28},{5,9},{1... | collective-permute-start | bytes 344072 | tf_op jit(solution)/shard_map/ppermute | solution.py:87
  20.6 5.6 %copy-start = (f32[64,256]{1,0:T(8,128)S(1)}, f32[64,256]{1,0:T(8,128)}, u32[]{:S(2)}) copy-start(f32[64,256]{1,0:T(8,128)} %rate_ref.1) | copy-start | bytes 196612
  20.6 5.6 %copy-start.1 = (f32[64,256]{1,0:T(8,128)S(1)}, f32[64,256]{1,0:T(8,128)}, u32[]{:S(2)}) copy-start(f32[64,256]{1,0:T(8,128)} %raw_ref.1) | copy-start | bytes 196612
  20.6 5.6 %copy-start.2 = (f32[64,256]{1,0:T(8,128)S(1)}, f32[64,256]{1,0:T(8,128)}, u32[]{:S(2)}) copy-start(f32[64,256]{1,0:T(8,128)} %coupling_ref.3) | copy-start | bytes 196612
  20.6 5.6 %copy-start.3 = (s32[64,1]{0,1:T(1,128)S(1)}, s32[64,1]{0,1:T(1,128)}, u32[]{:S(2)}) copy-start(s32[64,1]{0,1:T(1,128)} %param.24) | copy-start | bytes 772
  20.7 5.6 %copy-start.4 = (s32[64]{0:T(128)S(1)}, s32[64]{0:T(128)}, u32[]{:S(2)}) copy-start(s32[64]{0:T(128)} %param.23) | copy-start | bytes 772
  22.9 6.4 %copy-start.6 = (f32[5,512,128]{2,1,0:T(8,128)}, f32[5,512,128]{2,1,0:T(8,128)S(1)}, u32[]{:S(2)}) copy-start(f32[5,512,128]{2,1,0:T(8,128)S(1)} %get-tuple-element.70.refs_2_) | copy-start | bytes 3932164
  23.0 7.0 %copy-start.5 = (f32[6,512,128]{2,1,0:T(8,128)}, f32[6,512,128]{2,1,0:T(8,128)S(1)}, u32[]{:S(2)}) copy-start(f32[6,512,128]{2,1,0:T(8,128)S(1)} %get-tuple-element.55.refs_1_) | copy-start | bytes 4718596
  23.0 7.0 %copy-start.7 = (f32[3,512,128]{2,1,0:T(8,128)}, f32[3,512,128]{2,1,0:T(8,128)S(1)}, u32[]{:S(2)}) copy-start(f32[3,512,128]{2,1,0:T(8,128)S(1)} %get-tuple-element.56.refs_2_) | copy-start | bytes 2359300
  23.0 6.4 %collective-permute-start.6 = (f32[16,512]{1,0:T(8,128)S(1)}, f32[16,512]{1,0:T(8,128)S(1)}, u32[]{:S(2)}, u32[]{:S(2)}) collective-permute-start(f32[16,512]{1,0:T(8,128)S(1)} %get-tuple-element.59), channel_id=1, source_target_pairs={{0,1},{2,3},{1,0},{3,2},{4,5},{6,7},{5,4},{7,6},{8,9},{10,11},{9,8... | collective-permute-start | bytes 98312 | tf_op jit(solution)/shard_map/ppermute | solution.py:87
  23.6 5.7 %collective-permute-start.7 = (f32[16,512]{1,0:T(8,128)S(1)}, f32[16,512]{1,0:T(8,128)S(1)}, u32[]{:S(2)}, u32[]{:S(2)}) collective-permute-start(f32[16,512]{1,0:T(8,128)S(1)} %get-tuple-element.59), channel_id=1, source_target_pairs={{1,2},{3,0},{2,1},{0,3},{5,6},{7,4},{6,5},{4,7},{9,10},{11,8},{10,... | collective-permute-start | bytes 98312 | tf_op jit(solution)/shard_map/ppermute | solution.py:87
  25.0 4.4 %collective-permute-start.4 = (f32[5,32,128]{2,1,0:T(8,128)S(1)}, f32[5,32,128]{2,1,0:T(8,128)S(1)}, u32[]{:S(2)}, u32[]{:S(2)}) collective-permute-start(f32[5,32,128]{2,1,0:T(8,128)S(1)} %get-tuple-element.57), channel_id=1, source_target_pairs={{0,4},{8,12},{16,20},{24,28},{4,0},{12,8},{20,16},{28,24},{1,5},{9... | collective-permute-start | bytes 245768 | tf_op jit(solution)/shard_map/ppermute | solution.py:87
  25.0 5.0 %collective-permute-start.5 = (f32[5,32,128]{2,1,0:T(8,128)S(1)}, f32[5,32,128]{2,1,0:T(8,128)S(1)}, u32[]{:S(2)}, u32[]{:S(2)}) collective-permute-start(f32[5,32,128]{2,1,0:T(8,128)S(1)} %get-tuple-element.58), channel_id=1, source_target_pairs={{4,8},{12,16},{20,24},{28,0},{8,4},{16,12},{24,20},{0,28},{5,9},{1... | collective-permute-start | bytes 245768 | tf_op jit(solution)/shard_map/ppermute | solution.py:87
  31.4 8.6 %collective-permute-start.10 = (f32[16,512]{1,0:T(8,128)S(1)}, f32[16,512]{1,0:T(8,128)S(1)}, u32[]{:S(2)}, u32[]{:S(2)}) collective-permute-start(f32[16,512]{1,0:T(8,128)S(1)} %get-tuple-element.73), channel_id=1, source_target_pairs={{0,1},{2,3},{1,0},{3,2},{4,5},{6,7},{5,4},{7,6},{8,9},{10,11},{9,8... | collective-permute-start | bytes 98312 | tf_op jit(solution)/shard_map/ppermute | solution.py:87
  31.9 8.2 %collective-permute-start.11 = (f32[16,512]{1,0:T(8,128)S(1)}, f32[16,512]{1,0:T(8,128)S(1)}, u32[]{:S(2)}, u32[]{:S(2)}) collective-permute-start(f32[16,512]{1,0:T(8,128)S(1)} %get-tuple-element.73), channel_id=1, source_target_pairs={{1,2},{3,0},{2,1},{0,3},{5,6},{7,4},{6,5},{4,7},{9,10},{11,8},{10,... | collective-permute-start | bytes 98312 | tf_op jit(solution)/shard_map/ppermute | solution.py:87
  34.3 5.8 %collective-permute-start.8 = (f32[5,32,128]{2,1,0:T(8,128)S(1)}, f32[5,32,128]{2,1,0:T(8,128)S(1)}, u32[]{:S(2)}, u32[]{:S(2)}) collective-permute-start(f32[5,32,128]{2,1,0:T(8,128)S(1)} %get-tuple-element.71), channel_id=1, source_target_pairs={{0,4},{8,12},{16,20},{24,28},{4,0},{12,8},{20,16},{28,24},{1,5},{9... | collective-permute-start | bytes 245768 | tf_op jit(solution)/shard_map/ppermute | solution.py:87
  34.3 5.8 %collective-permute-start.9 = (f32[5,32,128]{2,1,0:T(8,128)S(1)}, f32[5,32,128]{2,1,0:T(8,128)S(1)}, u32[]{:S(2)}, u32[]{:S(2)}) collective-permute-start(f32[5,32,128]{2,1,0:T(8,128)S(1)} %get-tuple-element.72), channel_id=1, source_target_pairs={{4,8},{12,16},{20,24},{28,0},{8,4},{16,12},{24,20},{0,28},{5,9},{1... | collective-permute-start | bytes 245768 | tf_op jit(solution)/shard_map/ppermute | solution.py:87
  37.1 12.2 %all-to-all-start.1 = ((f32[32,2,128]{2,1,0:T(2,128)}), f32[32,2,128]{2,1,0:T(2,128)S(1)}, u32[]{:S(2)}, u32[]{:S(2)}) async-start(f32[32,2,128]{2,1,0:T(2,128)} %bitcast.10), calls=%async_computation.1 | async-start | bytes 65536 | tf_op jit(solution)/shard_map/all_to_all | solution.py:906
  42.5 9.2 %collective-permute-start.14 = (f32[16,512]{1,0:T(8,128)S(1)}, f32[16,512]{1,0:T(8,128)S(1)}, u32[]{:S(2)}, u32[]{:S(2)}) collective-permute-start(f32[16,512]{1,0:T(8,128)S(1)} %get-tuple-element.78), channel_id=1, source_target_pairs={{0,1},{2,3},{1,0},{3,2},{4,5},{6,7},{5,4},{7,6},{8,9},{10,11},{9,8... | collective-permute-start | bytes 98312 | tf_op jit(solution)/shard_map/ppermute | solution.py:87
  44.4 7.3 %collective-permute-start.15 = (f32[16,512]{1,0:T(8,128)S(1)}, f32[16,512]{1,0:T(8,128)S(1)}, u32[]{:S(2)}, u32[]{:S(2)}) collective-permute-start(f32[16,512]{1,0:T(8,128)S(1)} %get-tuple-element.78), channel_id=1, source_target_pairs={{1,2},{3,0},{2,1},{0,3},{5,6},{7,4},{6,5},{4,7},{9,10},{11,8},{10,... | collective-permute-start | bytes 98312 | tf_op jit(solution)/shard_map/ppermute | solution.py:87
  46.8 5.0 %collective-permute-start.12 = (f32[5,32,128]{2,1,0:T(8,128)S(1)}, f32[5,32,128]{2,1,0:T(8,128)S(1)}, u32[]{:S(2)}, u32[]{:S(2)}) collective-permute-start(f32[5,32,128]{2,1,0:T(8,128)S(1)} %get-tuple-element.76), channel_id=1, source_target_pairs={{0,4},{8,12},{16,20},{24,28},{4,0},{12,8},{20,16},{28,24},{1,5},{9... | collective-permute-start | bytes 245768 | tf_op jit(solution)/shard_map/ppermute | solution.py:87
  46.8 5.0 %collective-permute-start.13 = (f32[5,32,128]{2,1,0:T(8,128)S(1)}, f32[5,32,128]{2,1,0:T(8,128)S(1)}, u32[]{:S(2)}, u32[]{:S(2)}) collective-permute-start(f32[5,32,128]{2,1,0:T(8,128)S(1)} %get-tuple-element.77), channel_id=1, source_target_pairs={{4,8},{12,16},{20,24},{28,0},{8,4},{16,12},{24,20},{0,28},{5,9},{1... | collective-permute-start | bytes 245768 | tf_op jit(solution)/shard_map/ppermute | solution.py:87
  49.3 2.5 %copy-start.8 = (f32[3,512,128]{2,1,0:T(8,128)S(1)}, f32[3,512,128]{2,1,0:T(8,128)}, u32[]{:S(2)}) copy-start(f32[3,512,128]{2,1,0:T(8,128)} %copy-done.7) | copy-start | bytes 2359300
